TPU v7x, 256 devices: a whole 4x4x8 slice. The times are simulated.
256 devices in a mesh: group: 4 (over x), member: 64 (over y, z, core).
Axes of the slice: x: 4, y: 4, z: 8, core: 2. Of those that a mesh axis runs over, the one named last changes fastest.
Arguments:
- embeddings: bfloat16 [49152, 1024], P(('group', 'member'))
- first_size: int32 [4], P('group'), may hold values from 1536 to 10751
Outputs:
- best_match: float32 [49152], P(('group', 'member'))
All inputs are finite; a program needn't handle non-finite values.
Results may differ from a plain program's by a relative error of at most 0.0045.
Values may be sent and summed in bfloat16 or wider, within the bound.
No kernel may reach another device: no remote copies, remote signals or barrier semaphores. Data moves between devices by JAX's collectives and lax.ppermute only.
A program may use at most 64 MiB of HBM per device.

v0:
```python
import jax
import jax.numpy as jnp
from jax import lax
from jax.sharding import PartitionSpec as P


def normalize(rows):
    values = rows.astype(jnp.float32)
    return (values * lax.rsqrt(jnp.sum(values * values, axis=1, keepdims=True) + 1e-06)).astype(
        jnp.bfloat16
    )


def tile_scores(left, right):
    return jnp.einsum("rd,cd->rc", left, right, preferred_element_type=jnp.float32)


def shards(embeddings, first_size):
    unit = normalize(embeddings)
    rows = unit.shape[0]
    member_id = lax.axis_index("member")
    split = first_size[0]
    own_index = member_id * rows + jnp.arange(rows, dtype=jnp.int32)
    own_cluster = own_index >= split
    start_best = jnp.full((rows,), -1.0, jnp.float32)
    piece = lax.all_gather(unit, "member", axis=0, tiled=True)
    col_index = jnp.arange(piece.shape[0], dtype=jnp.int32)
    keep = (col_index[None, :] < own_index[:, None]) & (
        (col_index >= split)[None, :] == own_cluster[:, None]
    )
    scores = jnp.where(keep, tile_scores(unit, piece), -1.0)
    return jnp.maximum(start_best, jnp.max(scores, axis=1))


def solution(mesh):
    placed = (P(("group", "member"), None), P("group"))
    return jax.shard_map(
        shards, mesh=mesh, in_specs=placed, out_specs=P(("group", "member")), check_vma=False
    )
```

profile of v0, /device:TPU:1, one launch (start us, length us, event | category | flops | bytes accessed | tf_op | source)
XLA Modules:
  0.0 157.1 jit_solution(9612826746208971448)
XLA Ops:
  6.5 0.0 all-gather.2.cloned.1.call-start
  6.5 1.2 fusion.2
  7.7 1.9 %fusion.3 = bf16[192,1024]{1,0:T(8,128)(2,1)} fusion(bf16[192,1024]{1,0:T(8,128)(2,1)} %param.2, f32[192]{0:T(256)S(1)} %add_rsqrt_fusion), kind=kLoop, calls=%fused_computation.7 | loop fusion | flops 589824 | bytes 787200 | tf_op jit(solution)/shard_map/convert_element_type | solution.py:9
  9.6 0.0 all-gather.2.cloned.1.call-update
  10.3 125.4 %all-gather.2.cloned.1.call-done = bf16[12288,1024]{1,0:T(8,128)(2,1)} async-done(((bf16[192,1024]{1,0:T(8,128)(2,1)}), bf16[12288,1024]{1,0:T(8,128)(2,1)}) %all-gather.2.cloned.1.call-update) | async-done | bytes 25165840 | tf_op jit(solution)/shard_map/all_gather | solution.py:26
  135.7 14.0 %fusion.1 = f32[192]{0:T(256)S(1)} fusion(bf16[192,1024]{1,0:T(8,128)(2,1)} %fusion.3, bf16[12288,1024]{1,0:T(8,128)(2,1)} %all-gather.2.cloned.1.call-done, pred[192]{0:T(512)(128)(4,1)S(1)} %broadcast_compare_fusion, pred[12288]{0:T(1024)(128)(4,1)S(1)} %iota_compare_fusion.1, s32[192]{0:T(256)S(1)} %iota_add_fusion), kind=kOutput, calls=%fused_computation.3 | convolution fusion | flops 4843634688 | bytes 25573056 | tf_op jit(solution)/shard_map/rd,cd->rc/dot_general | solution.py:15
  149.7 0.6 broadcast_maximum_fusion
  (4 shorter events, 0.0 us)
Async XLA Ops:
  6.5 129.2 %all-gather.2.cloned.1.call-start = ((), (), s32[]{:S(2)}) async-start(), calls=%async_computation | async-start | bytes 25559040 | tf_op jit(solution)/shard_map/all_gather | solution.py:26
Sparse Core Ops, SparseCore 0:
  10.1 125.5 all-gather.1
where the time goes:
time: 157 us
  waiting for transfers between devices  125 us (80%)
  between operations  14.1 us (9%)
  matrix products  14 us (9%)
  other arithmetic  3.68 us (2%)
    all_gather x1, waiting for transfers between devices, shards(): piece = lax.all_gather(unit, 'member', axis=0, tiled=True)  125 us
    dot_general x1, matrix products, tile_scores(): jnp.einsum('rd,cd->rc', left, right, preferred_element_type=jnp.float32)  14 us
  transfers between devices with their start and end apart: 1, of which 1 were waited for; matrix products, arithmetic and copies ran while one was open for 0% of the time, Pallas kernels for 0%

commit v1 on v0

v1 whole, which is shorter than its diff:
```python
import jax
import jax.numpy as jnp
from jax import lax
from jax.experimental import pallas as pl
from jax.experimental.pallas import tpu as pltpu
from jax.sharding import PartitionSpec as P

Y, Z, CORES = 4, 8, 2
ROWS = 192
HALF = ROWS // 2
CHIP = ROWS * CORES
WIDE = Y * CHIP
D = 1024
NONE = -2.0


def device(y, z, core):
    return ((y % Y) * Z + z % Z) * CORES + core % CORES


def move(value, dy, dz, dcore=0):
    pairs = [
        (device(y, z, core), device(y + dy, z + dz, core + dcore))
        for y in range(Y)
        for z in range(Z)
        for core in range(CORES)
    ]
    return lax.ppermute(value, "member", pairs)


def normalize_kernel(rows_ref, low_ref, high_ref):
    values = rows_ref[...].astype(jnp.float32)
    unit = (values * lax.rsqrt(jnp.sum(values * values, axis=1, keepdims=True) + 1e-06)).astype(
        jnp.bfloat16
    )
    low_ref[...] = unit[:HALF]
    high_ref[...] = unit[HALF:]


def normalize(rows):
    half = jax.ShapeDtypeStruct((HALF, D), jnp.bfloat16)
    return pl.pallas_call(
        normalize_kernel,
        out_shape=(half, half),
        cost_estimate=pl.CostEstimate(flops=4 * ROWS * D, bytes_accessed=4 * ROWS * D, transcendentals=ROWS),
        name="normalize",
    )(rows)


def match_kernel(starts_ref, lo_ref, hi_ref, best_ref, right_ref, *rest):
    *piece_refs, out_ref = rest
    tile = 256
    for n in range(WIDE // tile):
        lanes = slice(n * tile, (n + 1) * tile)
        right = right_ref[lanes, :]
        lo = lo_ref[:, lanes]
        hi = hi_ref[:, lanes]
        best = best_ref[:, lanes]
        for i, piece_ref in enumerate(piece_refs):
            scores = lax.dot_general(
                piece_ref[...], right, (((1,), (1,)), ((), ())), preferred_element_type=jnp.float32
            )
            index = starts_ref[i] + lax.broadcasted_iota(jnp.int32, scores.shape, 0)
            scores = jnp.where((index >= lo) & (index < hi), scores, NONE)
            best = jnp.maximum(best, jnp.max(scores.reshape(-1, 8, tile), axis=0))
        out_ref[:, lanes] = best


def match(starts, lo, hi, best, right, pieces):
    vmem = pl.BlockSpec(memory_space=pltpu.VMEM)
    rows = sum(piece.shape[0] for piece in pieces)
    return pl.pallas_call(
        match_kernel,
        out_shape=jax.ShapeDtypeStruct((8, WIDE), jnp.float32),
        in_specs=[pl.BlockSpec(memory_space=pltpu.SMEM)] + [vmem] * (4 + len(pieces)),
        out_specs=vmem,
        cost_estimate=pl.CostEstimate(
            flops=2 * rows * WIDE * D, bytes_accessed=2 * D * (rows + WIDE), transcendentals=0
        ),
        compiler_params=pltpu.CompilerParams(vmem_limit_bytes=24 * 1024 * 1024),
        name="match",
    )(starts, lo, hi, best, right, *pieces)


def shards(embeddings, first_size):
    member = lax.axis_index("member")
    core = member % CORES
    z = member // CORES % Z
    y = member // (CORES * Z)
    split = first_size[0]

    unit = normalize(embeddings)

    def start(dy, dz, half, dcore=0):
        return device(y + dy, z + dz, core + dcore) * ROWS + half * HALF

    row_index = jnp.concatenate(
        [
            start(dy, 0, 0, dcore) + jnp.arange(ROWS, dtype=jnp.int32)
            for dcore in (0, 1)
            for dy in (0, -1, 1, 2)
        ]
    )[None]
    lo = jnp.where(row_index >= split, split, 0)

    up, down = [unit], [unit]
    for _ in range(3):
        up.append([move(half, 0, 1) for half in up[-1]])
        down.append([move(half, 0, -1) for half in down[-1]])
    far = [move(up[3][0], 0, 1), move(down[3][1], 0, -1)]

    above = [move(half, 1, 0) for half in unit]
    below = [move(half, -1, 0) for half in unit]
    across = [move(above[0], 1, 0), move(below[1], -1, 0)]
    mine = jnp.concatenate(list(unit) + above + below + across)
    right = jnp.concatenate([mine, move(mine, 0, 0, 1)])

    best = jnp.full((8, WIDE), NONE, jnp.float32)
    best = match(jnp.stack([start(0, 0, h) for h in (0, 1)]), lo, row_index, best, right, unit)
    for k in (1, 2, 3):
        starts = jnp.stack([start(0, d, h) for d in (-k, k) for h in (0, 1)])
        best = match(starts, lo, row_index, best, right, up[k] + down[k])
    best = match(jnp.stack([start(0, 4, h) for h in (0, 1)]), lo, row_index, best, right, far)

    best = jnp.max(best, axis=0).reshape(CORES, Y, ROWS)
    best = jnp.maximum(best[0], move(best[1], 0, 0, 1))
    best = jnp.maximum(
        jnp.maximum(best[0], move(best[1], -1, 0)),
        jnp.maximum(move(best[2], 1, 0), move(best[3], 2, 0)),
    )
    return jnp.maximum(best, -1.0)


def solution(mesh):
    placed = (P(("group", "member"), None), P("group"))
    return jax.shard_map(
        shards, mesh=mesh, in_specs=placed, out_specs=P(("group", "member")), check_vma=False
    )
```

time: 157 us -> 89.3 us (0.57)
  waiting for transfers between devices: 125 us -> 10.1 us
  starting transfers between devices: 0.01 us -> 40.9 us
  Pallas kernels: 0 us -> 21.7 us
  matrix products: 14 us -> 0 us
  between operations: 14.1 us -> 0.85 us
  local copies, waits for them, and re-layouts: 0 us -> 12.2 us
    all_gather x1 -> x0, waiting for transfers between devices: 125 us -> none  [shards(): piece = lax.all_gather(unit, 'member', axis=0, tiled=True)]
    ppermute x0 -> x25, starting transfers between devices: none -> 40.9 us  [move(): return lax.ppermute(value, 'member', pairs)]
    pallas_call x0 -> x6, Pallas kernels: none -> 21.7 us  [the longest x5 19.9 us: match(): pl.pallas_call(match_kernel, out_shape=jax.ShapeDtypeStruct((8, WIDE), jn...]
    dot_general x1 -> x0, matrix products: 14 us -> none  [tile_scores(): jnp.einsum('rd,cd->rc', left, right, preferred_element_type=jnp.float32)]
    ppermute x0 -> x25, waiting for transfers between devices: none -> 10.1 us  [move(): return lax.ppermute(value, 'member', pairs)]
    unnamed x0 -> x15, local copies, waits for them, and re-layouts: none -> 6.91 us
    concatenate x0 -> x4, local copies, waits for them, and re-layouts: none -> 4.41 us  [the longest x2 2.18 us: shards(): jnp.concatenate([start(dy, 0, 0, dcore) + jnp.arange(ROWS, dtype=jnp.int3...]
    convert_element_type x1 -> x0, other arithmetic: 1.93 us -> none  [normalize(): (values * lax.rsqrt(jnp.sum(values * values, axis=1, keepdims=True) + 1e-...]
  transfers between devices with their start and end apart: 1 -> 25, of which waited for: 1 -> 8; matrix products, arithmetic and copies ran while one was open for 0% -> 15% of each run, Pallas kernels for 0% -> 19%
where the time goes in v1:
time: 89.3 us; the launch traced here: 88.5 us
  starting transfers between devices  40.9 us (46%)
  Pallas kernels  21.7 us (24%)
  local copies, waits for them, and re-layouts  12.2 us (14%)
  waiting for transfers between devices  10.1 us (11%)
  other arithmetic  2.74 us (3%)
    ppermute x25, starting transfers between devices, move(): return lax.ppermute(value, 'member', pairs)  40.9 us
    pallas_call x5, Pallas kernels, match(): pl.pallas_call(match_kernel, out_shape=jax.ShapeDtypeStruct((8, WIDE), jn...  19.9 us
    ppermute x25, waiting for transfers between devices, move(): return lax.ppermute(value, 'member', pairs)  10.1 us
    unnamed x15, local copies, waits for them, and re-layouts  6.91 us
    concatenate x2, local copies, waits for them, and re-layouts, shards(): jnp.concatenate([start(dy, 0, 0, dcore) + jnp.arange(ROWS, dtype=jnp.int3...  2.18 us
    pallas_call x1, Pallas kernels, normalize(): pl.pallas_call(normalize_kernel, out_shape=(half, half), cost_estimate=pl...  1.87 us
  transfers between devices with their start and end apart: 25, of which 8 were waited for; matrix products, arithmetic and copies ran while one was open for 15% of the time, Pallas kernels for 19%

profile of v1, /device:TPU:1, one launch (start us, length us, event | category | flops | bytes accessed | tf_op | source)
XLA Modules:
  0.0 88.5 jit_solution(15051844990916410216)
XLA Ops:
  0.0 1.9 %normalize.1 = (bf16[96,1024]{1,0:T(8,128)(2,1)}, bf16[96,1024]{1,0:T(8,128)(2,1)}) custom-call(bf16[192,1024]{1,0:T(8,128)(2,1)} %rows_ref.1), custom_call_target="tpu_custom_call" | custom-call | flops 786432 | bytes 786432 | tf_op jit(solution)/shard_map/normalize/pallas_call | solution.py:42
  1.9 2.1 %collective-permute-start = (bf16[96,1024]{1,0:T(8,128)(2,1)}, bf16[96,1024]{1,0:T(8,128)(2,1)S(1)}, u32[]{:S(2)}, u32[]{:S(2)}) collective-permute-start(bf16[96,1024]{1,0:T(8,128)(2,1)} %get-tuple-element.7.rest_0_), channel_id=1, source_target_pairs={{0,16},{1,17},{2,18},{3,19},{4,20},{5,21},{6,22},{7,23},{8,24},{9,... | collective-permute-start | bytes 589832 | tf_op jit(solution)/shard_map/ppermute | solution.py:28
  5.5 2.7 %collective-permute-start.3 = (bf16[96,1024]{1,0:T(8,128)(2,1)}, bf16[96,1024]{1,0:T(8,128)(2,1)S(1)}, u32[]{:S(2)}, u32[]{:S(2)}) collective-permute-start(bf16[96,1024]{1,0:T(8,128)(2,1)} %get-tuple-element.8.rest_1_), channel_id=1, source_target_pairs={{0,48},{1,49},{2,50},{3,51},{4,52},{5,53},{6,54},{7,55},{8,56},{9,... | collective-permute-start | bytes 589832 | tf_op jit(solution)/shard_map/ppermute | solution.py:28
  8.2 1.6 %constant_dynamic-update-slice_fusion.7 = (bf16[768,1024]{1,0:T(8,128)(2,1)}, bf16[1536,1024]{1,0:T(8,128)(2,1)S(1)}) fusion(bf16[96,1024]{1,0:T(8,128)(2,1)} %get-tuple-element.7.rest_0_), kind=kLoop, calls=%fused_computation.7 | loop fusion | bytes 589824
  9.8 1.7 %constant_dynamic-update-slice_fusion.6 = (bf16[768,1024]{1,0:T(8,128)(2,1)}, bf16[1536,1024]{1,0:T(8,128)(2,1)S(1)}) fusion(bf16[768,1024]{1,0:T(8,128)(2,1)} %get-tuple-element.23, bf16[96,1024]{1,0:T(8,128)(2,1)} %get-tuple-element.8.rest_1_, bf16[1536,1024]{1,0:T(8,128)(2,1)S(1)} %get-tuple-element.24), kind=kLoop, calls=%fused_computation.6 | loop fusion | bytes 589824
  11.5 2.1 %collective-permute-done.3 = bf16[96,1024]{1,0:T(8,128)(2,1)S(1)} collective-permute-done((bf16[96,1024]{1,0:T(8,128)(2,1)}, bf16[96,1024]{1,0:T(8,128)(2,1)S(1)}, u32[]{:S(2)}, u32[]{:S(2)}) %collective-permute-start.3) | collective-permute-done | bytes 196640 | tf_op jit(solution)/shard_map/ppermute | solution.py:28
  13.6 2.6 %collective-permute-start.5 = (bf16[96,1024]{1,0:T(8,128)(2,1)S(1)}, bf16[96,1024]{1,0:T(8,128)(2,1)S(1)}, u32[]{:S(2)}, u32[]{:S(2)}) collective-permute-start(bf16[96,1024]{1,0:T(8,128)(2,1)S(1)} %collective-permute-done.3), channel_id=1, source_target_pairs={{0,48},{1,49},{2,50},{3,51},{4,52},{5,53},{6,54},{7,55},{8,56},{9,... | collective-permute-start | bytes 589832 | tf_op jit(solution)/shard_map/ppermute | solution.py:28
  20.5 3.1 %collective-permute-start.6 = (bf16[768,1024]{1,0:T(8,128)(2,1)}, bf16[768,1024]{1,0:T(8,128)(2,1)}, u32[]{:S(2)}, u32[]{:S(2)}) collective-permute-start(bf16[768,1024]{1,0:T(8,128)(2,1)} %get-tuple-element.9), channel_id=1, source_target_pairs={{0,1},{1,0},{2,3},{3,2},{4,5},{5,4},{6,7},{7,6},{8,9},{9,8},{10,11... | collective-permute-start | bytes 4718600 | tf_op jit(solution)/shard_map/ppermute | solution.py:28
  23.6 5.0 %collective-permute-start.10 = (bf16[96,1024]{1,0:T(8,128)(2,1)S(1)}, bf16[96,1024]{1,0:T(8,128)(2,1)}, u32[]{:S(2)}, u32[]{:S(2)}) collective-permute-start(bf16[96,1024]{1,0:T(8,128)(2,1)S(1)} %copy-done.1), channel_id=1, source_target_pairs={{0,14},{1,15},{2,0},{3,1},{4,2},{5,3},{6,4},{7,5},{8,6},{9,7},{10,... | collective-permute-start | bytes 589832 | tf_op jit(solution)/shard_map/ppermute | solution.py:28
  28.7 2.7 %collective-permute-start.9 = (bf16[96,1024]{1,0:T(8,128)(2,1)S(1)}, bf16[96,1024]{1,0:T(8,128)(2,1)}, u32[]{:S(2)}, u32[]{:S(2)}) collective-permute-start(bf16[96,1024]{1,0:T(8,128)(2,1)S(1)} %copy-done), channel_id=1, source_target_pairs={{0,14},{1,15},{2,0},{3,1},{4,2},{5,3},{6,4},{7,5},{8,6},{9,7},{10,... | collective-permute-start | bytes 589832 | tf_op jit(solution)/shard_map/ppermute | solution.py:28
  36.9 2.7 %collective-permute-start.14 = (bf16[96,1024]{1,0:T(8,128)(2,1)}, bf16[96,1024]{1,0:T(8,128)(2,1)S(1)}, u32[]{:S(2)}, u32[]{:S(2)}) collective-permute-start(bf16[96,1024]{1,0:T(8,128)(2,1)} %collective-permute-done.10.rest_3_), channel_id=1, source_target_pairs={{0,14},{1,15},{2,0},{3,1},{4,2},{5,3},{6,4},{7,5},{8,6},{9,7},{10,... | collective-permute-start | bytes 589832 | tf_op jit(solution)/shard_map/ppermute | solution.py:28
  40.4 2.7 %collective-permute-start.13 = (bf16[96,1024]{1,0:T(8,128)(2,1)}, bf16[96,1024]{1,0:T(8,128)(2,1)S(1)}, u32[]{:S(2)}, u32[]{:S(2)}) collective-permute-start(bf16[96,1024]{1,0:T(8,128)(2,1)} %collective-permute-done.9.rest_2_), channel_id=1, source_target_pairs={{0,14},{1,15},{2,0},{3,1},{4,2},{5,3},{6,4},{7,5},{8,6},{9,7},{10,... | collective-permute-start | bytes 589832 | tf_op jit(solution)/shard_map/ppermute | solution.py:28
  43.6 2.7 %collective-permute-start.18 = (bf16[96,1024]{1,0:T(8,128)(2,1)S(1)}, bf16[96,1024]{1,0:T(8,128)(2,1)S(1)}, u32[]{:S(2)}, u32[]{:S(2)}) collective-permute-start(bf16[96,1024]{1,0:T(8,128)(2,1)S(1)} %collective-permute-done.14.rest_3_), channel_id=1, source_target_pairs={{0,14},{1,15},{2,0},{3,1},{4,2},{5,3},{6,4},{7,5},{8,6},{9,7},{10,... | collective-permute-start | bytes 589832 | tf_op jit(solution)/shard_map/ppermute | solution.py:28
  46.4 2.1 %collective-permute-done.12.rest_1_ = bf16[96,1024]{1,0:T(8,128)(2,1)S(1)} collective-permute-done((bf16[96,1024]{1,0:T(8,128)(2,1)}, bf16[96,1024]{1,0:T(8,128)(2,1)S(1)}, u32[]{:S(2)}, u32[]{:S(2)}) %collective-permute-start.12) | collective-permute-done | bytes 196640 | tf_op jit(solution)/shard_map/ppermute | solution.py:28
  48.5 2.7 %collective-permute-start.17 = (bf16[96,1024]{1,0:T(8,128)(2,1)S(1)}, bf16[96,1024]{1,0:T(8,128)(2,1)S(1)}, u32[]{:S(2)}, u32[]{:S(2)}) collective-permute-start(bf16[96,1024]{1,0:T(8,128)(2,1)S(1)} %collective-permute-done.13.rest_2_), channel_id=1, source_target_pairs={{0,14},{1,15},{2,0},{3,1},{4,2},{5,3},{6,4},{7,5},{8,6},{9,7},{10,... | collective-permute-start | bytes 589832 | tf_op jit(solution)/shard_map/ppermute | solution.py:28
  52.4 2.7 %collective-permute-start.20 = (bf16[96,1024]{1,0:T(8,128)(2,1)S(1)}, bf16[96,1024]{1,0:T(8,128)(2,1)S(1)}, u32[]{:S(2)}, u32[]{:S(2)}) collective-permute-start(bf16[96,1024]{1,0:T(8,128)(2,1)S(1)} %collective-permute-done.18.rest_3_), channel_id=1, source_target_pairs={{0,14},{1,15},{2,0},{3,1},{4,2},{5,3},{6,4},{7,5},{8,6},{9,7},{10,... | collective-permute-start | bytes 589832 | tf_op jit(solution)/shard_map/ppermute | solution.py:28
  56.6 2.6 %match.5.best_ref = f32[8,1536]{1,0:T(8,128)S(1)} custom-call(s32[2]{0:T(128)S(1)} %pad_add_fusion.4.starts_ref, s32[1,1536]{1,0:T(1,128)S(1)} %compare_select_fusion.lo_ref, s32[1,1536]{1,0:T(1,128)S(1)} %broadcast_in_dim.13.hi_ref, f32[8,1536]{1,0:T(8,128)S(1)} %broadcast_in_dim.14.best_ref, ...), custom_call_target="tpu_custom_call" | custom-call | flops 603979776 | bytes 3538944 | tf_op jit(solution)/shard_map/match/pallas_call | solution.py:72
  59.2 5.3 %match.6.best_ref = f32[8,1536]{1,0:T(8,128)S(1)} custom-call(s32[4]{0:T(128)S(1)} %pad_add_fusion.3.starts_ref, s32[1,1536]{1,0:T(1,128)S(1)} %compare_select_fusion.lo_ref, s32[1,1536]{1,0:T(1,128)S(1)} %broadcast_in_dim.13.hi_ref, f32[8,1536]{1,0:T(8,128)S(1)} %match.5.best_ref, bf16[1536,1024]{1,0:T(8,128)(2,1)S(1)} %constant_dynamic-update-slice_fusion.8.right_ref, ...), custom_call_target="tpu_custom_call" | custom-call | flops 1207959552 | bytes 3932160 | tf_op jit(solution)/shard_map/match/pallas_call | solution.py:72
  64.5 4.7 %match.7.best_ref = f32[8,1536]{1,0:T(8,128)S(1)} custom-call(s32[4]{0:T(128)S(1)} %pad_add_fusion.2.starts_ref, s32[1,1536]{1,0:T(1,128)S(1)} %compare_select_fusion.lo_ref, s32[1,1536]{1,0:T(1,128)S(1)} %broadcast_in_dim.13.hi_ref, f32[8,1536]{1,0:T(8,128)S(1)} %match.6.best_ref, bf16[1536,1024]{1,0:T(8,128)(2,1)S(1)} %constant_dynamic-update-slice_fusion.8.right_ref, ...), custom_call_target="tpu_custom_call" | custom-call | flops 1207959552 | bytes 3932160 | tf_op jit(solution)/shard_map/match/pallas_call | solution.py:72
  69.2 4.6 %match.8.best_ref = f32[8,1536]{1,0:T(8,128)S(1)} custom-call(s32[4]{0:T(128)S(1)} %pad_add_fusion.1.starts_ref, s32[1,1536]{1,0:T(1,128)S(1)} %compare_select_fusion.lo_ref, s32[1,1536]{1,0:T(1,128)S(1)} %broadcast_in_dim.13.hi_ref, f32[8,1536]{1,0:T(8,128)S(1)} %match.7.best_ref, bf16[1536,1024]{1,0:T(8,128)(2,1)S(1)} %constant_dynamic-update-slice_fusion.8.right_ref, ...), custom_call_target="tpu_custom_call" | custom-call | flops 1207959552 | bytes 3932160 | tf_op jit(solution)/shard_map/match/pallas_call | solution.py:72
  73.9 2.7 %match.9 = f32[8,1536]{1,0:T(8,128)S(1)} custom-call(s32[2]{0:T(128)S(1)} %pad_add_fusion.starts_ref, s32[1,1536]{1,0:T(1,128)S(1)} %compare_select_fusion.lo_ref, s32[1,1536]{1,0:T(1,128)S(1)} %broadcast_in_dim.13.hi_ref, f32[8,1536]{1,0:T(8,128)S(1)} %match.8.best_ref, bf16[1536,1024]{1,0:T(8,128)(2,1)S(1)} %constant_dynamic-update-slice_fusion.8.right_ref, ...), custom_call_target="tpu_custom_call" | custom-call | flops 603979776 | bytes 3538944 | tf_op jit(solution)/shard_map/match/pallas_call | solution.py:72
  76.7 3.4 %collective-permute-start.21 = (f32[4,192]{1,0:T(4,128)S(1)}, f32[4,192]{1,0:T(4,128)S(1)}, u32[]{:S(2)}, u32[]{:S(2)}) collective-permute-start(f32[4,192]{1,0:T(4,128)S(1)} %squeeze.23), channel_id=1, source_target_pairs={{0,1},{1,0},{2,3},{3,2},{4,5},{5,4},{6,7},{7,6},{8,9},{9,8},{10,11... | collective-permute-start | bytes 9224 | tf_op jit(solution)/shard_map/ppermute | solution.py:28
  80.9 3.1 %collective-permute-start.22 = (f32[192]{0:T(256)S(1)}, f32[192]{0:T(256)S(1)}, u32[]{:S(2)}, u32[]{:S(2)}) collective-permute-start(f32[192]{0:T(256)S(1)} %bitcast.41), channel_id=1, source_target_pairs={{0,48},{1,49},{2,50},{3,51},{4,52},{5,53},{6,54},{7,55},{8,56},{9,... | collective-permute-start | bytes 2312 | tf_op jit(solution)/shard_map/ppermute | solution.py:28
  85.2 2.4 %collective-permute-done.23 = f32[192]{0:T(256)S(1)} collective-permute-done((f32[192]{0:T(256)S(1)}, f32[192]{0:T(256)S(1)}, u32[]{:S(2)}, u32[]{:S(2)}) %collective-permute-start.23) | collective-permute-done | bytes 800 | tf_op jit(solution)/shard_map/ppermute | solution.py:28
  (70 shorter events, 18.0 us)
Async XLA Ops:
  1.9 9.6 %collective-permute-start = (bf16[96,1024]{1,0:T(8,128)(2,1)}, bf16[96,1024]{1,0:T(8,128)(2,1)S(1)}, u32[]{:S(2)}, u32[]{:S(2)}) collective-permute-start(bf16[96,1024]{1,0:T(8,128)(2,1)} %get-tuple-element.7.rest_0_), channel_id=1, source_target_pairs={{0,16},{1,17},{2,18},{3,19},{4,20},{5,21},{6,22},{7,23},{8,24},{9,... | collective-permute-start | bytes 589832 | tf_op jit(solution)/shard_map/ppermute | solution.py:28
  4.0 13.6 %collective-permute-start.2 = (bf16[96,1024]{1,0:T(8,128)(2,1)}, bf16[96,1024]{1,0:T(8,128)(2,1)S(1)}, u32[]{:S(2)}, u32[]{:S(2)}) collective-permute-start(bf16[96,1024]{1,0:T(8,128)(2,1)} %get-tuple-element.7.rest_0_), channel_id=1, source_target_pairs={{0,48},{1,49},{2,50},{3,51},{4,52},{5,53},{6,54},{7,55},{8,56},{9,... | collective-permute-start | bytes 589832 | tf_op jit(solution)/shard_map/ppermute | solution.py:28
  5.5 11.4 %collective-permute-start.1 = (bf16[96,1024]{1,0:T(8,128)(2,1)}, bf16[96,1024]{1,0:T(8,128)(2,1)S(1)}, u32[]{:S(2)}, u32[]{:S(2)}) collective-permute-start(bf16[96,1024]{1,0:T(8,128)(2,1)} %get-tuple-element.8.rest_1_), channel_id=1, source_target_pairs={{0,16},{1,17},{2,18},{3,19},{4,20},{5,21},{6,22},{7,23},{8,24},{9,... | collective-permute-start | bytes 589832 | tf_op jit(solution)/shard_map/ppermute | solution.py:28
  5.5 8.1 %collective-permute-start.3 = (bf16[96,1024]{1,0:T(8,128)(2,1)}, bf16[96,1024]{1,0:T(8,128)(2,1)S(1)}, u32[]{:S(2)}, u32[]{:S(2)}) collective-permute-start(bf16[96,1024]{1,0:T(8,128)(2,1)} %get-tuple-element.8.rest_1_), channel_id=1, source_target_pairs={{0,48},{1,49},{2,50},{3,51},{4,52},{5,53},{6,54},{7,55},{8,56},{9,... | collective-permute-start | bytes 589832 | tf_op jit(solution)/shard_map/ppermute | solution.py:28
  11.5 7.6 %collective-permute-start.4 = (bf16[96,1024]{1,0:T(8,128)(2,1)S(1)}, bf16[96,1024]{1,0:T(8,128)(2,1)S(1)}, u32[]{:S(2)}, u32[]{:S(2)}) collective-permute-start(bf16[96,1024]{1,0:T(8,128)(2,1)S(1)} %collective-permute-done), channel_id=1, source_target_pairs={{0,16},{1,17},{2,18},{3,19},{4,20},{5,21},{6,22},{7,23},{8,24},{9,... | collective-permute-start | bytes 589832 | tf_op jit(solution)/shard_map/ppermute | solution.py:28
  13.6 6.2 %collective-permute-start.5 = (bf16[96,1024]{1,0:T(8,128)(2,1)S(1)}, bf16[96,1024]{1,0:T(8,128)(2,1)S(1)}, u32[]{:S(2)}, u32[]{:S(2)}) collective-permute-start(bf16[96,1024]{1,0:T(8,128)(2,1)S(1)} %collective-permute-done.3), channel_id=1, source_target_pairs={{0,48},{1,49},{2,50},{3,51},{4,52},{5,53},{6,54},{7,55},{8,56},{9,... | collective-permute-start | bytes 589832 | tf_op jit(solution)/shard_map/ppermute | solution.py:28
  20.5 34.6 %collective-permute-start.6 = (bf16[768,1024]{1,0:T(8,128)(2,1)}, bf16[768,1024]{1,0:T(8,128)(2,1)}, u32[]{:S(2)}, u32[]{:S(2)}) collective-permute-start(bf16[768,1024]{1,0:T(8,128)(2,1)} %get-tuple-element.9), channel_id=1, source_target_pairs={{0,1},{1,0},{2,3},{3,2},{4,5},{5,4},{6,7},{7,6},{8,9},{9,8},{10,11... | collective-permute-start | bytes 4718600 | tf_op jit(solution)/shard_map/ppermute | solution.py:28
  23.6 13.2 %collective-permute-start.10 = (bf16[96,1024]{1,0:T(8,128)(2,1)S(1)}, bf16[96,1024]{1,0:T(8,128)(2,1)}, u32[]{:S(2)}, u32[]{:S(2)}) collective-permute-start(bf16[96,1024]{1,0:T(8,128)(2,1)S(1)} %copy-done.1), channel_id=1, source_target_pairs={{0,14},{1,15},{2,0},{3,1},{4,2},{5,3},{6,4},{7,5},{8,6},{9,7},{10,... | collective-permute-start | bytes 589832 | tf_op jit(solution)/shard_map/ppermute | solution.py:28
  28.7 8.1 %collective-permute-start.7 = (bf16[96,1024]{1,0:T(8,128)(2,1)S(1)}, bf16[96,1024]{1,0:T(8,128)(2,1)}, u32[]{:S(2)}, u32[]{:S(2)}) collective-permute-start(bf16[96,1024]{1,0:T(8,128)(2,1)S(1)} %copy-done), channel_id=1, source_target_pairs={{0,2},{1,3},{2,4},{3,5},{4,6},{5,7},{6,8},{7,9},{8,10},{9,11},{10,... | collective-permute-start | bytes 589832 | tf_op jit(solution)/shard_map/ppermute | solution.py:28
  28.7 11.7 %collective-permute-start.8 = (bf16[96,1024]{1,0:T(8,128)(2,1)S(1)}, bf16[96,1024]{1,0:T(8,128)(2,1)}, u32[]{:S(2)}, u32[]{:S(2)}) collective-permute-start(bf16[96,1024]{1,0:T(8,128)(2,1)S(1)} %copy-done.1), channel_id=1, source_target_pairs={{0,2},{1,3},{2,4},{3,5},{4,6},{5,7},{6,8},{7,9},{8,10},{9,11},{10,... | collective-permute-start | bytes 589832 | tf_op jit(solution)/shard_map/ppermute | solution.py:28
  28.7 11.7 %collective-permute-start.9 = (bf16[96,1024]{1,0:T(8,128)(2,1)S(1)}, bf16[96,1024]{1,0:T(8,128)(2,1)}, u32[]{:S(2)}, u32[]{:S(2)}) collective-permute-start(bf16[96,1024]{1,0:T(8,128)(2,1)S(1)} %copy-done), channel_id=1, source_target_pairs={{0,14},{1,15},{2,0},{3,1},{4,2},{5,3},{6,4},{7,5},{8,6},{9,7},{10,... | collective-permute-start | bytes 589832 | tf_op jit(solution)/shard_map/ppermute | solution.py:28
  36.8 6.8 %collective-permute-start.11 = (bf16[96,1024]{1,0:T(8,128)(2,1)}, bf16[96,1024]{1,0:T(8,128)(2,1)S(1)}, u32[]{:S(2)}, u32[]{:S(2)}) collective-permute-start(bf16[96,1024]{1,0:T(8,128)(2,1)} %collective-permute-done.7.rest_0_), channel_id=1, source_target_pairs={{0,2},{1,3},{2,4},{3,5},{4,6},{5,7},{6,8},{7,9},{8,10},{9,11},{10,... | collective-permute-start | bytes 589832 | tf_op jit(solution)/shard_map/ppermute | solution.py:28
  36.9 6.7 %collective-permute-start.14 = (bf16[96,1024]{1,0:T(8,128)(2,1)}, bf16[96,1024]{1,0:T(8,128)(2,1)S(1)}, u32[]{:S(2)}, u32[]{:S(2)}) collective-permute-start(bf16[96,1024]{1,0:T(8,128)(2,1)} %collective-permute-done.10.rest_3_), channel_id=1, source_target_pairs={{0,14},{1,15},{2,0},{3,1},{4,2},{5,3},{6,4},{7,5},{8,6},{9,7},{10,... | collective-permute-start | bytes 589832 | tf_op jit(solution)/shard_map/ppermute | solution.py:28
  40.4 8.1 %collective-permute-start.12 = (bf16[96,1024]{1,0:T(8,128)(2,1)}, bf16[96,1024]{1,0:T(8,128)(2,1)S(1)}, u32[]{:S(2)}, u32[]{:S(2)}) collective-permute-start(bf16[96,1024]{1,0:T(8,128)(2,1)} %collective-permute-done.8.rest_1_), channel_id=1, source_target_pairs={{0,2},{1,3},{2,4},{3,5},{4,6},{5,7},{6,8},{7,9},{8,10},{9,11},{10,... | collective-permute-start | bytes 589832 | tf_op jit(solution)/shard_map/ppermute | solution.py:28
  40.4 8.1 %collective-permute-start.13 = (bf16[96,1024]{1,0:T(8,128)(2,1)}, bf16[96,1024]{1,0:T(8,128)(2,1)S(1)}, u32[]{:S(2)}, u32[]{:S(2)}) collective-permute-start(bf16[96,1024]{1,0:T(8,128)(2,1)} %collective-permute-done.9.rest_2_), channel_id=1, source_target_pairs={{0,14},{1,15},{2,0},{3,1},{4,2},{5,3},{6,4},{7,5},{8,6},{9,7},{10,... | collective-permute-start | bytes 589832 | tf_op jit(solution)/shard_map/ppermute | solution.py:28
  43.6 8.8 %collective-permute-start.15 = (bf16[96,1024]{1,0:T(8,128)(2,1)S(1)}, bf16[96,1024]{1,0:T(8,128)(2,1)S(1)}, u32[]{:S(2)}, u32[]{:S(2)}) collective-permute-start(bf16[96,1024]{1,0:T(8,128)(2,1)S(1)} %collective-permute-done.11.rest_0_), channel_id=1, source_target_pairs={{0,2},{1,3},{2,4},{3,5},{4,6},{5,7},{6,8},{7,9},{8,10},{9,11},{10,... | collective-permute-start | bytes 589832 | tf_op jit(solution)/shard_map/ppermute | solution.py:28
  43.6 8.8 %collective-permute-start.18 = (bf16[96,1024]{1,0:T(8,128)(2,1)S(1)}, bf16[96,1024]{1,0:T(8,128)(2,1)S(1)}, u32[]{:S(2)}, u32[]{:S(2)}) collective-permute-start(bf16[96,1024]{1,0:T(8,128)(2,1)S(1)} %collective-permute-done.14.rest_3_), channel_id=1, source_target_pairs={{0,14},{1,15},{2,0},{3,1},{4,2},{5,3},{6,4},{7,5},{8,6},{9,7},{10,... | collective-permute-start | bytes 589832 | tf_op jit(solution)/shard_map/ppermute | solution.py:28
  48.5 20.7 %collective-permute-start.16 = (bf16[96,1024]{1,0:T(8,128)(2,1)S(1)}, bf16[96,1024]{1,0:T(8,128)(2,1)S(1)}, u32[]{:S(2)}, u32[]{:S(2)}) collective-permute-start(bf16[96,1024]{1,0:T(8,128)(2,1)S(1)} %collective-permute-done.12.rest_1_), channel_id=1, source_target_pairs={{0,2},{1,3},{2,4},{3,5},{4,6},{5,7},{6,8},{7,9},{8,10},{9,11},{10,... | collective-permute-start | bytes 589832 | tf_op jit(solution)/shard_map/ppermute | solution.py:28
  48.5 20.7 %collective-permute-start.17 = (bf16[96,1024]{1,0:T(8,128)(2,1)S(1)}, bf16[96,1024]{1,0:T(8,128)(2,1)S(1)}, u32[]{:S(2)}, u32[]{:S(2)}) collective-permute-start(bf16[96,1024]{1,0:T(8,128)(2,1)S(1)} %collective-permute-done.13.rest_2_), channel_id=1, source_target_pairs={{0,14},{1,15},{2,0},{3,1},{4,2},{5,3},{6,4},{7,5},{8,6},{9,7},{10,... | collective-permute-start | bytes 589832 | tf_op jit(solution)/shard_map/ppermute | solution.py:28
  52.4 21.5 %collective-permute-start.19 = (bf16[96,1024]{1,0:T(8,128)(2,1)S(1)}, bf16[96,1024]{1,0:T(8,128)(2,1)S(1)}, u32[]{:S(2)}, u32[]{:S(2)}) collective-permute-start(bf16[96,1024]{1,0:T(8,128)(2,1)S(1)} %collective-permute-done.15.rest_0_), channel_id=1, source_target_pairs={{0,2},{1,3},{2,4},{3,5},{4,6},{5,7},{6,8},{7,9},{8,10},{9,11},{10,... | collective-permute-start | bytes 589832 | tf_op jit(solution)/shard_map/ppermute | solution.py:28
  52.4 21.5 %collective-permute-start.20 = (bf16[96,1024]{1,0:T(8,128)(2,1)S(1)}, bf16[96,1024]{1,0:T(8,128)(2,1)S(1)}, u32[]{:S(2)}, u32[]{:S(2)}) collective-permute-start(bf16[96,1024]{1,0:T(8,128)(2,1)S(1)} %collective-permute-done.18.rest_3_), channel_id=1, source_target_pairs={{0,14},{1,15},{2,0},{3,1},{4,2},{5,3},{6,4},{7,5},{8,6},{9,7},{10,... | collective-permute-start | bytes 589832 | tf_op jit(solution)/shard_map/ppermute | solution.py:28
  76.7 4.2 %collective-permute-start.21 = (f32[4,192]{1,0:T(4,128)S(1)}, f32[4,192]{1,0:T(4,128)S(1)}, u32[]{:S(2)}, u32[]{:S(2)}) collective-permute-start(f32[4,192]{1,0:T(4,128)S(1)} %squeeze.23), channel_id=1, source_target_pairs={{0,1},{1,0},{2,3},{3,2},{4,5},{5,4},{6,7},{7,6},{8,9},{9,8},{10,11... | collective-permute-start | bytes 9224 | tf_op jit(solution)/shard_map/ppermute | solution.py:28
  80.9 4.3 %collective-permute-start.22 = (f32[192]{0:T(256)S(1)}, f32[192]{0:T(256)S(1)}, u32[]{:S(2)}, u32[]{:S(2)}) collective-permute-start(f32[192]{0:T(256)S(1)} %bitcast.41), channel_id=1, source_target_pairs={{0,48},{1,49},{2,50},{3,51},{4,52},{5,53},{6,54},{7,55},{8,56},{9,... | collective-permute-start | bytes 2312 | tf_op jit(solution)/shard_map/ppermute | solution.py:28
  84.0 3.9 %collective-permute-start.24 = (f32[192]{0:T(256)S(1)}, f32[192]{0:T(256)S(1)}, u32[]{:S(2)}, u32[]{:S(2)}) collective-permute-start(f32[192]{0:T(256)S(1)} %bitcast.39), channel_id=1, source_target_pairs={{0,32},{1,33},{2,34},{3,35},{4,36},{5,37},{6,38},{7,39},{8,40},{9,... | collective-permute-start | bytes 2312 | tf_op jit(solution)/shard_map/ppermute | solution.py:28
  (5 other events, 57.4 us)

commit v2 on v0

v2 whole, which is shorter than its diff:
```python
import functools

import jax
import jax.numpy as jnp
from jax import lax
from jax.experimental import pallas as pl
from jax.experimental.pallas import tpu as pltpu
from jax.sharding import PartitionSpec as P

Y, Z, CORES = 4, 8, 2
ROWS = 192
SEGMENTS = Y * CORES
WIDE = SEGMENTS * ROWS
TILE = 256
D = 1024
NONE = -2.0
VMEM = pl.BlockSpec(memory_space=pltpu.VMEM)
SMEM = pl.BlockSpec(memory_space=pltpu.SMEM)


def device(y, z, core):
    return ((y % Y) * Z + z % Z) * CORES + core % CORES


def permute(value, target):
    pairs = [
        (device(y, z, core), device(*target(y, z, core)))
        for y in range(Y)
        for z in range(Z)
        for core in range(CORES)
    ]
    return lax.ppermute(value, "member", pairs)


def along_y(value, dy):
    return permute(value, lambda y, z, core: (y + dy, z, core))


def along_z(value):
    return permute(value, lambda y, z, core: (y, z + (1, -1)[core], core))


def swap(value):
    return permute(value, lambda y, z, core: (y, z, core + 1))


def normalize_kernel(rows_ref, unit_ref):
    values = rows_ref[...].astype(jnp.float32)
    unit_ref[...] = (
        values * lax.rsqrt(jnp.sum(values * values, axis=1, keepdims=True) + 1e-06)
    ).astype(jnp.bfloat16)


def normalize(rows):
    return pl.pallas_call(
        normalize_kernel,
        out_shape=jax.ShapeDtypeStruct((ROWS, D), jnp.bfloat16),
        in_specs=[VMEM],
        out_specs=VMEM,
        cost_estimate=pl.CostEstimate(flops=4 * ROWS * D, bytes_accessed=4 * ROWS * D, transcendentals=ROWS),
        compiler_params=pltpu.CompilerParams(vmem_limit_bytes=8 * 1024 * 1024),
        name="normalize",
    )(rows)


def fold(starts_ref, lo_ref, hi_ref, best_ref, right_ref, left, out_ref):
    for n in range(WIDE // TILE):
        lanes = slice(n * TILE, (n + 1) * TILE)
        scores = lax.dot_general(
            left[...], right_ref[lanes, :], (((1,), (1,)), ((), ())), preferred_element_type=jnp.float32
        )
        lo, hi = lo_ref[:, lanes], hi_ref[:, lanes]
        best = None if best_ref is None else best_ref[:, lanes]
        for i in range(left.shape[0] // ROWS):
            index = starts_ref[i] + lax.broadcasted_iota(jnp.int32, (ROWS, TILE), 0)
            part = jnp.where((index >= lo) & (index < hi), scores[i * ROWS : (i + 1) * ROWS], NONE)
            part = jnp.max(part.reshape(-1, 8, TILE), axis=0)
            best = part if best is None else jnp.maximum(best, part)
        out_ref[:, lanes] = best


def stack(piece_refs, left):
    if len(piece_refs) == 1:
        return piece_refs[0]
    for i, piece_ref in enumerate(piece_refs):
        left[i * ROWS : (i + 1) * ROWS, :] = piece_ref[...]
    return left


def first_kernel(starts_ref, lo_ref, hi_ref, *refs):
    segments, pieces = refs[:SEGMENTS], refs[SEGMENTS:-3]
    right_ref, out_ref, left = refs[-3:]
    for i, segment in enumerate(segments):
        right_ref[i * ROWS : (i + 1) * ROWS, :] = segment[...]
    fold(starts_ref, lo_ref, hi_ref, None, right_ref, stack(pieces, left), out_ref)


def match_kernel(starts_ref, lo_ref, hi_ref, best_ref, right_ref, *refs):
    pieces, (out_ref, left) = refs[:-2], refs[-2:]
    fold(starts_ref, lo_ref, hi_ref, best_ref, right_ref, stack(pieces, left), out_ref)


def match(kernel, starts, lo, hi, others, pieces):
    rows = ROWS * len(pieces)
    best = jax.ShapeDtypeStruct((8, WIDE), jnp.float32)
    first = kernel is first_kernel
    return pl.pallas_call(
        kernel,
        out_shape=(jax.ShapeDtypeStruct((WIDE, D), jnp.bfloat16), best) if first else best,
        in_specs=[SMEM] + [VMEM] * (2 + len(others) + len(pieces)),
        out_specs=(VMEM, VMEM) if first else VMEM,
        scratch_shapes=[pltpu.VMEM((rows, D), jnp.bfloat16)],
        cost_estimate=pl.CostEstimate(
            flops=2 * rows * WIDE * D, bytes_accessed=2 * D * (rows + WIDE), transcendentals=0
        ),
        compiler_params=pltpu.CompilerParams(vmem_limit_bytes=16 * 1024 * 1024),
        name="match",
    )(jnp.stack(starts), lo, hi, *others, *pieces)


def shards(embeddings, first_size):
    member = lax.axis_index("member")
    core = member % CORES
    z = member // CORES % Z
    y = member // (CORES * Z)
    split = first_size[0]
    toward = 2 * core - 1

    unit = normalize(embeddings)

    def start(dy, dz, dcore):
        return device(y + dy, z + dz, core + dcore) * ROWS

    segment = jnp.arange(SEGMENTS, dtype=jnp.int32)[:, None]
    segment_dy = jnp.array([0, 3, 1, 2], jnp.int32)[segment % Y]
    row_index = start(segment_dy, 0, segment // Y) + jnp.arange(ROWS, dtype=jnp.int32)[None]
    row_index = row_index.reshape(1, WIDE)
    lo = jnp.where(row_index >= split, split, 0)

    own, other = [unit], [swap(unit)]
    for _ in range(3):
        own.append(along_z(own[-1]))
        other.append(along_z(other[-1]))
    own.append(along_z(own[-1]))

    mine = [unit] + [along_y(unit, dy) for dy in (1, -1, 2)]
    theirs = [other[0]] + [swap(segment) for segment in mine[1:]]

    def starts(pieces):
        return [start(0, toward * k, dcore) for k, dcore in pieces]

    right, best = match(
        first_kernel,
        starts([(0, 0), (1, 0), (1, 1)]),
        lo,
        row_index,
        mine + theirs,
        [unit, own[1], other[1]],
    )
    for k in (2, 3):
        best = match(
            match_kernel, starts([(k, 0), (k, 1)]), lo, row_index, [best, right], [own[k], other[k]]
        )
    best = match(match_kernel, starts([(4, 0)]), lo, row_index, [best, right], [own[4]])

    best = jnp.max(best, axis=0).reshape(CORES, Y, ROWS)
    best = jnp.maximum(best[0], swap(best[1]))
    best = jnp.maximum(
        jnp.maximum(best[0], along_y(best[1], -1)),
        jnp.maximum(along_y(best[2], 1), along_y(best[3], 2)),
    )
    return jnp.maximum(best, -1.0)


def solution(mesh):
    placed = (P(("group", "member"), None), P("group"))
    return jax.shard_map(
        shards, mesh=mesh, in_specs=placed, out_specs=P(("group", "member")), check_vma=False
    )
```

time: 157 us -> 58.5 us (0.37)
  waiting for transfers between devices: 125 us -> 11 us
  starting transfers between devices: 0.01 us -> 34.5 us
  matrix products: 14 us -> 0 us
  between operations: 14.1 us -> 0.8 us
  Pallas kernels: 0 us -> 8.39 us
  other arithmetic: 3.68 us -> 0.92 us
  local copies, waits for them, and re-layouts: 0 us -> 2.54 us
    all_gather x1 -> x0, waiting for transfers between devices: 125 us -> none  [shards(): piece = lax.all_gather(unit, 'member', axis=0, tiled=True)]
    ppermute x0 -> x18, starting transfers between devices: none -> 34.5 us  [permute(): return lax.ppermute(value, 'member', pairs)]
    dot_general x1 -> x0, matrix products: 14 us -> none  [tile_scores(): jnp.einsum('rd,cd->rc', left, right, preferred_element_type=jnp.float32)]
    ppermute x0 -> x18, waiting for transfers between devices: none -> 11 us  [permute(): return lax.ppermute(value, 'member', pairs)]
    pallas_call x0 -> x5, Pallas kernels: none -> 8.39 us  [the longest x4 8.23 us: match(): pl.pallas_call(kernel, out_shape=(jax.ShapeDtypeStruct((WIDE, D), jnp.bfl...]
    convert_element_type x1 -> x0, other arithmetic: 1.93 us -> none  [normalize(): (values * lax.rsqrt(jnp.sum(values * values, axis=1, keepdims=True) + 1e-...]
  transfers between devices with their start and end apart: 1 -> 18, of which waited for: 1 -> 7; matrix products, arithmetic and copies ran while one was open for 0% -> 3% of each run, Pallas kernels for 0% -> 12%
where the time goes in v2:
time: 58.5 us; the launch traced here: 58.1 us
  starting transfers between devices  34.5 us (59%)
  waiting for transfers between devices  11 us (19%)
  Pallas kernels  8.39 us (14%)
  local copies, waits for them, and re-layouts  2.54 us (4%)
  other arithmetic  0.92 us (2%)
  between operations  0.8 us (1%)
    ppermute x18, starting transfers between devices, permute(): return lax.ppermute(value, 'member', pairs)  34.5 us
    ppermute x18, waiting for transfers between devices, permute(): return lax.ppermute(value, 'member', pairs)  11 us
    pallas_call x4, Pallas kernels, match(): pl.pallas_call(kernel, out_shape=(jax.ShapeDtypeStruct((WIDE, D), jnp.bfl...  8.23 us
    gather x1, local copies, waits for them, and re-layouts, shards(): segment_dy = jnp.array([0, 3, 1, 2], jnp.int32)[segment % Y]  1.3 us
  transfers between devices with their start and end apart: 18, of which 7 were waited for; matrix products, arithmetic and copies ran while one was open for 3% of the time, Pallas kernels for 12%

profile of v2, /device:TPU:1, one launch (start us, length us, event | category | flops | bytes accessed | tf_op | source)
XLA Modules:
  0.0 58.1 jit_solution(3526962132878790288)
XLA Ops:
  0.0 1.0 %copy-done = bf16[192,1024]{1,0:T(8,128)(2,1)S(1)} copy-done((bf16[192,1024]{1,0:T(8,128)(2,1)S(1)}, bf16[192,1024]{1,0:T(8,128)(2,1)}, u32[]{:S(2)}) %copy-start) | copy-done | bytes 393240
  1.2 2.2 %collective-permute-start = (bf16[192,1024]{1,0:T(8,128)(2,1)S(1)}, bf16[192,1024]{1,0:T(8,128)(2,1)S(1)}, u32[]{:S(2)}, u32[]{:S(2)}) collective-permute-start(bf16[192,1024]{1,0:T(8,128)(2,1)S(1)} %normalize.1.refs_0_.refs_8_), channel_id=1, source_target_pairs={{0,16},{1,17},{2,18},{3,19},{4,20},{5,21},{6,22},{7,23},{8,24},{9,... | collective-permute-start | bytes 1179656 | tf_op jit(solution)/shard_map/ppermute | solution.py:32
  3.4 1.5 %collective-permute-start.1 = (bf16[192,1024]{1,0:T(8,128)(2,1)S(1)}, bf16[192,1024]{1,0:T(8,128)(2,1)S(1)}, u32[]{:S(2)}, u32[]{:S(2)}) collective-permute-start(bf16[192,1024]{1,0:T(8,128)(2,1)S(1)} %normalize.1.refs_0_.refs_8_), channel_id=1, source_target_pairs={{0,48},{1,49},{2,50},{3,51},{4,52},{5,53},{6,54},{7,55},{8,56},{9,... | collective-permute-start | bytes 1179656 | tf_op jit(solution)/shard_map/ppermute | solution.py:32
  4.9 1.6 %collective-permute-start.2 = (bf16[192,1024]{1,0:T(8,128)(2,1)S(1)}, bf16[192,1024]{1,0:T(8,128)(2,1)S(1)}, u32[]{:S(2)}, u32[]{:S(2)}) collective-permute-start(bf16[192,1024]{1,0:T(8,128)(2,1)S(1)} %normalize.1.refs_0_.refs_8_), channel_id=1, source_target_pairs={{0,32},{1,33},{2,34},{3,35},{4,36},{5,37},{6,38},{7,39},{8,40},{9,... | collective-permute-start | bytes 1179656 | tf_op jit(solution)/shard_map/ppermute | solution.py:32
  6.5 1.5 %collective-permute-start.3 = (bf16[192,1024]{1,0:T(8,128)(2,1)S(1)}, bf16[192,1024]{1,0:T(8,128)(2,1)S(1)}, u32[]{:S(2)}, u32[]{:S(2)}) collective-permute-start(bf16[192,1024]{1,0:T(8,128)(2,1)S(1)} %normalize.1.refs_0_.refs_8_), channel_id=1, source_target_pairs={{0,1},{1,0},{2,3},{3,2},{4,5},{5,4},{6,7},{7,6},{8,9},{9,8},{10,11... | collective-permute-start | bytes 1179656 | tf_op jit(solution)/shard_map/ppermute | solution.py:32
  8.0 5.6 %collective-permute-start.7 = (bf16[192,1024]{1,0:T(8,128)(2,1)S(1)}, bf16[192,1024]{1,0:T(8,128)(2,1)S(1)}, u32[]{:S(2)}, u32[]{:S(2)}) collective-permute-start(bf16[192,1024]{1,0:T(8,128)(2,1)S(1)} %normalize.1.refs_0_.refs_8_), channel_id=1, source_target_pairs={{0,2},{1,15},{2,4},{3,1},{4,6},{5,3},{6,8},{7,5},{8,10},{9,7},{10,... | collective-permute-start | bytes 1179656 | tf_op jit(solution)/shard_map/ppermute | solution.py:32
  13.6 1.3 %gather_fusion = s32[8]{0:T(128)S(1)} fusion(s32[4]{0:T(128)} %constant.168.clone, s32[1024]{0:T(1024)S(1)} %pad_clamp_fusion), kind=kCustom, calls=%fused_computation | custom fusion | bytes 96 | tf_op jit(solution)/shard_map/gather | solution.py:135
  15.7 2.6 %collective-permute-done.7.refs_9_ = bf16[192,1024]{1,0:T(8,128)(2,1)S(1)} collective-permute-done((bf16[192,1024]{1,0:T(8,128)(2,1)S(1)}, bf16[192,1024]{1,0:T(8,128)(2,1)S(1)}, u32[]{:S(2)}, u32[]{:S(2)}) %collective-permute-start.7) | collective-permute-done | bytes 393248 | tf_op jit(solution)/shard_map/ppermute | solution.py:32
  18.3 3.1 %collective-permute-start.9 = (bf16[192,1024]{1,0:T(8,128)(2,1)S(1)}, bf16[192,1024]{1,0:T(8,128)(2,1)S(1)}, u32[]{:S(2)}, u32[]{:S(2)}) collective-permute-start(bf16[192,1024]{1,0:T(8,128)(2,1)S(1)} %collective-permute-done.7.refs_9_), channel_id=1, source_target_pairs={{0,2},{1,15},{2,4},{3,1},{4,6},{5,3},{6,8},{7,5},{8,10},{9,7},{10,... | collective-permute-start | bytes 1179656 | tf_op jit(solution)/shard_map/ppermute | solution.py:32
  22.9 1.5 %collective-permute-start.6 = (bf16[192,1024]{1,0:T(8,128)(2,1)S(1)}, bf16[192,1024]{1,0:T(8,128)(2,1)S(1)}, u32[]{:S(2)}, u32[]{:S(2)}) collective-permute-start(bf16[192,1024]{1,0:T(8,128)(2,1)S(1)} %collective-permute-done.2.refs_3_), channel_id=1, source_target_pairs={{0,1},{1,0},{2,3},{3,2},{4,5},{5,4},{6,7},{7,6},{8,9},{9,8},{10,11... | collective-permute-start | bytes 1179656 | tf_op jit(solution)/shard_map/ppermute | solution.py:32
  24.5 5.6 %collective-permute-start.10 = (bf16[192,1024]{1,0:T(8,128)(2,1)S(1)}, bf16[192,1024]{1,0:T(8,128)(2,1)S(1)}, u32[]{:S(2)}, u32[]{:S(2)}) collective-permute-start(bf16[192,1024]{1,0:T(8,128)(2,1)S(1)} %collective-permute-done.8.refs_10_), channel_id=1, source_target_pairs={{0,2},{1,15},{2,4},{3,1},{4,6},{5,3},{6,8},{7,5},{8,10},{9,7},{10,... | collective-permute-start | bytes 1179656 | tf_op jit(solution)/shard_map/ppermute | solution.py:32
  30.8 4.0 %collective-permute-done.10.refs_1_ = bf16[192,1024]{1,0:T(8,128)(2,1)S(1)} collective-permute-done((bf16[192,1024]{1,0:T(8,128)(2,1)S(1)}, bf16[192,1024]{1,0:T(8,128)(2,1)S(1)}, u32[]{:S(2)}, u32[]{:S(2)}) %collective-permute-start.10) | collective-permute-done | bytes 393248 | tf_op jit(solution)/shard_map/ppermute | solution.py:32
  34.8 3.1 %collective-permute-start.12 = (bf16[192,1024]{1,0:T(8,128)(2,1)S(1)}, bf16[192,1024]{1,0:T(8,128)(2,1)S(1)}, u32[]{:S(2)}, u32[]{:S(2)}) collective-permute-start(bf16[192,1024]{1,0:T(8,128)(2,1)S(1)} %collective-permute-done.10.refs_1_), channel_id=1, source_target_pairs={{0,2},{1,15},{2,4},{3,1},{4,6},{5,3},{6,8},{7,5},{8,10},{9,7},{10,... | collective-permute-start | bytes 1179656 | tf_op jit(solution)/shard_map/ppermute | solution.py:32
  38.0 1.0 %collective-permute-done.11.refs_0_ = bf16[192,1024]{1,0:T(8,128)(2,1)S(1)} collective-permute-done((bf16[192,1024]{1,0:T(8,128)(2,1)S(1)}, bf16[192,1024]{1,0:T(8,128)(2,1)S(1)}, u32[]{:S(2)}, u32[]{:S(2)}) %collective-permute-start.11) | collective-permute-done | bytes 393248 | tf_op jit(solution)/shard_map/ppermute | solution.py:32
  39.0 3.1 %collective-permute-start.13 = (bf16[192,1024]{1,0:T(8,128)(2,1)S(1)}, bf16[192,1024]{1,0:T(8,128)(2,1)S(1)}, u32[]{:S(2)}, u32[]{:S(2)}) collective-permute-start(bf16[192,1024]{1,0:T(8,128)(2,1)S(1)} %collective-permute-done.11.refs_0_), channel_id=1, source_target_pairs={{0,2},{1,15},{2,4},{3,1},{4,6},{5,3},{6,8},{7,5},{8,10},{9,7},{10,... | collective-permute-start | bytes 1179656 | tf_op jit(solution)/shard_map/ppermute | solution.py:32
  42.1 2.8 %match.4 = (bf16[1536,1024]{1,0:T(8,128)(2,1)S(1)}, f32[8,1536]{1,0:T(8,128)S(1)}) custom-call(s32[3]{0:T(128)S(1)} %pad_add_fusion.2.starts_ref, s32[1,1536]{1,0:T(1,128)S(1)} %compare_select_fusion.lo_ref, s32[1,1536]{1,0:T(1,128)S(1)} %add.260.hi_ref, bf16[192,1024]{1,0:T(8,128)(2,1)S(1)} %normalize.1.refs_0_.refs_8_, ...), custom_call_target="tpu_custom_call" | custom-call | flops 1811939328 | bytes 4325376 | tf_op jit(solution)/shard_map/match/pallas_call | solution.py:107
  44.9 2.1 %match.5.best_ref = f32[8,1536]{1,0:T(8,128)S(1)} custom-call(s32[2]{0:T(128)S(1)} %pad_add_fusion.1.starts_ref, s32[1,1536]{1,0:T(1,128)S(1)} %compare_select_fusion.lo_ref, s32[1,1536]{1,0:T(1,128)S(1)} %add.260.hi_ref, f32[8,1536]{1,0:T(8,128)S(1)} %get-tuple-element.7.best_ref, bf16[1536,1024]{1,0:T(8,128)(2,1)S(1)} %get-tuple-element.8.right_ref, ...), custom_call_target="tpu_custom_call" | custom-call | flops 1207959552 | bytes 3932160 | tf_op jit(solution)/shard_map/match/pallas_call | solution.py:107
  47.0 2.1 %match.6.best_ref = f32[8,1536]{1,0:T(8,128)S(1)} custom-call(s32[2]{0:T(128)S(1)} %pad_add_fusion.starts_ref, s32[1,1536]{1,0:T(1,128)S(1)} %compare_select_fusion.lo_ref, s32[1,1536]{1,0:T(1,128)S(1)} %add.260.hi_ref, f32[8,1536]{1,0:T(8,128)S(1)} %match.5.best_ref, bf16[1536,1024]{1,0:T(8,128)(2,1)S(1)} %get-tuple-element.8.right_ref, ...), custom_call_target="tpu_custom_call" | custom-call | flops 1207959552 | bytes 3932160 | tf_op jit(solution)/shard_map/match/pallas_call | solution.py:107
  49.2 1.2 %match.7 = f32[8,1536]{1,0:T(8,128)S(1)} custom-call(s32[1]{0:T(128)} %bitcast.starts_ref, s32[1,1536]{1,0:T(1,128)S(1)} %compare_select_fusion.lo_ref, s32[1,1536]{1,0:T(1,128)S(1)} %add.260.hi_ref, f32[8,1536]{1,0:T(8,128)S(1)} %match.6.best_ref, bf16[1536,1024]{1,0:T(8,128)(2,1)S(1)} %get-tuple-element.8.right_ref, ...), custom_call_target="tpu_custom_call" | custom-call | flops 603979776 | bytes 3538944 | tf_op jit(solution)/shard_map/match/pallas_call | solution.py:107
  50.7 1.0 %collective-permute-done.14 = f32[4,192]{1,0:T(4,128)S(1)} collective-permute-done((f32[4,192]{1,0:T(4,128)S(1)}, f32[4,192]{1,0:T(4,128)S(1)}, u32[]{:S(2)}, u32[]{:S(2)}) %collective-permute-start.14) | collective-permute-done | bytes 3104 | tf_op jit(solution)/shard_map/ppermute | solution.py:32
  51.7 0.9 %collective-permute-start.16 = (f32[192]{0:T(256)S(1)}, f32[192]{0:T(256)S(1)}, u32[]{:S(2)}, u32[]{:S(2)}) collective-permute-start(f32[192]{0:T(256)S(1)} %bitcast.19), channel_id=1, source_target_pairs={{0,16},{1,17},{2,18},{3,19},{4,20},{5,21},{6,22},{7,23},{8,24},{9,... | collective-permute-start | bytes 2312 | tf_op jit(solution)/shard_map/ppermute | solution.py:32
  52.7 2.2 %collective-permute-start.17 = (f32[192]{0:T(256)S(1)}, f32[192]{0:T(256)S(1)}, u32[]{:S(2)}, u32[]{:S(2)}) collective-permute-start(f32[192]{0:T(256)S(1)} %bitcast.18), channel_id=1, source_target_pairs={{0,32},{1,33},{2,34},{3,35},{4,36},{5,37},{6,38},{7,39},{8,40},{9,... | collective-permute-start | bytes 2312 | tf_op jit(solution)/shard_map/ppermute | solution.py:32
  55.4 1.2 %collective-permute-done.17 = f32[192]{0:T(256)S(1)} collective-permute-done((f32[192]{0:T(256)S(1)}, f32[192]{0:T(256)S(1)}, u32[]{:S(2)}, u32[]{:S(2)}) %collective-permute-start.17) | collective-permute-done | bytes 800 | tf_op jit(solution)/shard_map/ppermute | solution.py:32
  56.6 1.0 %collective-permute-done.15 = f32[192]{0:T(256)S(1)} collective-permute-done((f32[192]{0:T(256)S(1)}, f32[192]{0:T(256)S(1)}, u32[]{:S(2)}, u32[]{:S(2)}) %collective-permute-start.15) | collective-permute-done | bytes 800 | tf_op jit(solution)/shard_map/ppermute | solution.py:32
  (36 shorter events, 4.2 us)
Async XLA Ops:
  0.0 1.0 %copy-start = (bf16[192,1024]{1,0:T(8,128)(2,1)S(1)}, bf16[192,1024]{1,0:T(8,128)(2,1)}, u32[]{:S(2)}) copy-start(bf16[192,1024]{1,0:T(8,128)(2,1)} %rows_ref.1) | copy-start | bytes 1179652
  1.2 21.2 %collective-permute-start = (bf16[192,1024]{1,0:T(8,128)(2,1)S(1)}, bf16[192,1024]{1,0:T(8,128)(2,1)S(1)}, u32[]{:S(2)}, u32[]{:S(2)}) collective-permute-start(bf16[192,1024]{1,0:T(8,128)(2,1)S(1)} %normalize.1.refs_0_.refs_8_), channel_id=1, source_target_pairs={{0,16},{1,17},{2,18},{3,19},{4,20},{5,21},{6,22},{7,23},{8,24},{9,... | collective-permute-start | bytes 1179656 | tf_op jit(solution)/shard_map/ppermute | solution.py:32
  3.4 19.0 %collective-permute-start.1 = (bf16[192,1024]{1,0:T(8,128)(2,1)S(1)}, bf16[192,1024]{1,0:T(8,128)(2,1)S(1)}, u32[]{:S(2)}, u32[]{:S(2)}) collective-permute-start(bf16[192,1024]{1,0:T(8,128)(2,1)S(1)} %normalize.1.refs_0_.refs_8_), channel_id=1, source_target_pairs={{0,48},{1,49},{2,50},{3,51},{4,52},{5,53},{6,54},{7,55},{8,56},{9,... | collective-permute-start | bytes 1179656 | tf_op jit(solution)/shard_map/ppermute | solution.py:32
  4.9 18.0 %collective-permute-start.2 = (bf16[192,1024]{1,0:T(8,128)(2,1)S(1)}, bf16[192,1024]{1,0:T(8,128)(2,1)S(1)}, u32[]{:S(2)}, u32[]{:S(2)}) collective-permute-start(bf16[192,1024]{1,0:T(8,128)(2,1)S(1)} %normalize.1.refs_0_.refs_8_), channel_id=1, source_target_pairs={{0,32},{1,33},{2,34},{3,35},{4,36},{5,37},{6,38},{7,39},{8,40},{9,... | collective-permute-start | bytes 1179656 | tf_op jit(solution)/shard_map/ppermute | solution.py:32
  6.5 8.4 %collective-permute-start.3 = (bf16[192,1024]{1,0:T(8,128)(2,1)S(1)}, bf16[192,1024]{1,0:T(8,128)(2,1)S(1)}, u32[]{:S(2)}, u32[]{:S(2)}) collective-permute-start(bf16[192,1024]{1,0:T(8,128)(2,1)S(1)} %normalize.1.refs_0_.refs_8_), channel_id=1, source_target_pairs={{0,1},{1,0},{2,3},{3,2},{4,5},{5,4},{6,7},{7,6},{8,9},{9,8},{10,11... | collective-permute-start | bytes 1179656 | tf_op jit(solution)/shard_map/ppermute | solution.py:32
  8.0 10.3 %collective-permute-start.7 = (bf16[192,1024]{1,0:T(8,128)(2,1)S(1)}, bf16[192,1024]{1,0:T(8,128)(2,1)S(1)}, u32[]{:S(2)}, u32[]{:S(2)}) collective-permute-start(bf16[192,1024]{1,0:T(8,128)(2,1)S(1)} %normalize.1.refs_0_.refs_8_), channel_id=1, source_target_pairs={{0,2},{1,15},{2,4},{3,1},{4,6},{5,3},{6,8},{7,5},{8,10},{9,7},{10,... | collective-permute-start | bytes 1179656 | tf_op jit(solution)/shard_map/ppermute | solution.py:32
  14.9 9.6 %collective-permute-start.8 = (bf16[192,1024]{1,0:T(8,128)(2,1)S(1)}, bf16[192,1024]{1,0:T(8,128)(2,1)S(1)}, u32[]{:S(2)}, u32[]{:S(2)}) collective-permute-start(bf16[192,1024]{1,0:T(8,128)(2,1)S(1)} %collective-permute-done.3.refs_4_), channel_id=1, source_target_pairs={{0,2},{1,15},{2,4},{3,1},{4,6},{5,3},{6,8},{7,5},{8,10},{9,7},{10,... | collective-permute-start | bytes 1179656 | tf_op jit(solution)/shard_map/ppermute | solution.py:32
  18.3 11.8 %collective-permute-start.9 = (bf16[192,1024]{1,0:T(8,128)(2,1)S(1)}, bf16[192,1024]{1,0:T(8,128)(2,1)S(1)}, u32[]{:S(2)}, u32[]{:S(2)}) collective-permute-start(bf16[192,1024]{1,0:T(8,128)(2,1)S(1)} %collective-permute-done.7.refs_9_), channel_id=1, source_target_pairs={{0,2},{1,15},{2,4},{3,1},{4,6},{5,3},{6,8},{7,5},{8,10},{9,7},{10,... | collective-permute-start | bytes 1179656 | tf_op jit(solution)/shard_map/ppermute | solution.py:32
  22.4 19.7 %collective-permute-start.4 = (bf16[192,1024]{1,0:T(8,128)(2,1)S(1)}, bf16[192,1024]{1,0:T(8,128)(2,1)S(1)}, u32[]{:S(2)}, u32[]{:S(2)}) collective-permute-start(bf16[192,1024]{1,0:T(8,128)(2,1)S(1)} %collective-permute-done.refs_1_), channel_id=1, source_target_pairs={{0,1},{1,0},{2,3},{3,2},{4,5},{5,4},{6,7},{7,6},{8,9},{9,8},{10,11... | collective-permute-start | bytes 1179656 | tf_op jit(solution)/shard_map/ppermute | solution.py:32
  22.4 19.7 %collective-permute-start.5 = (bf16[192,1024]{1,0:T(8,128)(2,1)S(1)}, bf16[192,1024]{1,0:T(8,128)(2,1)S(1)}, u32[]{:S(2)}, u32[]{:S(2)}) collective-permute-start(bf16[192,1024]{1,0:T(8,128)(2,1)S(1)} %collective-permute-done.1.refs_2_), channel_id=1, source_target_pairs={{0,1},{1,0},{2,3},{3,2},{4,5},{5,4},{6,7},{7,6},{8,9},{9,8},{10,11... | collective-permute-start | bytes 1179656 | tf_op jit(solution)/shard_map/ppermute | solution.py:32
  22.9 19.2 %collective-permute-start.6 = (bf16[192,1024]{1,0:T(8,128)(2,1)S(1)}, bf16[192,1024]{1,0:T(8,128)(2,1)S(1)}, u32[]{:S(2)}, u32[]{:S(2)}) collective-permute-start(bf16[192,1024]{1,0:T(8,128)(2,1)S(1)} %collective-permute-done.2.refs_3_), channel_id=1, source_target_pairs={{0,1},{1,0},{2,3},{3,2},{4,5},{5,4},{6,7},{7,6},{8,9},{9,8},{10,11... | collective-permute-start | bytes 1179656 | tf_op jit(solution)/shard_map/ppermute | solution.py:32
  24.5 10.3 %collective-permute-start.10 = (bf16[192,1024]{1,0:T(8,128)(2,1)S(1)}, bf16[192,1024]{1,0:T(8,128)(2,1)S(1)}, u32[]{:S(2)}, u32[]{:S(2)}) collective-permute-start(bf16[192,1024]{1,0:T(8,128)(2,1)S(1)} %collective-permute-done.8.refs_10_), channel_id=1, source_target_pairs={{0,2},{1,15},{2,4},{3,1},{4,6},{5,3},{6,8},{7,5},{8,10},{9,7},{10,... | collective-permute-start | bytes 1179656 | tf_op jit(solution)/shard_map/ppermute | solution.py:32
  30.1 8.9 %collective-permute-start.11 = (bf16[192,1024]{1,0:T(8,128)(2,1)S(1)}, bf16[192,1024]{1,0:T(8,128)(2,1)S(1)}, u32[]{:S(2)}, u32[]{:S(2)}) collective-permute-start(bf16[192,1024]{1,0:T(8,128)(2,1)S(1)} %collective-permute-done.9.refs_0_), channel_id=1, source_target_pairs={{0,2},{1,15},{2,4},{3,1},{4,6},{5,3},{6,8},{7,5},{8,10},{9,7},{10,... | collective-permute-start | bytes 1179656 | tf_op jit(solution)/shard_map/ppermute | solution.py:32
  34.8 12.3 %collective-permute-start.12 = (bf16[192,1024]{1,0:T(8,128)(2,1)S(1)}, bf16[192,1024]{1,0:T(8,128)(2,1)S(1)}, u32[]{:S(2)}, u32[]{:S(2)}) collective-permute-start(bf16[192,1024]{1,0:T(8,128)(2,1)S(1)} %collective-permute-done.10.refs_1_), channel_id=1, source_target_pairs={{0,2},{1,15},{2,4},{3,1},{4,6},{5,3},{6,8},{7,5},{8,10},{9,7},{10,... | collective-permute-start | bytes 1179656 | tf_op jit(solution)/shard_map/ppermute | solution.py:32
  39.0 10.2 %collective-permute-start.13 = (bf16[192,1024]{1,0:T(8,128)(2,1)S(1)}, bf16[192,1024]{1,0:T(8,128)(2,1)S(1)}, u32[]{:S(2)}, u32[]{:S(2)}) collective-permute-start(bf16[192,1024]{1,0:T(8,128)(2,1)S(1)} %collective-permute-done.11.refs_0_), channel_id=1, source_target_pairs={{0,2},{1,15},{2,4},{3,1},{4,6},{5,3},{6,8},{7,5},{8,10},{9,7},{10,... | collective-permute-start | bytes 1179656 | tf_op jit(solution)/shard_map/ppermute | solution.py:32
  50.5 1.2 %collective-permute-start.14 = (f32[4,192]{1,0:T(4,128)S(1)}, f32[4,192]{1,0:T(4,128)S(1)}, u32[]{:S(2)}, u32[]{:S(2)}) collective-permute-start(f32[4,192]{1,0:T(4,128)S(1)} %squeeze.23), channel_id=1, source_target_pairs={{0,1},{1,0},{2,3},{3,2},{4,5},{5,4},{6,7},{7,6},{8,9},{9,8},{10,11... | collective-permute-start | bytes 9224 | tf_op jit(solution)/shard_map/ppermute | solution.py:32
  51.7 3.7 %collective-permute-start.16 = (f32[192]{0:T(256)S(1)}, f32[192]{0:T(256)S(1)}, u32[]{:S(2)}, u32[]{:S(2)}) collective-permute-start(f32[192]{0:T(256)S(1)} %bitcast.19), channel_id=1, source_target_pairs={{0,16},{1,17},{2,18},{3,19},{4,20},{5,21},{6,22},{7,23},{8,24},{9,... | collective-permute-start | bytes 2312 | tf_op jit(solution)/shard_map/ppermute | solution.py:32
  52.7 3.9 %collective-permute-start.17 = (f32[192]{0:T(256)S(1)}, f32[192]{0:T(256)S(1)}, u32[]{:S(2)}, u32[]{:S(2)}) collective-permute-start(f32[192]{0:T(256)S(1)} %bitcast.18), channel_id=1, source_target_pairs={{0,32},{1,33},{2,34},{3,35},{4,36},{5,37},{6,38},{7,39},{8,40},{9,... | collective-permute-start | bytes 2312 | tf_op jit(solution)/shard_map/ppermute | solution.py:32
  54.9 2.7 %collective-permute-start.15 = (f32[192]{0:T(256)S(1)}, f32[192]{0:T(256)S(1)}, u32[]{:S(2)}, u32[]{:S(2)}) collective-permute-start(f32[192]{0:T(256)S(1)} %bitcast.17), channel_id=1, source_target_pairs={{0,48},{1,49},{2,50},{3,51},{4,52},{5,53},{6,54},{7,55},{8,56},{9,... | collective-permute-start | bytes 2312 | tf_op jit(solution)/shard_map/ppermute | solution.py:32

commit v3 on v2

--- a/solution.py
+++ b/solution.py
@@ -33,7 +33,7 @@
 
 
 def along_y(value, dy):
-    return permute(value, lambda y, z, core: (y + dy, z, core))
+    return permute(value, lambda y, z, core: (y + (dy, -dy)[core], z, core))
 
 
 def along_z(value):
@@ -79,37 +79,50 @@
         out_ref[:, lanes] = best
 
 
-def stack(piece_refs, left):
-    if len(piece_refs) == 1:
-        return piece_refs[0]
-    for i, piece_ref in enumerate(piece_refs):
-        left[i * ROWS : (i + 1) * ROWS, :] = piece_ref[...]
+def gather(piece_refs, left):
+    first = 0
+    for piece_ref in piece_refs:
+        last = first + piece_ref.shape[0]
+        left[first:last, :] = piece_ref[...]
+        first = last
     return left
 
 
 def first_kernel(starts_ref, lo_ref, hi_ref, *refs):
     segments, pieces = refs[:SEGMENTS], refs[SEGMENTS:-3]
     right_ref, out_ref, left = refs[-3:]
-    for i, segment in enumerate(segments):
-        right_ref[i * ROWS : (i + 1) * ROWS, :] = segment[...]
-    fold(starts_ref, lo_ref, hi_ref, None, right_ref, stack(pieces, left), out_ref)
+    gather(segments, right_ref)
+    fold(starts_ref, lo_ref, hi_ref, None, right_ref, gather(pieces, left), out_ref)
 
 
 def match_kernel(starts_ref, lo_ref, hi_ref, best_ref, right_ref, *refs):
     pieces, (out_ref, left) = refs[:-2], refs[-2:]
-    fold(starts_ref, lo_ref, hi_ref, best_ref, right_ref, stack(pieces, left), out_ref)
+    fold(starts_ref, lo_ref, hi_ref, best_ref, right_ref, gather(pieces, left), out_ref)
+
+
+def last_kernel(starts_ref, lo_ref, hi_ref, best_ref, right_ref, piece_ref, mine_ref, theirs_ref, best):
+    fold(starts_ref, lo_ref, hi_ref, best_ref, right_ref, piece_ref, best)
+    half = WIDE // CORES
+    mine_ref[...] = jnp.max(best[:, :half], axis=0, keepdims=True)
+    theirs_ref[...] = jnp.max(best[:, half:], axis=0, keepdims=True)
 
 
 def match(kernel, starts, lo, hi, others, pieces):
     rows = ROWS * len(pieces)
     best = jax.ShapeDtypeStruct((8, WIDE), jnp.float32)
-    first = kernel is first_kernel
+    out = best
+    scratch = pltpu.VMEM((rows, D), jnp.bfloat16)
+    if kernel is first_kernel:
+        out = (jax.ShapeDtypeStruct((WIDE, D), jnp.bfloat16), best)
+    if kernel is last_kernel:
+        out = (jax.ShapeDtypeStruct((1, WIDE // CORES), jnp.float32),) * CORES
+        scratch = pltpu.VMEM((8, WIDE), jnp.float32)
     return pl.pallas_call(
         kernel,
-        out_shape=(jax.ShapeDtypeStruct((WIDE, D), jnp.bfloat16), best) if first else best,
+        out_shape=out,
         in_specs=[SMEM] + [VMEM] * (2 + len(others) + len(pieces)),
-        out_specs=(VMEM, VMEM) if first else VMEM,
-        scratch_shapes=[pltpu.VMEM((rows, D), jnp.bfloat16)],
+        out_specs=jax.tree.map(lambda _: VMEM, out),
+        scratch_shapes=[scratch],
         cost_estimate=pl.CostEstimate(
             flops=2 * rows * WIDE * D, bytes_accessed=2 * D * (rows + WIDE), transcendentals=0
         ),
@@ -131,20 +144,29 @@
     def start(dy, dz, dcore):
         return device(y + dy, z + dz, core + dcore) * ROWS
 
-    segment = jnp.arange(SEGMENTS, dtype=jnp.int32)[:, None]
-    segment_dy = jnp.array([0, 3, 1, 2], jnp.int32)[segment % Y]
-    row_index = start(segment_dy, 0, segment // Y) + jnp.arange(ROWS, dtype=jnp.int32)[None]
-    row_index = row_index.reshape(1, WIDE)
+    row_index = jnp.concatenate(
+        [
+            start(toward * dy, 0, dcore) + jnp.arange(ROWS, dtype=jnp.int32)
+            for dy, dcore in ((0, 0), (1, 0), (-1, 0), (2, 0), (0, 1), (-1, 1), (1, 1), (2, 1))
+        ]
+    )[None]
     lo = jnp.where(row_index >= split, split, 0)
 
-    own, other = [unit], [swap(unit)]
+    def after(value, *earlier):
+        return lax.optimization_barrier((value,) + earlier)[0]
+
+    partner = swap(unit)
+    own, other = [unit], [partner]
     for _ in range(3):
         own.append(along_z(own[-1]))
         other.append(along_z(other[-1]))
     own.append(along_z(own[-1]))
 
-    mine = [unit] + [along_y(unit, dy) for dy in (1, -1, 2)]
-    theirs = [other[0]] + [swap(segment) for segment in mine[1:]]
+    near = along_y(after(unit, partner), 1)
+    near_other = along_y(after(partner, near), 1)
+    far = along_y(near, 1)
+    mine = [unit, near, swap(near_other), far]
+    theirs = [partner, swap(near), near_other, swap(far)]
 
     def starts(pieces):
         return [start(0, toward * k, dcore) for k, dcore in pieces]
@@ -161,10 +183,9 @@
         best = match(
             match_kernel, starts([(k, 0), (k, 1)]), lo, row_index, [best, right], [own[k], other[k]]
         )
-    best = match(match_kernel, starts([(4, 0)]), lo, row_index, [best, right], [own[4]])
-
-    best = jnp.max(best, axis=0).reshape(CORES, Y, ROWS)
-    best = jnp.maximum(best[0], swap(best[1]))
+    mine, other = match(last_kernel, starts([(4, 0)]), lo, row_index, [best, right], [own[4]])
+
+    best = jnp.maximum(mine, swap(other)).reshape(Y, ROWS)
     best = jnp.maximum(
         jnp.maximum(best[0], along_y(best[1], -1)),
         jnp.maximum(along_y(best[2], 1), along_y(best[3], 2)),

time: 58.5 us -> 52.8 us (0.903)
  waiting for transfers between devices: 11 us -> 8.65 us
  starting transfers between devices: 34.5 us -> 32.8 us
  local copies, waits for them, and re-layouts: 2.54 us -> 1.26 us
    ppermute x18, waiting for transfers between devices: 11 us -> 8.65 us  [permute(): return lax.ppermute(value, 'member', pairs)]
    ppermute x18, starting transfers between devices: 34.5 us -> 32.8 us  [permute(): return lax.ppermute(value, 'member', pairs)]
    gather x1 -> x0, local copies, waits for them, and re-layouts: 1.3 us -> none  [shards(): segment_dy = jnp.array([0, 3, 1, 2], jnp.int32)[segment % Y]]
  transfers between devices with their start and end apart: 18 -> 18, of which waited for: 7 -> 7; matrix products, arithmetic and copies ran while one was open for 3% -> 1% of each run, Pallas kernels for 12% -> 13%
where the time goes in v3:
time: 52.8 us; the launch traced here: 52.7 us
  starting transfers between devices  32.8 us (62%)
  waiting for transfers between devices  8.65 us (16%)
  Pallas kernels  8.4 us (16%)
  local copies, waits for them, and re-layouts  1.26 us (2%)
  other arithmetic  0.82 us (2%)
  between operations  0.77 us (1%)
    ppermute x18, starting transfers between devices, permute(): return lax.ppermute(value, 'member', pairs)  32.8 us
    ppermute x18, waiting for transfers between devices, permute(): return lax.ppermute(value, 'member', pairs)  8.65 us
    pallas_call x4, Pallas kernels, match(): pl.pallas_call(kernel, out_shape=out, in_specs=[SMEM] + [VMEM] * (2 + len...  8.24 us
  transfers between devices with their start and end apart: 18, of which 7 were waited for; matrix products, arithmetic and copies ran while one was open for 1% of the time, Pallas kernels for 13%

profile of v3, /device:TPU:1, one launch (start us, length us, event | category | flops | bytes accessed | tf_op | source)
XLA Modules:
  0.0 52.7 jit_solution(9255758846469144768)
XLA Ops:
  0.0 1.0 %copy-done = bf16[192,1024]{1,0:T(8,128)(2,1)S(1)} copy-done((bf16[192,1024]{1,0:T(8,128)(2,1)S(1)}, bf16[192,1024]{1,0:T(8,128)(2,1)}, u32[]{:S(2)}) %copy-start) | copy-done | bytes 393240
  1.2 3.3 %collective-permute-start = (bf16[192,1024]{1,0:T(8,128)(2,1)S(1)}, bf16[192,1024]{1,0:T(8,128)(2,1)S(1)}, u32[]{:S(2)}, u32[]{:S(2)}) collective-permute-start(bf16[192,1024]{1,0:T(8,128)(2,1)S(1)} %normalize.1.refs_0_.refs_8_), channel_id=1, source_target_pairs={{0,1},{1,0},{2,3},{3,2},{4,5},{5,4},{6,7},{7,6},{8,9},{9,8},{10,11... | collective-permute-start | bytes 1179656 | tf_op jit(solution)/shard_map/ppermute | solution.py:32
  4.5 3.8 %collective-permute-start.7 = (bf16[192,1024]{1,0:T(8,128)(2,1)S(1)}, bf16[192,1024]{1,0:T(8,128)(2,1)S(1)}, u32[]{:S(2)}, u32[]{:S(2)}) collective-permute-start(bf16[192,1024]{1,0:T(8,128)(2,1)S(1)} %normalize.1.refs_0_.refs_8_), channel_id=1, source_target_pairs={{0,2},{1,15},{2,4},{3,1},{4,6},{5,3},{6,8},{7,5},{8,10},{9,7},{10,... | collective-permute-start | bytes 1179656 | tf_op jit(solution)/shard_map/ppermute | solution.py:32
  8.3 2.7 %collective-permute-start.1 = (bf16[192,1024]{1,0:T(8,128)(2,1)S(1)}, bf16[192,1024]{1,0:T(8,128)(2,1)S(1)}, u32[]{:S(2)}, u32[]{:S(2)}) collective-permute-start(bf16[192,1024]{1,0:T(8,128)(2,1)S(1)} %normalize.1.refs_0_.refs_8_), channel_id=1, source_target_pairs={{0,16},{1,49},{2,18},{3,51},{4,20},{5,53},{6,22},{7,55},{8,24},{9,... | collective-permute-start | bytes 1179656 | tf_op jit(solution)/shard_map/ppermute | solution.py:32
  11.1 1.3 %collective-permute-start.8 = (bf16[192,1024]{1,0:T(8,128)(2,1)S(1)}, bf16[192,1024]{1,0:T(8,128)(2,1)S(1)}, u32[]{:S(2)}, u32[]{:S(2)}) collective-permute-start(bf16[192,1024]{1,0:T(8,128)(2,1)S(1)} %collective-permute-done.refs_4_), channel_id=1, source_target_pairs={{0,2},{1,15},{2,4},{3,1},{4,6},{5,3},{6,8},{7,5},{8,10},{9,7},{10,... | collective-permute-start | bytes 1179656 | tf_op jit(solution)/shard_map/ppermute | solution.py:32
  12.4 0.6 %collective-permute-done.7.refs_9_ = bf16[192,1024]{1,0:T(8,128)(2,1)S(1)} collective-permute-done((bf16[192,1024]{1,0:T(8,128)(2,1)S(1)}, bf16[192,1024]{1,0:T(8,128)(2,1)S(1)}, u32[]{:S(2)}, u32[]{:S(2)}) %collective-permute-start.7) | collective-permute-done | bytes 393248 | tf_op jit(solution)/shard_map/ppermute | solution.py:32
  13.1 3.4 %collective-permute-start.9 = (bf16[192,1024]{1,0:T(8,128)(2,1)S(1)}, bf16[192,1024]{1,0:T(8,128)(2,1)S(1)}, u32[]{:S(2)}, u32[]{:S(2)}) collective-permute-start(bf16[192,1024]{1,0:T(8,128)(2,1)S(1)} %collective-permute-done.7.refs_9_), channel_id=1, source_target_pairs={{0,2},{1,15},{2,4},{3,1},{4,6},{5,3},{6,8},{7,5},{8,10},{9,7},{10,... | collective-permute-start | bytes 1179656 | tf_op jit(solution)/shard_map/ppermute | solution.py:32
  16.5 2.7 %collective-permute-start.2 = (bf16[192,1024]{1,0:T(8,128)(2,1)S(1)}, bf16[192,1024]{1,0:T(8,128)(2,1)S(1)}, u32[]{:S(2)}, u32[]{:S(2)}) collective-permute-start(bf16[192,1024]{1,0:T(8,128)(2,1)S(1)} %collective-permute-done.refs_4_), channel_id=1, source_target_pairs={{0,16},{1,49},{2,18},{3,51},{4,20},{5,53},{6,22},{7,55},{8,24},{9,... | collective-permute-start | bytes 1179656 | tf_op jit(solution)/shard_map/ppermute | solution.py:32
  20.4 1.6 %collective-permute-start.10 = (bf16[192,1024]{1,0:T(8,128)(2,1)S(1)}, bf16[192,1024]{1,0:T(8,128)(2,1)S(1)}, u32[]{:S(2)}, u32[]{:S(2)}) collective-permute-start(bf16[192,1024]{1,0:T(8,128)(2,1)S(1)} %collective-permute-done.8.refs_10_), channel_id=1, source_target_pairs={{0,2},{1,15},{2,4},{3,1},{4,6},{5,3},{6,8},{7,5},{8,10},{9,7},{10,... | collective-permute-start | bytes 1179656 | tf_op jit(solution)/shard_map/ppermute | solution.py:32
  22.2 2.7 %collective-permute-start.11 = (bf16[192,1024]{1,0:T(8,128)(2,1)S(1)}, bf16[192,1024]{1,0:T(8,128)(2,1)S(1)}, u32[]{:S(2)}, u32[]{:S(2)}) collective-permute-start(bf16[192,1024]{1,0:T(8,128)(2,1)S(1)} %collective-permute-done.9.refs_0_), channel_id=1, source_target_pairs={{0,2},{1,15},{2,4},{3,1},{4,6},{5,3},{6,8},{7,5},{8,10},{9,7},{10,... | collective-permute-start | bytes 1179656 | tf_op jit(solution)/shard_map/ppermute | solution.py:32
  24.9 3.2 %collective-permute-done.4.refs_3_ = bf16[192,1024]{1,0:T(8,128)(2,1)S(1)} collective-permute-done((bf16[192,1024]{1,0:T(8,128)(2,1)S(1)}, bf16[192,1024]{1,0:T(8,128)(2,1)S(1)}, u32[]{:S(2)}, u32[]{:S(2)}) %collective-permute-start.4) | collective-permute-done | bytes 393248 | tf_op jit(solution)/shard_map/ppermute | solution.py:32
  28.4 3.9 %collective-permute-start.12 = (bf16[192,1024]{1,0:T(8,128)(2,1)S(1)}, bf16[192,1024]{1,0:T(8,128)(2,1)S(1)}, u32[]{:S(2)}, u32[]{:S(2)}) collective-permute-start(bf16[192,1024]{1,0:T(8,128)(2,1)S(1)} %collective-permute-done.10.refs_1_), channel_id=1, source_target_pairs={{0,2},{1,15},{2,4},{3,1},{4,6},{5,3},{6,8},{7,5},{8,10},{9,7},{10,... | collective-permute-start | bytes 1179656 | tf_op jit(solution)/shard_map/ppermute | solution.py:32
  32.4 1.7 %collective-permute-start.13 = (bf16[192,1024]{1,0:T(8,128)(2,1)S(1)}, bf16[192,1024]{1,0:T(8,128)(2,1)S(1)}, u32[]{:S(2)}, u32[]{:S(2)}) collective-permute-start(bf16[192,1024]{1,0:T(8,128)(2,1)S(1)} %collective-permute-done.11.refs_0_), channel_id=1, source_target_pairs={{0,2},{1,15},{2,4},{3,1},{4,6},{5,3},{6,8},{7,5},{8,10},{9,7},{10,... | collective-permute-start | bytes 1179656 | tf_op jit(solution)/shard_map/ppermute | solution.py:32
  34.1 2.8 %match.4 = (bf16[1536,1024]{1,0:T(8,128)(2,1)S(1)}, f32[8,1536]{1,0:T(8,128)S(1)}) custom-call(s32[3]{0:T(128)S(1)} %pad_add_fusion.2.starts_ref, s32[1,1536]{1,0:T(1,128)S(1)} %compare_select_fusion.lo_ref, s32[1,1536]{1,0:T(1,128)S(1)} %broadcast_in_dim.10.hi_ref, bf16[192,1024]{1,0:T(8,128)(2,1)S(1)} %normalize.1.refs_0_.refs_8_, ...), custom_call_target="tpu_custom_call" | custom-call | flops 1811939328 | bytes 4325376 | tf_op jit(solution)/shard_map/match/pallas_call | solution.py:120
  36.9 2.1 %match.5.best_ref = f32[8,1536]{1,0:T(8,128)S(1)} custom-call(s32[2]{0:T(128)S(1)} %pad_add_fusion.1.starts_ref, s32[1,1536]{1,0:T(1,128)S(1)} %compare_select_fusion.lo_ref, s32[1,1536]{1,0:T(1,128)S(1)} %broadcast_in_dim.10.hi_ref, f32[8,1536]{1,0:T(8,128)S(1)} %get-tuple-element.13.best_ref, bf16[1536,1024]{1,0:T(8,128)(2,1)S(1)} %get-tuple-element.14.right_ref, ...), custom_call_target="tpu_custom_call" | custom-call | flops 1207959552 | bytes 3932160 | tf_op jit(solution)/shard_map/match/pallas_call | solution.py:120
  39.0 2.1 %match.6.best_ref = f32[8,1536]{1,0:T(8,128)S(1)} custom-call(s32[2]{0:T(128)S(1)} %pad_add_fusion.starts_ref, s32[1,1536]{1,0:T(1,128)S(1)} %compare_select_fusion.lo_ref, s32[1,1536]{1,0:T(1,128)S(1)} %broadcast_in_dim.10.hi_ref, f32[8,1536]{1,0:T(8,128)S(1)} %match.5.best_ref, bf16[1536,1024]{1,0:T(8,128)(2,1)S(1)} %get-tuple-element.14.right_ref, ...), custom_call_target="tpu_custom_call" | custom-call | flops 1207959552 | bytes 3932160 | tf_op jit(solution)/shard_map/match/pallas_call | solution.py:120
  41.3 1.2 %match.7 = (f32[1,768]{1,0:T(1,128)S(1)}, f32[1,768]{1,0:T(1,128)S(1)}) custom-call(s32[1]{0:T(128)} %bitcast.starts_ref, s32[1,1536]{1,0:T(1,128)S(1)} %compare_select_fusion.lo_ref, s32[1,1536]{1,0:T(1,128)S(1)} %broadcast_in_dim.10.hi_ref, f32[8,1536]{1,0:T(8,128)S(1)} %match.6.best_ref, bf16[1536,1024]{1,0:T(8,128)(2,1)S(1)} %get-tuple-element.14.right_ref, ...), custom_call_target="tpu_custom_call" | custom-call | flops 603979776 | bytes 3538944 | tf_op jit(solution)/shard_map/match/pallas_call | solution.py:120
  42.5 1.9 %collective-permute-start.14 = (f32[1,768]{1,0:T(1,128)S(1)}, f32[1,768]{1,0:T(1,128)S(1)}, u32[]{:S(2)}, u32[]{:S(2)}) collective-permute-start(f32[1,768]{1,0:T(1,128)S(1)} %get-tuple-element.16), channel_id=1, source_target_pairs={{0,1},{1,0},{2,3},{3,2},{4,5},{5,4},{6,7},{7,6},{8,9},{9,8},{10,11... | collective-permute-start | bytes 9224 | tf_op jit(solution)/shard_map/ppermute | solution.py:32
  44.5 0.8 %collective-permute-done.14 = f32[1,768]{1,0:T(1,128)S(1)} collective-permute-done((f32[1,768]{1,0:T(1,128)S(1)}, f32[1,768]{1,0:T(1,128)S(1)}, u32[]{:S(2)}, u32[]{:S(2)}) %collective-permute-start.14) | collective-permute-done | bytes 3104 | tf_op jit(solution)/shard_map/ppermute | solution.py:32
  45.4 2.2 %collective-permute-start.16 = (f32[192]{0:T(256)S(1)}, f32[192]{0:T(256)S(1)}, u32[]{:S(2)}, u32[]{:S(2)}) collective-permute-start(f32[192]{0:T(256)S(1)} %bitcast.33), channel_id=1, source_target_pairs={{0,16},{1,49},{2,18},{3,51},{4,20},{5,53},{6,22},{7,55},{8,24},{9,... | collective-permute-start | bytes 2312 | tf_op jit(solution)/shard_map/ppermute | solution.py:32
  47.6 0.9 %collective-permute-start.17 = (f32[192]{0:T(256)S(1)}, f32[192]{0:T(256)S(1)}, u32[]{:S(2)}, u32[]{:S(2)}) collective-permute-start(f32[192]{0:T(256)S(1)} %bitcast.32), channel_id=1, source_target_pairs={{0,32},{1,33},{2,34},{3,35},{4,36},{5,37},{6,38},{7,39},{8,40},{9,... | collective-permute-start | bytes 2312 | tf_op jit(solution)/shard_map/ppermute | solution.py:32
  48.5 3.1 %collective-permute-done.17 = f32[192]{0:T(256)S(1)} collective-permute-done((f32[192]{0:T(256)S(1)}, f32[192]{0:T(256)S(1)}, u32[]{:S(2)}, u32[]{:S(2)}) %collective-permute-start.17) | collective-permute-done | bytes 800 | tf_op jit(solution)/shard_map/ppermute | solution.py:32
  51.5 0.6 %collective-permute-done.15 = f32[192]{0:T(256)S(1)} collective-permute-done((f32[192]{0:T(256)S(1)}, f32[192]{0:T(256)S(1)}, u32[]{:S(2)}, u32[]{:S(2)}) %collective-permute-start.15) | collective-permute-done | bytes 800 | tf_op jit(solution)/shard_map/ppermute | solution.py:32
  52.1 0.6 %maximum_maximum_fusion = f32[192]{0:T(256)} fusion(f32[192]{0:T(256)S(1)} %collective-permute-done.16, f32[192]{0:T(256)S(1)} %collective-permute-done.17, f32[192]{0:T(256)S(1)} %bitcast.30, f32[192]{0:T(256)S(1)} %collective-permute-done.15), kind=kLoop, calls=%fused_computation.1 | loop fusion | flops 768 | bytes 3840 | tf_op jit(solution)/shard_map/max | solution.py:193
  (33 shorter events, 1.5 us)
Async XLA Ops:
  0.0 1.0 %copy-start = (bf16[192,1024]{1,0:T(8,128)(2,1)S(1)}, bf16[192,1024]{1,0:T(8,128)(2,1)}, u32[]{:S(2)}) copy-start(bf16[192,1024]{1,0:T(8,128)(2,1)} %rows_ref.1) | copy-start | bytes 1179652
  1.2 7.2 %collective-permute-start = (bf16[192,1024]{1,0:T(8,128)(2,1)S(1)}, bf16[192,1024]{1,0:T(8,128)(2,1)S(1)}, u32[]{:S(2)}, u32[]{:S(2)}) collective-permute-start(bf16[192,1024]{1,0:T(8,128)(2,1)S(1)} %normalize.1.refs_0_.refs_8_), channel_id=1, source_target_pairs={{0,1},{1,0},{2,3},{3,2},{4,5},{5,4},{6,7},{7,6},{8,9},{9,8},{10,11... | collective-permute-start | bytes 1179656 | tf_op jit(solution)/shard_map/ppermute | solution.py:32
  4.5 8.6 %collective-permute-start.7 = (bf16[192,1024]{1,0:T(8,128)(2,1)S(1)}, bf16[192,1024]{1,0:T(8,128)(2,1)S(1)}, u32[]{:S(2)}, u32[]{:S(2)}) collective-permute-start(bf16[192,1024]{1,0:T(8,128)(2,1)S(1)} %normalize.1.refs_0_.refs_8_), channel_id=1, source_target_pairs={{0,2},{1,15},{2,4},{3,1},{4,6},{5,3},{6,8},{7,5},{8,10},{9,7},{10,... | collective-permute-start | bytes 1179656 | tf_op jit(solution)/shard_map/ppermute | solution.py:32
  8.3 8.1 %collective-permute-start.1 = (bf16[192,1024]{1,0:T(8,128)(2,1)S(1)}, bf16[192,1024]{1,0:T(8,128)(2,1)S(1)}, u32[]{:S(2)}, u32[]{:S(2)}) collective-permute-start(bf16[192,1024]{1,0:T(8,128)(2,1)S(1)} %normalize.1.refs_0_.refs_8_), channel_id=1, source_target_pairs={{0,16},{1,49},{2,18},{3,51},{4,20},{5,53},{6,22},{7,55},{8,24},{9,... | collective-permute-start | bytes 1179656 | tf_op jit(solution)/shard_map/ppermute | solution.py:32
  11.1 9.4 %collective-permute-start.8 = (bf16[192,1024]{1,0:T(8,128)(2,1)S(1)}, bf16[192,1024]{1,0:T(8,128)(2,1)S(1)}, u32[]{:S(2)}, u32[]{:S(2)}) collective-permute-start(bf16[192,1024]{1,0:T(8,128)(2,1)S(1)} %collective-permute-done.refs_4_), channel_id=1, source_target_pairs={{0,2},{1,15},{2,4},{3,1},{4,6},{5,3},{6,8},{7,5},{8,10},{9,7},{10,... | collective-permute-start | bytes 1179656 | tf_op jit(solution)/shard_map/ppermute | solution.py:32
  13.1 9.2 %collective-permute-start.9 = (bf16[192,1024]{1,0:T(8,128)(2,1)S(1)}, bf16[192,1024]{1,0:T(8,128)(2,1)S(1)}, u32[]{:S(2)}, u32[]{:S(2)}) collective-permute-start(bf16[192,1024]{1,0:T(8,128)(2,1)S(1)} %collective-permute-done.7.refs_9_), channel_id=1, source_target_pairs={{0,2},{1,15},{2,4},{3,1},{4,6},{5,3},{6,8},{7,5},{8,10},{9,7},{10,... | collective-permute-start | bytes 1179656 | tf_op jit(solution)/shard_map/ppermute | solution.py:32
  16.5 8.4 %collective-permute-start.2 = (bf16[192,1024]{1,0:T(8,128)(2,1)S(1)}, bf16[192,1024]{1,0:T(8,128)(2,1)S(1)}, u32[]{:S(2)}, u32[]{:S(2)}) collective-permute-start(bf16[192,1024]{1,0:T(8,128)(2,1)S(1)} %collective-permute-done.refs_4_), channel_id=1, source_target_pairs={{0,16},{1,49},{2,18},{3,51},{4,20},{5,53},{6,22},{7,55},{8,24},{9,... | collective-permute-start | bytes 1179656 | tf_op jit(solution)/shard_map/ppermute | solution.py:32
  19.2 8.9 %collective-permute-start.4 = (bf16[192,1024]{1,0:T(8,128)(2,1)S(1)}, bf16[192,1024]{1,0:T(8,128)(2,1)S(1)}, u32[]{:S(2)}, u32[]{:S(2)}) collective-permute-start(bf16[192,1024]{1,0:T(8,128)(2,1)S(1)} %collective-permute-done.1.refs_1_), channel_id=1, source_target_pairs={{0,16},{1,49},{2,18},{3,51},{4,20},{5,53},{6,22},{7,55},{8,24},{9,... | collective-permute-start | bytes 1179656 | tf_op jit(solution)/shard_map/ppermute | solution.py:32
  20.4 13.7 %collective-permute-start.5 = (bf16[192,1024]{1,0:T(8,128)(2,1)S(1)}, bf16[192,1024]{1,0:T(8,128)(2,1)S(1)}, u32[]{:S(2)}, u32[]{:S(2)}) collective-permute-start(bf16[192,1024]{1,0:T(8,128)(2,1)S(1)} %collective-permute-done.1.refs_1_), channel_id=1, source_target_pairs={{0,1},{1,0},{2,3},{3,2},{4,5},{5,4},{6,7},{7,6},{8,9},{9,8},{10,11... | collective-permute-start | bytes 1179656 | tf_op jit(solution)/shard_map/ppermute | solution.py:32
  20.4 8.0 %collective-permute-start.10 = (bf16[192,1024]{1,0:T(8,128)(2,1)S(1)}, bf16[192,1024]{1,0:T(8,128)(2,1)S(1)}, u32[]{:S(2)}, u32[]{:S(2)}) collective-permute-start(bf16[192,1024]{1,0:T(8,128)(2,1)S(1)} %collective-permute-done.8.refs_10_), channel_id=1, source_target_pairs={{0,2},{1,15},{2,4},{3,1},{4,6},{5,3},{6,8},{7,5},{8,10},{9,7},{10,... | collective-permute-start | bytes 1179656 | tf_op jit(solution)/shard_map/ppermute | solution.py:32
  22.2 10.2 %collective-permute-start.11 = (bf16[192,1024]{1,0:T(8,128)(2,1)S(1)}, bf16[192,1024]{1,0:T(8,128)(2,1)S(1)}, u32[]{:S(2)}, u32[]{:S(2)}) collective-permute-start(bf16[192,1024]{1,0:T(8,128)(2,1)S(1)} %collective-permute-done.9.refs_0_), channel_id=1, source_target_pairs={{0,2},{1,15},{2,4},{3,1},{4,6},{5,3},{6,8},{7,5},{8,10},{9,7},{10,... | collective-permute-start | bytes 1179656 | tf_op jit(solution)/shard_map/ppermute | solution.py:32
  24.9 9.2 %collective-permute-start.3 = (bf16[192,1024]{1,0:T(8,128)(2,1)S(1)}, bf16[192,1024]{1,0:T(8,128)(2,1)S(1)}, u32[]{:S(2)}, u32[]{:S(2)}) collective-permute-start(bf16[192,1024]{1,0:T(8,128)(2,1)S(1)} %collective-permute-done.2.refs_6_), channel_id=1, source_target_pairs={{0,1},{1,0},{2,3},{3,2},{4,5},{5,4},{6,7},{7,6},{8,9},{9,8},{10,11... | collective-permute-start | bytes 1179656 | tf_op jit(solution)/shard_map/ppermute | solution.py:32
  28.1 6.0 %collective-permute-start.6 = (bf16[192,1024]{1,0:T(8,128)(2,1)S(1)}, bf16[192,1024]{1,0:T(8,128)(2,1)S(1)}, u32[]{:S(2)}, u32[]{:S(2)}) collective-permute-start(bf16[192,1024]{1,0:T(8,128)(2,1)S(1)} %collective-permute-done.4.refs_3_), channel_id=1, source_target_pairs={{0,1},{1,0},{2,3},{3,2},{4,5},{5,4},{6,7},{7,6},{8,9},{9,8},{10,11... | collective-permute-start | bytes 1179656 | tf_op jit(solution)/shard_map/ppermute | solution.py:32
  28.4 10.6 %collective-permute-start.12 = (bf16[192,1024]{1,0:T(8,128)(2,1)S(1)}, bf16[192,1024]{1,0:T(8,128)(2,1)S(1)}, u32[]{:S(2)}, u32[]{:S(2)}) collective-permute-start(bf16[192,1024]{1,0:T(8,128)(2,1)S(1)} %collective-permute-done.10.refs_1_), channel_id=1, source_target_pairs={{0,2},{1,15},{2,4},{3,1},{4,6},{5,3},{6,8},{7,5},{8,10},{9,7},{10,... | collective-permute-start | bytes 1179656 | tf_op jit(solution)/shard_map/ppermute | solution.py:32
  32.4 8.9 %collective-permute-start.13 = (bf16[192,1024]{1,0:T(8,128)(2,1)S(1)}, bf16[192,1024]{1,0:T(8,128)(2,1)S(1)}, u32[]{:S(2)}, u32[]{:S(2)}) collective-permute-start(bf16[192,1024]{1,0:T(8,128)(2,1)S(1)} %collective-permute-done.11.refs_0_), channel_id=1, source_target_pairs={{0,2},{1,15},{2,4},{3,1},{4,6},{5,3},{6,8},{7,5},{8,10},{9,7},{10,... | collective-permute-start | bytes 1179656 | tf_op jit(solution)/shard_map/ppermute | solution.py:32
  42.5 2.8 %collective-permute-start.14 = (f32[1,768]{1,0:T(1,128)S(1)}, f32[1,768]{1,0:T(1,128)S(1)}, u32[]{:S(2)}, u32[]{:S(2)}) collective-permute-start(f32[1,768]{1,0:T(1,128)S(1)} %get-tuple-element.16), channel_id=1, source_target_pairs={{0,1},{1,0},{2,3},{3,2},{4,5},{5,4},{6,7},{7,6},{8,9},{9,8},{10,11... | collective-permute-start | bytes 9224 | tf_op jit(solution)/shard_map/ppermute | solution.py:32
  45.4 3.1 %collective-permute-start.16 = (f32[192]{0:T(256)S(1)}, f32[192]{0:T(256)S(1)}, u32[]{:S(2)}, u32[]{:S(2)}) collective-permute-start(f32[192]{0:T(256)S(1)} %bitcast.33), channel_id=1, source_target_pairs={{0,16},{1,49},{2,18},{3,51},{4,20},{5,53},{6,22},{7,55},{8,24},{9,... | collective-permute-start | bytes 2312 | tf_op jit(solution)/shard_map/ppermute | solution.py:32
  47.6 3.9 %collective-permute-start.17 = (f32[192]{0:T(256)S(1)}, f32[192]{0:T(256)S(1)}, u32[]{:S(2)}, u32[]{:S(2)}) collective-permute-start(f32[192]{0:T(256)S(1)} %bitcast.32), channel_id=1, source_target_pairs={{0,32},{1,33},{2,34},{3,35},{4,36},{5,37},{6,38},{7,39},{8,40},{9,... | collective-permute-start | bytes 2312 | tf_op jit(solution)/shard_map/ppermute | solution.py:32
  48.5 3.6 %collective-permute-start.15 = (f32[192]{0:T(256)S(1)}, f32[192]{0:T(256)S(1)}, u32[]{:S(2)}, u32[]{:S(2)}) collective-permute-start(f32[192]{0:T(256)S(1)} %bitcast.31), channel_id=1, source_target_pairs={{0,48},{1,17},{2,50},{3,19},{4,52},{5,21},{6,54},{7,23},{8,56},{9,... | collective-permute-start | bytes 2312 | tf_op jit(solution)/shard_map/ppermute | solution.py:32

commit v4 on v0

v4 whole, which is shorter than its diff:
```python
import functools

import jax
import jax.numpy as jnp
from jax import lax
from jax.experimental import pallas as pl
from jax.experimental.pallas import tpu as pltpu
from jax.sharding import PartitionSpec as P

Y, Z, CORES = 4, 8, 2
ROWS = 192
SEGMENTS = Y * CORES
WIDE = SEGMENTS * ROWS
HALF = WIDE // CORES
TILE = 256
D = 1024
NONE = -2.0
NEVER = 1 << 30
PIECES = ((0, 0), (1, 0), (1, 1), (2, 0), (2, 1), (3, 0), (3, 1), (4, 0))
VMEM = pl.BlockSpec(memory_space=pltpu.VMEM)
LAYOUT = ((0, 0), (1, 0), (-1, 0), (2, 0), (0, 1), (-1, 1), (1, 1), (2, 1))


def device(y, z, core):
    return ((y % Y) * Z + z % Z) * CORES + core % CORES


def permute(value, target):
    pairs = [
        (device(y, z, core), device(*target(y, z, core)))
        for y in range(Y)
        for z in range(Z)
        for core in range(CORES)
    ]
    return lax.ppermute(value, "member", pairs)


def along_y(value, dy):
    return permute(value, lambda y, z, core: (y + (dy, -dy)[core], z, core))


def along_z(value):
    return permute(value, lambda y, z, core: (y, z + (1, -1)[core], core))


def swap(value):
    return permute(value, lambda y, z, core: (y, z, core + 1))


def after(value, *earlier):
    return lax.optimization_barrier((value,) + earlier)[0]


def local(kernel, out_shape, operands, scratch=(), flops=0, mib=8, name=None):
    arrays = operands + jax.tree.leaves(out_shape)
    return pl.pallas_call(
        kernel,
        out_shape=out_shape,
        in_specs=[VMEM] * len(operands),
        out_specs=jax.tree.map(lambda _: VMEM, out_shape),
        scratch_shapes=list(scratch),
        cost_estimate=pl.CostEstimate(
            flops=flops,
            bytes_accessed=sum(array.size * array.dtype.itemsize for array in arrays),
            transcendentals=0,
        ),
        compiler_params=pltpu.CompilerParams(vmem_limit_bytes=mib * 1024 * 1024),
        name=name,
    )(*operands)


def normalize_kernel(rows_ref, unit_ref):
    values = rows_ref[...].astype(jnp.float32)
    unit_ref[...] = (
        values * lax.rsqrt(jnp.sum(values * values, axis=1, keepdims=True) + 1e-06)
    ).astype(jnp.bfloat16)


def normalize(rows):
    return local(normalize_kernel, jax.ShapeDtypeStruct(rows.shape, rows.dtype), [rows], name="normalize")


def first_rows(member, offsets, shape, axis):
    core = member % CORES
    z = member // CORES % Z
    y = member // (CORES * Z)
    toward = 1 - 2 * core
    slot = lax.broadcasted_iota(jnp.int32, shape, axis)
    rows = jnp.zeros(shape, jnp.int32)
    for i, (dy, dz, dcore) in enumerate(offsets):
        first = device(y - toward * dy, z - toward * dz, core + dcore) * ROWS
        if axis == len(shape) - 1:
            rows = jnp.where(slot >= i * ROWS, first + slot - i * ROWS, rows)
        else:
            rows = jnp.where(slot == i, first, rows)
    return rows


def gather(piece_refs, out_ref):
    for i, piece_ref in enumerate(piece_refs):
        out_ref[i * ROWS : (i + 1) * ROWS, :] = piece_ref[...]
    return out_ref


def fold(pieces, low_ref, high_ref, best_ref, right_ref, left, out_ref, first=0):
    for n in range(out_ref.shape[1] // TILE):
        lanes = slice(first + n * TILE, first + (n + 1) * TILE)
        scores = lax.dot_general(
            left[...], right_ref[lanes, :], (((1,), (1,)), ((), ())), preferred_element_type=jnp.float32
        )
        best = None if best_ref is None else best_ref[:, lanes]
        index = lax.broadcasted_iota(jnp.int32, (ROWS, TILE), 0)
        for i, piece in enumerate(pieces):
            keep = index >= low_ref[piece : piece + 1, lanes]
            if piece == 0:
                keep &= index < high_ref[:, lanes]
            part = jnp.where(keep, scores[i * ROWS : (i + 1) * ROWS], NONE)
            part = jnp.max(part.reshape(-1, 8, TILE), axis=0)
            best = part if best is None else jnp.maximum(best, part)
        out_ref[:, n * TILE : (n + 1) * TILE] = best


def first_kernel(pieces, low_ref, high_ref, *refs):
    segments, piece_refs = refs[:SEGMENTS], refs[SEGMENTS:-3]
    right_ref, out_ref, left = refs[-3:]
    gather(segments, right_ref)
    fold(pieces, low_ref, high_ref, None, right_ref, gather(piece_refs, left), out_ref)


def match_kernel(pieces, low_ref, best_ref, right_ref, *refs):
    *piece_refs, out_ref, left = refs
    fold(pieces, low_ref, None, best_ref, right_ref, gather(piece_refs, left), out_ref)


def last_kernel(first, pieces, low_ref, best_ref, right_ref, piece_ref, out_ref, best):
    fold(pieces, low_ref, None, best_ref, right_ref, piece_ref, best, first)
    out_ref[...] = jnp.max(best[...], axis=0, keepdims=True)


def match(kernel, pieces, operands):
    rows = ROWS * len(pieces)
    best = jax.ShapeDtypeStruct((8, WIDE), jnp.float32)
    out, scratch = best, pltpu.VMEM((rows, D), jnp.bfloat16)
    if kernel is first_kernel:
        out = (jax.ShapeDtypeStruct((WIDE, D), jnp.bfloat16), best)
    return local(
        functools.partial(kernel, pieces),
        out,
        operands,
        scratch=[scratch],
        flops=2 * rows * WIDE * D,
        mib=16,
        name="match",
    )


def last(first, pieces, operands):
    return local(
        functools.partial(last_kernel, first, pieces),
        jax.ShapeDtypeStruct((1, HALF), jnp.float32),
        operands,
        scratch=[pltpu.VMEM((8, HALF), jnp.float32)],
        flops=2 * ROWS * HALF * D,
        mib=16,
        name="last",
    )


def shards(embeddings, first_size):
    member = lax.axis_index("member")
    split = first_size[0]
    row = first_rows(member, [(dy, 0, dcore) for dy, dcore in LAYOUT], (1, WIDE), 1)
    start = first_rows(member, [(0, dz, dcore) for dz, dcore in PIECES], (len(PIECES), WIDE), 0)
    low = jnp.where(row > start, jnp.where(row >= split, split, 0) - start, NEVER)
    high = row - start[:1]

    unit = normalize(embeddings)
    own = [unit, along_z(unit)]
    partner = swap(unit)
    other = [partner, along_z(partner)]
    for k in (1, 2):
        own.append(along_z(own[k]))
        other.append(along_z(other[k]))
    own.append(along_z(own[3]))

    near = along_y(after(unit, partner), 1)
    near_other = along_y(after(partner, near), 1)
    far = along_y(near, 1)
    mine = [unit, near, swap(after(near_other, own[2])), far]
    theirs = [partner, swap(after(near, other[1])), near_other, swap(after(far, other[2]))]

    right, best = match(first_kernel, (0, 1, 2), [low, high, *mine, *theirs, unit, own[1], other[1]])
    best = match(match_kernel, (3, 4), [low, best, right, own[2], other[2]])
    best = match(match_kernel, (5, 6), [low, best, right, own[3], other[3]])
    others = swap(last(HALF, (7,), [low, best, right, own[4]]))
    best = last(0, (7,), [low, best, right, own[4]])

    best = jnp.maximum(best, others).reshape(Y, ROWS)
    far_best = along_y(best[3], 2)
    best = jnp.maximum(
        jnp.maximum(best[0], far_best), jnp.maximum(along_y(best[2], 1), along_y(best[1], -1))
    )
    return jnp.maximum(best, -1.0)


def solution(mesh):
    placed = (P(("group", "member"), None), P("group"))
    return jax.shard_map(
        shards, mesh=mesh, in_specs=placed, out_specs=P(("group", "member")), check_vma=False
    )
```

time: 157 us -> 52.2 us (0.33)
  waiting for transfers between devices: 125 us -> 12.7 us
  starting transfers between devices: 0.01 us -> 30.1 us
  matrix products: 14 us -> 0 us
  between operations: 14.1 us -> 0.79 us
  Pallas kernels: 0 us -> 6.75 us
  other arithmetic: 3.68 us -> 0.71 us
    all_gather x1 -> x0, waiting for transfers between devices: 125 us -> none  [shards(): piece = lax.all_gather(unit, 'member', axis=0, tiled=True)]
    ppermute x0 -> x18, starting transfers between devices: none -> 30.1 us  [permute(): return lax.ppermute(value, 'member', pairs)]
    dot_general x1 -> x0, matrix products: 14 us -> none  [tile_scores(): jnp.einsum('rd,cd->rc', left, right, preferred_element_type=jnp.float32)]
    ppermute x0 -> x18, waiting for transfers between devices: none -> 12.7 us  [permute(): return lax.ppermute(value, 'member', pairs)]
    pallas_call x0 -> x6, Pallas kernels: none -> 6.75 us  [local(): pl.pallas_call(kernel, out_shape=out_shape, in_specs=[VMEM] * len(operand...]
    convert_element_type x1 -> x0, other arithmetic: 1.93 us -> none  [normalize(): (values * lax.rsqrt(jnp.sum(values * values, axis=1, keepdims=True) + 1e-...]
  transfers between devices with their start and end apart: 1 -> 18, of which waited for: 1 -> 8; matrix products, arithmetic and copies ran while one was open for 0% -> 0% of each run, Pallas kernels for 0% -> 11%
where the time goes in v4:
time: 52.2 us; the launch traced here: 52 us
  starting transfers between devices  30.1 us (58%)
  waiting for transfers between devices  12.7 us (24%)
  Pallas kernels  6.75 us (13%)
  local copies, waits for them, and re-layouts  1.07 us (2%)
  between operations  0.79 us (2%)
  other arithmetic  0.71 us (1%)
    ppermute x18, starting transfers between devices, permute(): return lax.ppermute(value, 'member', pairs)  30.1 us
    ppermute x18, waiting for transfers between devices, permute(): return lax.ppermute(value, 'member', pairs)  12.7 us
    pallas_call x6, Pallas kernels, local(): pl.pallas_call(kernel, out_shape=out_shape, in_specs=[VMEM] * len(operand...  6.75 us
  transfers between devices with their start and end apart: 18, of which 8 were waited for; matrix products, arithmetic and copies ran while one was open for 0% of the time, Pallas kernels for 11%

profile of v4, /device:TPU:1, one launch (start us, length us, event | category | flops | bytes accessed | tf_op | source)
XLA Modules:
  0.0 52.0 jit_solution(10920283625113446879)
XLA Ops:
  0.0 1.0 %copy-done = bf16[192,1024]{1,0:T(8,128)(2,1)S(1)} copy-done((bf16[192,1024]{1,0:T(8,128)(2,1)S(1)}, bf16[192,1024]{1,0:T(8,128)(2,1)}, u32[]{:S(2)}) %copy-start) | copy-done | bytes 393240
  1.2 3.3 %collective-permute-start = (bf16[192,1024]{1,0:T(8,128)(2,1)S(1)}, bf16[192,1024]{1,0:T(8,128)(2,1)S(1)}, u32[]{:S(2)}, u32[]{:S(2)}) collective-permute-start(bf16[192,1024]{1,0:T(8,128)(2,1)S(1)} %normalize.1.refs_0_.refs_8_), channel_id=1, source_target_pairs={{0,1},{1,0},{2,3},{3,2},{4,5},{5,4},{6,7},{7,6},{8,9},{9,8},{10,11... | collective-permute-start | bytes 1179656 | tf_op jit(solution)/shard_map/ppermute | solution.py:35
  4.5 3.8 %collective-permute-start.3 = (bf16[192,1024]{1,0:T(8,128)(2,1)S(1)}, bf16[192,1024]{1,0:T(8,128)(2,1)S(1)}, u32[]{:S(2)}, u32[]{:S(2)}) collective-permute-start(bf16[192,1024]{1,0:T(8,128)(2,1)S(1)} %normalize.1.refs_0_.refs_8_), channel_id=1, source_target_pairs={{0,2},{1,15},{2,4},{3,1},{4,6},{5,3},{6,8},{7,5},{8,10},{9,7},{10,... | collective-permute-start | bytes 1179656 | tf_op jit(solution)/shard_map/ppermute | solution.py:35
  9.0 2.8 %collective-permute-start.1 = (bf16[192,1024]{1,0:T(8,128)(2,1)S(1)}, bf16[192,1024]{1,0:T(8,128)(2,1)S(1)}, u32[]{:S(2)}, u32[]{:S(2)}) collective-permute-start(bf16[192,1024]{1,0:T(8,128)(2,1)S(1)} %normalize.1.refs_0_.refs_8_), channel_id=1, source_target_pairs={{0,16},{1,49},{2,18},{3,51},{4,20},{5,53},{6,22},{7,55},{8,24},{9,... | collective-permute-start | bytes 1179656 | tf_op jit(solution)/shard_map/ppermute | solution.py:35
  11.8 0.7 %collective-permute-start.7 = (bf16[192,1024]{1,0:T(8,128)(2,1)S(1)}, bf16[192,1024]{1,0:T(8,128)(2,1)S(1)}, u32[]{:S(2)}, u32[]{:S(2)}) collective-permute-start(bf16[192,1024]{1,0:T(8,128)(2,1)S(1)} %collective-permute-done.refs_4_), channel_id=1, source_target_pairs={{0,2},{1,15},{2,4},{3,1},{4,6},{5,3},{6,8},{7,5},{8,10},{9,7},{10,... | collective-permute-start | bytes 1179656 | tf_op jit(solution)/shard_map/ppermute | solution.py:35
  13.1 3.4 %collective-permute-start.4 = (bf16[192,1024]{1,0:T(8,128)(2,1)S(1)}, bf16[192,1024]{1,0:T(8,128)(2,1)S(1)}, u32[]{:S(2)}, u32[]{:S(2)}) collective-permute-start(bf16[192,1024]{1,0:T(8,128)(2,1)S(1)} %collective-permute-done.3.refs_9_), channel_id=1, source_target_pairs={{0,2},{1,15},{2,4},{3,1},{4,6},{5,3},{6,8},{7,5},{8,10},{9,7},{10,... | collective-permute-start | bytes 1179656 | tf_op jit(solution)/shard_map/ppermute | solution.py:35
  16.6 3.4 %collective-permute-start.2 = (bf16[192,1024]{1,0:T(8,128)(2,1)S(1)}, bf16[192,1024]{1,0:T(8,128)(2,1)S(1)}, u32[]{:S(2)}, u32[]{:S(2)}) collective-permute-start(bf16[192,1024]{1,0:T(8,128)(2,1)S(1)} %collective-permute-done.refs_4_), channel_id=1, source_target_pairs={{0,16},{1,49},{2,18},{3,51},{4,20},{5,53},{6,22},{7,55},{8,24},{9,... | collective-permute-start | bytes 1179656 | tf_op jit(solution)/shard_map/ppermute | solution.py:35
  20.6 2.3 %collective-permute-done.4.refs_0_ = bf16[192,1024]{1,0:T(8,128)(2,1)S(1)} collective-permute-done((bf16[192,1024]{1,0:T(8,128)(2,1)S(1)}, bf16[192,1024]{1,0:T(8,128)(2,1)S(1)}, u32[]{:S(2)}, u32[]{:S(2)}) %collective-permute-start.4) | collective-permute-done | bytes 393248 | tf_op jit(solution)/shard_map/ppermute | solution.py:35
  23.0 1.9 %collective-permute-start.11 = (bf16[192,1024]{1,0:T(8,128)(2,1)S(1)}, bf16[192,1024]{1,0:T(8,128)(2,1)S(1)}, u32[]{:S(2)}, u32[]{:S(2)}) collective-permute-start(bf16[192,1024]{1,0:T(8,128)(2,1)S(1)} %collective-permute-done.4.refs_0_), channel_id=1, source_target_pairs={{0,2},{1,15},{2,4},{3,1},{4,6},{5,3},{6,8},{7,5},{8,10},{9,7},{10,... | collective-permute-start | bytes 1179656 | tf_op jit(solution)/shard_map/ppermute | solution.py:35
  24.9 4.0 %collective-permute-done.6.refs_3_ = bf16[192,1024]{1,0:T(8,128)(2,1)S(1)} collective-permute-done((bf16[192,1024]{1,0:T(8,128)(2,1)S(1)}, bf16[192,1024]{1,0:T(8,128)(2,1)S(1)}, u32[]{:S(2)}, u32[]{:S(2)}) %collective-permute-start.6) | collective-permute-done | bytes 393248 | tf_op jit(solution)/shard_map/ppermute | solution.py:35
  28.9 3.3 %collective-permute-start.12 = (bf16[192,1024]{1,0:T(8,128)(2,1)S(1)}, bf16[192,1024]{1,0:T(8,128)(2,1)S(1)}, u32[]{:S(2)}, u32[]{:S(2)}) collective-permute-start(bf16[192,1024]{1,0:T(8,128)(2,1)S(1)} %collective-permute-done.9.refs_1_), channel_id=1, source_target_pairs={{0,2},{1,15},{2,4},{3,1},{4,6},{5,3},{6,8},{7,5},{8,10},{9,7},{10,... | collective-permute-start | bytes 1179656 | tf_op jit(solution)/shard_map/ppermute | solution.py:35
  32.3 1.1 %collective-permute-start.13 = (bf16[192,1024]{1,0:T(8,128)(2,1)S(1)}, bf16[192,1024]{1,0:T(8,128)(2,1)S(1)}, u32[]{:S(2)}, u32[]{:S(2)}) collective-permute-start(bf16[192,1024]{1,0:T(8,128)(2,1)S(1)} %collective-permute-done.11.refs_0_), channel_id=1, source_target_pairs={{0,2},{1,15},{2,4},{3,1},{4,6},{5,3},{6,8},{7,5},{8,10},{9,7},{10,... | collective-permute-start | bytes 1179656 | tf_op jit(solution)/shard_map/ppermute | solution.py:35
  33.4 2.3 %match.3 = (bf16[1536,1024]{1,0:T(8,128)(2,1)S(1)}, f32[8,1536]{1,0:T(8,128)S(1)}) custom-call(s32[8,1536]{1,0:T(8,128)S(1)} %get-tuple-element.20.low_ref, s32[1,1536]{1,0:T(1,128)S(1)} %fusion.high_ref, bf16[192,1024]{1,0:T(8,128)(2,1)S(1)} %normalize.1.refs_0_.refs_8_, bf16[192,1024]{1,0:T(8,128)(2,1)S(1)} %collective-permute-done.1.refs_1_, ...), custom_call_target="tpu_custom_call" | custom-call | flops 1811939328 | bytes 7575552 | tf_op jit(solution)/shard_map/match/pallas_call | solution.py:56
  35.8 1.5 %match.4.best_ref = f32[8,1536]{1,0:T(8,128)S(1)} custom-call(s32[8,1536]{1,0:T(8,128)S(1)} %get-tuple-element.20.low_ref, f32[8,1536]{1,0:T(8,128)S(1)} %get-tuple-element.17.best_ref, bf16[1536,1024]{1,0:T(8,128)(2,1)S(1)} %get-tuple-element.18.right_ref, bf16[192,1024]{1,0:T(8,128)(2,1)S(1)} %collective-permute-done.4.refs_0_, ...), custom_call_target="tpu_custom_call" | custom-call | flops 1207959552 | bytes 4079616 | tf_op jit(solution)/shard_map/match/pallas_call | solution.py:56
  37.2 1.5 %match.5.best_ref = f32[8,1536]{1,0:T(8,128)S(1)} custom-call(s32[8,1536]{1,0:T(8,128)S(1)} %get-tuple-element.20.low_ref, f32[8,1536]{1,0:T(8,128)S(1)} %match.4.best_ref, bf16[1536,1024]{1,0:T(8,128)(2,1)S(1)} %get-tuple-element.18.right_ref, bf16[192,1024]{1,0:T(8,128)(2,1)S(1)} %collective-permute-done.11.refs_0_, ...), custom_call_target="tpu_custom_call" | custom-call | flops 1207959552 | bytes 4079616 | tf_op jit(solution)/shard_map/match/pallas_call | solution.py:56
  38.7 2.5 %collective-permute-done.13.piece_ref = bf16[192,1024]{1,0:T(8,128)(2,1)S(1)} collective-permute-done((bf16[192,1024]{1,0:T(8,128)(2,1)S(1)}, bf16[192,1024]{1,0:T(8,128)(2,1)S(1)}, u32[]{:S(2)}, u32[]{:S(2)}) %collective-permute-start.13) | collective-permute-done | bytes 393248 | tf_op jit(solution)/shard_map/ppermute | solution.py:35
  41.2 0.7 %last.3 = f32[1,768]{1,0:T(1,128)S(1)} custom-call(s32[8,1536]{1,0:T(8,128)S(1)} %get-tuple-element.20.low_ref, f32[8,1536]{1,0:T(8,128)S(1)} %match.5.best_ref, bf16[1536,1024]{1,0:T(8,128)(2,1)S(1)} %get-tuple-element.18.right_ref, bf16[192,1024]{1,0:T(8,128)(2,1)S(1)} %collective-permute-done.13.piece_ref), custom_call_target="tpu_custom_call" | custom-call | flops 301989888 | bytes 3640320 | tf_op jit(solution)/shard_map/last/pallas_call | solution.py:56
  41.9 1.5 %collective-permute-start.14 = (f32[1,768]{1,0:T(1,128)S(1)}, f32[1,768]{1,0:T(1,128)S(1)}, u32[]{:S(2)}, u32[]{:S(2)}) collective-permute-start(f32[1,768]{1,0:T(1,128)S(1)} %last.3), channel_id=1, source_target_pairs={{0,1},{1,0},{2,3},{3,2},{4,5},{5,4},{6,7},{7,6},{8,9},{9,8},{10,11... | collective-permute-start | bytes 9224 | tf_op jit(solution)/shard_map/ppermute | solution.py:35
  43.4 0.7 %last.2 = f32[1,768]{1,0:T(1,128)S(1)} custom-call(s32[8,1536]{1,0:T(8,128)S(1)} %get-tuple-element.20.low_ref, f32[8,1536]{1,0:T(8,128)S(1)} %match.5.best_ref, bf16[1536,1024]{1,0:T(8,128)(2,1)S(1)} %get-tuple-element.18.right_ref, bf16[192,1024]{1,0:T(8,128)(2,1)S(1)} %collective-permute-done.13.piece_ref), custom_call_target="tpu_custom_call" | custom-call | flops 301989888 | bytes 3640320 | tf_op jit(solution)/shard_map/last/pallas_call | solution.py:56
  44.3 1.9 %collective-permute-start.15 = (f32[192]{0:T(256)S(1)}, f32[192]{0:T(256)S(1)}, u32[]{:S(2)}, u32[]{:S(2)}) collective-permute-start(f32[192]{0:T(256)S(1)} %bitcast.9), channel_id=1, source_target_pairs={{0,32},{1,33},{2,34},{3,35},{4,36},{5,37},{6,38},{7,39},{8,40},{9,... | collective-permute-start | bytes 2312 | tf_op jit(solution)/shard_map/ppermute | solution.py:35
  46.3 1.6 %collective-permute-start.16 = (f32[192]{0:T(256)S(1)}, f32[192]{0:T(256)S(1)}, u32[]{:S(2)}, u32[]{:S(2)}) collective-permute-start(f32[192]{0:T(256)S(1)} %bitcast.8), channel_id=1, source_target_pairs={{0,16},{1,49},{2,18},{3,51},{4,20},{5,53},{6,22},{7,55},{8,24},{9,... | collective-permute-start | bytes 2312 | tf_op jit(solution)/shard_map/ppermute | solution.py:35
  48.3 1.0 %collective-permute-done.16 = f32[192]{0:T(256)S(1)} collective-permute-done((f32[192]{0:T(256)S(1)}, f32[192]{0:T(256)S(1)}, u32[]{:S(2)}, u32[]{:S(2)}) %collective-permute-start.16) | collective-permute-done | bytes 800 | tf_op jit(solution)/shard_map/ppermute | solution.py:35
  49.4 2.1 %collective-permute-done.17 = f32[192]{0:T(256)S(1)} collective-permute-done((f32[192]{0:T(256)S(1)}, f32[192]{0:T(256)S(1)}, u32[]{:S(2)}, u32[]{:S(2)}) %collective-permute-start.17) | collective-permute-done | bytes 800 | tf_op jit(solution)/shard_map/ppermute | solution.py:35
  51.5 0.6 %maximum_maximum_fusion = f32[192]{0:T(256)} fusion(f32[192]{0:T(256)S(1)} %collective-permute-done.16, f32[192]{0:T(256)S(1)} %collective-permute-done.17, f32[192]{0:T(256)S(1)} %bitcast.6, f32[192]{0:T(256)S(1)} %collective-permute-done.15), kind=kLoop, calls=%fused_computation.20 | loop fusion | flops 768 | bytes 3840 | tf_op jit(solution)/shard_map/max | solution.py:203
  (31 shorter events, 2.1 us)
Async XLA Ops:
  0.0 1.0 %copy-start = (bf16[192,1024]{1,0:T(8,128)(2,1)S(1)}, bf16[192,1024]{1,0:T(8,128)(2,1)}, u32[]{:S(2)}) copy-start(bf16[192,1024]{1,0:T(8,128)(2,1)} %rows_ref.1) | copy-start | bytes 1179652
  1.2 7.9 %collective-permute-start = (bf16[192,1024]{1,0:T(8,128)(2,1)S(1)}, bf16[192,1024]{1,0:T(8,128)(2,1)S(1)}, u32[]{:S(2)}, u32[]{:S(2)}) collective-permute-start(bf16[192,1024]{1,0:T(8,128)(2,1)S(1)} %normalize.1.refs_0_.refs_8_), channel_id=1, source_target_pairs={{0,1},{1,0},{2,3},{3,2},{4,5},{5,4},{6,7},{7,6},{8,9},{9,8},{10,11... | collective-permute-start | bytes 1179656 | tf_op jit(solution)/shard_map/ppermute | solution.py:35
  4.5 8.6 %collective-permute-start.3 = (bf16[192,1024]{1,0:T(8,128)(2,1)S(1)}, bf16[192,1024]{1,0:T(8,128)(2,1)S(1)}, u32[]{:S(2)}, u32[]{:S(2)}) collective-permute-start(bf16[192,1024]{1,0:T(8,128)(2,1)S(1)} %normalize.1.refs_0_.refs_8_), channel_id=1, source_target_pairs={{0,2},{1,15},{2,4},{3,1},{4,6},{5,3},{6,8},{7,5},{8,10},{9,7},{10,... | collective-permute-start | bytes 1179656 | tf_op jit(solution)/shard_map/ppermute | solution.py:35
  9.0 7.5 %collective-permute-start.1 = (bf16[192,1024]{1,0:T(8,128)(2,1)S(1)}, bf16[192,1024]{1,0:T(8,128)(2,1)S(1)}, u32[]{:S(2)}, u32[]{:S(2)}) collective-permute-start(bf16[192,1024]{1,0:T(8,128)(2,1)S(1)} %normalize.1.refs_0_.refs_8_), channel_id=1, source_target_pairs={{0,16},{1,49},{2,18},{3,51},{4,20},{5,53},{6,22},{7,55},{8,24},{9,... | collective-permute-start | bytes 1179656 | tf_op jit(solution)/shard_map/ppermute | solution.py:35
  11.8 8.2 %collective-permute-start.7 = (bf16[192,1024]{1,0:T(8,128)(2,1)S(1)}, bf16[192,1024]{1,0:T(8,128)(2,1)S(1)}, u32[]{:S(2)}, u32[]{:S(2)}) collective-permute-start(bf16[192,1024]{1,0:T(8,128)(2,1)S(1)} %collective-permute-done.refs_4_), channel_id=1, source_target_pairs={{0,2},{1,15},{2,4},{3,1},{4,6},{5,3},{6,8},{7,5},{8,10},{9,7},{10,... | collective-permute-start | bytes 1179656 | tf_op jit(solution)/shard_map/ppermute | solution.py:35
  13.1 9.9 %collective-permute-start.4 = (bf16[192,1024]{1,0:T(8,128)(2,1)S(1)}, bf16[192,1024]{1,0:T(8,128)(2,1)S(1)}, u32[]{:S(2)}, u32[]{:S(2)}) collective-permute-start(bf16[192,1024]{1,0:T(8,128)(2,1)S(1)} %collective-permute-done.3.refs_9_), channel_id=1, source_target_pairs={{0,2},{1,15},{2,4},{3,1},{4,6},{5,3},{6,8},{7,5},{8,10},{9,7},{10,... | collective-permute-start | bytes 1179656 | tf_op jit(solution)/shard_map/ppermute | solution.py:35
  16.6 8.4 %collective-permute-start.2 = (bf16[192,1024]{1,0:T(8,128)(2,1)S(1)}, bf16[192,1024]{1,0:T(8,128)(2,1)S(1)}, u32[]{:S(2)}, u32[]{:S(2)}) collective-permute-start(bf16[192,1024]{1,0:T(8,128)(2,1)S(1)} %collective-permute-done.refs_4_), channel_id=1, source_target_pairs={{0,16},{1,49},{2,18},{3,51},{4,20},{5,53},{6,22},{7,55},{8,24},{9,... | collective-permute-start | bytes 1179656 | tf_op jit(solution)/shard_map/ppermute | solution.py:35
  20.0 8.9 %collective-permute-start.6 = (bf16[192,1024]{1,0:T(8,128)(2,1)S(1)}, bf16[192,1024]{1,0:T(8,128)(2,1)S(1)}, u32[]{:S(2)}, u32[]{:S(2)}) collective-permute-start(bf16[192,1024]{1,0:T(8,128)(2,1)S(1)} %collective-permute-done.1.refs_1_), channel_id=1, source_target_pairs={{0,16},{1,49},{2,18},{3,51},{4,20},{5,53},{6,22},{7,55},{8,24},{9,... | collective-permute-start | bytes 1179656 | tf_op jit(solution)/shard_map/ppermute | solution.py:35
  20.0 8.9 %collective-permute-start.9 = (bf16[192,1024]{1,0:T(8,128)(2,1)S(1)}, bf16[192,1024]{1,0:T(8,128)(2,1)S(1)}, u32[]{:S(2)}, u32[]{:S(2)}) collective-permute-start(bf16[192,1024]{1,0:T(8,128)(2,1)S(1)} %collective-permute-done.7.refs_10_), channel_id=1, source_target_pairs={{0,2},{1,15},{2,4},{3,1},{4,6},{5,3},{6,8},{7,5},{8,10},{9,7},{10,... | collective-permute-start | bytes 1179656 | tf_op jit(solution)/shard_map/ppermute | solution.py:35
  20.5 12.9 %collective-permute-start.8 = (bf16[192,1024]{1,0:T(8,128)(2,1)S(1)}, bf16[192,1024]{1,0:T(8,128)(2,1)S(1)}, u32[]{:S(2)}, u32[]{:S(2)}) collective-permute-start(bf16[192,1024]{1,0:T(8,128)(2,1)S(1)} %collective-permute-done.1.refs_1_), channel_id=1, source_target_pairs={{0,1},{1,0},{2,3},{3,2},{4,5},{5,4},{6,7},{7,6},{8,9},{9,8},{10,11... | collective-permute-start | bytes 1179656 | tf_op jit(solution)/shard_map/ppermute | solution.py:35
  23.0 9.3 %collective-permute-start.11 = (bf16[192,1024]{1,0:T(8,128)(2,1)S(1)}, bf16[192,1024]{1,0:T(8,128)(2,1)S(1)}, u32[]{:S(2)}, u32[]{:S(2)}) collective-permute-start(bf16[192,1024]{1,0:T(8,128)(2,1)S(1)} %collective-permute-done.4.refs_0_), channel_id=1, source_target_pairs={{0,2},{1,15},{2,4},{3,1},{4,6},{5,3},{6,8},{7,5},{8,10},{9,7},{10,... | collective-permute-start | bytes 1179656 | tf_op jit(solution)/shard_map/ppermute | solution.py:35
  24.9 8.5 %collective-permute-start.5 = (bf16[192,1024]{1,0:T(8,128)(2,1)S(1)}, bf16[192,1024]{1,0:T(8,128)(2,1)S(1)}, u32[]{:S(2)}, u32[]{:S(2)}) collective-permute-start(bf16[192,1024]{1,0:T(8,128)(2,1)S(1)} %collective-permute-done.2.refs_6_), channel_id=1, source_target_pairs={{0,1},{1,0},{2,3},{3,2},{4,5},{5,4},{6,7},{7,6},{8,9},{9,8},{10,11... | collective-permute-start | bytes 1179656 | tf_op jit(solution)/shard_map/ppermute | solution.py:35
  28.9 4.5 %collective-permute-start.10 = (bf16[192,1024]{1,0:T(8,128)(2,1)S(1)}, bf16[192,1024]{1,0:T(8,128)(2,1)S(1)}, u32[]{:S(2)}, u32[]{:S(2)}) collective-permute-start(bf16[192,1024]{1,0:T(8,128)(2,1)S(1)} %collective-permute-done.6.refs_3_), channel_id=1, source_target_pairs={{0,1},{1,0},{2,3},{3,2},{4,5},{5,4},{6,7},{7,6},{8,9},{9,8},{10,11... | collective-permute-start | bytes 1179656 | tf_op jit(solution)/shard_map/ppermute | solution.py:35
  28.9 8.3 %collective-permute-start.12 = (bf16[192,1024]{1,0:T(8,128)(2,1)S(1)}, bf16[192,1024]{1,0:T(8,128)(2,1)S(1)}, u32[]{:S(2)}, u32[]{:S(2)}) collective-permute-start(bf16[192,1024]{1,0:T(8,128)(2,1)S(1)} %collective-permute-done.9.refs_1_), channel_id=1, source_target_pairs={{0,2},{1,15},{2,4},{3,1},{4,6},{5,3},{6,8},{7,5},{8,10},{9,7},{10,... | collective-permute-start | bytes 1179656 | tf_op jit(solution)/shard_map/ppermute | solution.py:35
  32.3 8.9 %collective-permute-start.13 = (bf16[192,1024]{1,0:T(8,128)(2,1)S(1)}, bf16[192,1024]{1,0:T(8,128)(2,1)S(1)}, u32[]{:S(2)}, u32[]{:S(2)}) collective-permute-start(bf16[192,1024]{1,0:T(8,128)(2,1)S(1)} %collective-permute-done.11.refs_0_), channel_id=1, source_target_pairs={{0,2},{1,15},{2,4},{3,1},{4,6},{5,3},{6,8},{7,5},{8,10},{9,7},{10,... | collective-permute-start | bytes 1179656 | tf_op jit(solution)/shard_map/ppermute | solution.py:35
  41.9 2.4 %collective-permute-start.14 = (f32[1,768]{1,0:T(1,128)S(1)}, f32[1,768]{1,0:T(1,128)S(1)}, u32[]{:S(2)}, u32[]{:S(2)}) collective-permute-start(f32[1,768]{1,0:T(1,128)S(1)} %last.3), channel_id=1, source_target_pairs={{0,1},{1,0},{2,3},{3,2},{4,5},{5,4},{6,7},{7,6},{8,9},{9,8},{10,11... | collective-permute-start | bytes 9224 | tf_op jit(solution)/shard_map/ppermute | solution.py:35
  44.3 4.0 %collective-permute-start.15 = (f32[192]{0:T(256)S(1)}, f32[192]{0:T(256)S(1)}, u32[]{:S(2)}, u32[]{:S(2)}) collective-permute-start(f32[192]{0:T(256)S(1)} %bitcast.9), channel_id=1, source_target_pairs={{0,32},{1,33},{2,34},{3,35},{4,36},{5,37},{6,38},{7,39},{8,40},{9,... | collective-permute-start | bytes 2312 | tf_op jit(solution)/shard_map/ppermute | solution.py:35
  46.3 3.1 %collective-permute-start.16 = (f32[192]{0:T(256)S(1)}, f32[192]{0:T(256)S(1)}, u32[]{:S(2)}, u32[]{:S(2)}) collective-permute-start(f32[192]{0:T(256)S(1)} %bitcast.8), channel_id=1, source_target_pairs={{0,16},{1,49},{2,18},{3,51},{4,20},{5,53},{6,22},{7,55},{8,24},{9,... | collective-permute-start | bytes 2312 | tf_op jit(solution)/shard_map/ppermute | solution.py:35
  47.8 3.6 %collective-permute-start.17 = (f32[192]{0:T(256)S(1)}, f32[192]{0:T(256)S(1)}, u32[]{:S(2)}, u32[]{:S(2)}) collective-permute-start(f32[192]{0:T(256)S(1)} %bitcast.7), channel_id=1, source_target_pairs={{0,48},{1,17},{2,50},{3,19},{4,52},{5,21},{6,54},{7,23},{8,56},{9,... | collective-permute-start | bytes 2312 | tf_op jit(solution)/shard_map/ppermute | solution.py:35

commit v5 on v4

--- a/solution.py
+++ b/solution.py
@@ -184,10 +184,10 @@
     own.append(along_z(own[3]))
 
     near = along_y(after(unit, partner), 1)
-    near_other = along_y(after(partner, near), 1)
+    near_other = along_y(partner, 1)
     far = along_y(near, 1)
-    mine = [unit, near, swap(after(near_other, own[2])), far]
-    theirs = [partner, swap(after(near, other[1])), near_other, swap(after(far, other[2]))]
+    mine = [unit, near, swap(near_other), far]
+    theirs = [partner, swap(after(near, other[1])), near_other, swap(far)]
 
     right, best = match(first_kernel, (0, 1, 2), [low, high, *mine, *theirs, unit, own[1], other[1]])
     best = match(match_kernel, (3, 4), [low, best, right, own[2], other[2]])

time: 52.2 us -> 51.1 us (0.979)
  waiting for transfers between devices: 12.7 us -> 11.1 us
    ppermute x18, waiting for transfers between devices: 12.7 us -> 11.1 us  [permute(): return lax.ppermute(value, 'member', pairs)]
  transfers between devices with their start and end apart: 18 -> 18, of which waited for: 8 -> 9; matrix products, arithmetic and copies ran while one was open for 0% -> 0% of each run, Pallas kernels for 11% -> 12%
where the time goes in v5:
time: 51.1 us; the launch traced here: 51 us
  starting transfers between devices  30.6 us (60%)
  waiting for transfers between devices  11.1 us (22%)
  Pallas kernels  6.75 us (13%)
  local copies, waits for them, and re-layouts  1.07 us (2%)
  between operations  0.79 us (2%)
  other arithmetic  0.71 us (1%)
    ppermute x18, starting transfers between devices, permute(): return lax.ppermute(value, 'member', pairs)  30.6 us
    ppermute x18, waiting for transfers between devices, permute(): return lax.ppermute(value, 'member', pairs)  11.1 us
    pallas_call x6, Pallas kernels, local(): pl.pallas_call(kernel, out_shape=out_shape, in_specs=[VMEM] * len(operand...  6.75 us
  transfers between devices with their start and end apart: 18, of which 9 were waited for; matrix products, arithmetic and copies ran while one was open for 0% of the time, Pallas kernels for 12%

profile of v5, /device:TPU:1, one launch (start us, length us, event | category | flops | bytes accessed | tf_op | source)
XLA Modules:
  0.0 51.0 jit_solution(7560300268147926073)
XLA Ops:
  0.0 1.0 %copy-done = bf16[192,1024]{1,0:T(8,128)(2,1)S(1)} copy-done((bf16[192,1024]{1,0:T(8,128)(2,1)S(1)}, bf16[192,1024]{1,0:T(8,128)(2,1)}, u32[]{:S(2)}) %copy-start) | copy-done | bytes 393240
  1.2 3.3 %collective-permute-start = (bf16[192,1024]{1,0:T(8,128)(2,1)S(1)}, bf16[192,1024]{1,0:T(8,128)(2,1)S(1)}, u32[]{:S(2)}, u32[]{:S(2)}) collective-permute-start(bf16[192,1024]{1,0:T(8,128)(2,1)S(1)} %normalize.1.refs_0_.refs_8_), channel_id=1, source_target_pairs={{0,1},{1,0},{2,3},{3,2},{4,5},{5,4},{6,7},{7,6},{8,9},{9,8},{10,11... | collective-permute-start | bytes 1179656 | tf_op jit(solution)/shard_map/ppermute | solution.py:35
  4.5 3.8 %collective-permute-start.8 = (bf16[192,1024]{1,0:T(8,128)(2,1)S(1)}, bf16[192,1024]{1,0:T(8,128)(2,1)S(1)}, u32[]{:S(2)}, u32[]{:S(2)}) collective-permute-start(bf16[192,1024]{1,0:T(8,128)(2,1)S(1)} %normalize.1.refs_0_.refs_8_), channel_id=1, source_target_pairs={{0,2},{1,15},{2,4},{3,1},{4,6},{5,3},{6,8},{7,5},{8,10},{9,7},{10,... | collective-permute-start | bytes 1179656 | tf_op jit(solution)/shard_map/ppermute | solution.py:35
  9.0 2.8 %collective-permute-start.1 = (bf16[192,1024]{1,0:T(8,128)(2,1)S(1)}, bf16[192,1024]{1,0:T(8,128)(2,1)S(1)}, u32[]{:S(2)}, u32[]{:S(2)}) collective-permute-start(bf16[192,1024]{1,0:T(8,128)(2,1)S(1)} %normalize.1.refs_0_.refs_8_), channel_id=1, source_target_pairs={{0,16},{1,49},{2,18},{3,51},{4,20},{5,53},{6,22},{7,55},{8,24},{9,... | collective-permute-start | bytes 1179656 | tf_op jit(solution)/shard_map/ppermute | solution.py:35
  11.8 0.7 %collective-permute-start.5 = (bf16[192,1024]{1,0:T(8,128)(2,1)S(1)}, bf16[192,1024]{1,0:T(8,128)(2,1)S(1)}, u32[]{:S(2)}, u32[]{:S(2)}) collective-permute-start(bf16[192,1024]{1,0:T(8,128)(2,1)S(1)} %collective-permute-done.refs_4_), channel_id=1, source_target_pairs={{0,2},{1,15},{2,4},{3,1},{4,6},{5,3},{6,8},{7,5},{8,10},{9,7},{10,... | collective-permute-start | bytes 1179656 | tf_op jit(solution)/shard_map/ppermute | solution.py:35
  13.2 3.3 %collective-permute-start.9 = (bf16[192,1024]{1,0:T(8,128)(2,1)S(1)}, bf16[192,1024]{1,0:T(8,128)(2,1)S(1)}, u32[]{:S(2)}, u32[]{:S(2)}) collective-permute-start(bf16[192,1024]{1,0:T(8,128)(2,1)S(1)} %collective-permute-done.8.refs_9_), channel_id=1, source_target_pairs={{0,2},{1,15},{2,4},{3,1},{4,6},{5,3},{6,8},{7,5},{8,10},{9,7},{10,... | collective-permute-start | bytes 1179656 | tf_op jit(solution)/shard_map/ppermute | solution.py:35
  16.6 3.4 %collective-permute-start.4 = (bf16[192,1024]{1,0:T(8,128)(2,1)S(1)}, bf16[192,1024]{1,0:T(8,128)(2,1)S(1)}, u32[]{:S(2)}, u32[]{:S(2)}) collective-permute-start(bf16[192,1024]{1,0:T(8,128)(2,1)S(1)} %collective-permute-done.1.refs_1_), channel_id=1, source_target_pairs={{0,16},{1,49},{2,18},{3,51},{4,20},{5,53},{6,22},{7,55},{8,24},{9,... | collective-permute-start | bytes 1179656 | tf_op jit(solution)/shard_map/ppermute | solution.py:35
  20.0 0.7 %collective-permute-start.10 = (bf16[192,1024]{1,0:T(8,128)(2,1)S(1)}, bf16[192,1024]{1,0:T(8,128)(2,1)S(1)}, u32[]{:S(2)}, u32[]{:S(2)}) collective-permute-start(bf16[192,1024]{1,0:T(8,128)(2,1)S(1)} %collective-permute-done.5.refs_10_), channel_id=1, source_target_pairs={{0,2},{1,15},{2,4},{3,1},{4,6},{5,3},{6,8},{7,5},{8,10},{9,7},{10,... | collective-permute-start | bytes 1179656 | tf_op jit(solution)/shard_map/ppermute | solution.py:35
  21.4 1.6 %collective-permute-done.9.refs_0_ = bf16[192,1024]{1,0:T(8,128)(2,1)S(1)} collective-permute-done((bf16[192,1024]{1,0:T(8,128)(2,1)S(1)}, bf16[192,1024]{1,0:T(8,128)(2,1)S(1)}, u32[]{:S(2)}, u32[]{:S(2)}) %collective-permute-start.9) | collective-permute-done | bytes 393248 | tf_op jit(solution)/shard_map/ppermute | solution.py:35
  23.0 1.9 %collective-permute-start.11 = (bf16[192,1024]{1,0:T(8,128)(2,1)S(1)}, bf16[192,1024]{1,0:T(8,128)(2,1)S(1)}, u32[]{:S(2)}, u32[]{:S(2)}) collective-permute-start(bf16[192,1024]{1,0:T(8,128)(2,1)S(1)} %collective-permute-done.9.refs_0_), channel_id=1, source_target_pairs={{0,2},{1,15},{2,4},{3,1},{4,6},{5,3},{6,8},{7,5},{8,10},{9,7},{10,... | collective-permute-start | bytes 1179656 | tf_op jit(solution)/shard_map/ppermute | solution.py:35
  25.0 2.2 %collective-permute-done.10.refs_1_ = bf16[192,1024]{1,0:T(8,128)(2,1)S(1)} collective-permute-done((bf16[192,1024]{1,0:T(8,128)(2,1)S(1)}, bf16[192,1024]{1,0:T(8,128)(2,1)S(1)}, u32[]{:S(2)}, u32[]{:S(2)}) %collective-permute-start.10) | collective-permute-done | bytes 393248 | tf_op jit(solution)/shard_map/ppermute | solution.py:35
  27.2 1.6 %collective-permute-start.12 = (bf16[192,1024]{1,0:T(8,128)(2,1)S(1)}, bf16[192,1024]{1,0:T(8,128)(2,1)S(1)}, u32[]{:S(2)}, u32[]{:S(2)}) collective-permute-start(bf16[192,1024]{1,0:T(8,128)(2,1)S(1)} %collective-permute-done.10.refs_1_), channel_id=1, source_target_pairs={{0,2},{1,15},{2,4},{3,1},{4,6},{5,3},{6,8},{7,5},{8,10},{9,7},{10,... | collective-permute-start | bytes 1179656 | tf_op jit(solution)/shard_map/ppermute | solution.py:35
  28.9 2.6 %collective-permute-done.11.refs_0_ = bf16[192,1024]{1,0:T(8,128)(2,1)S(1)} collective-permute-done((bf16[192,1024]{1,0:T(8,128)(2,1)S(1)}, bf16[192,1024]{1,0:T(8,128)(2,1)S(1)}, u32[]{:S(2)}, u32[]{:S(2)}) %collective-permute-start.11) | collective-permute-done | bytes 393248 | tf_op jit(solution)/shard_map/ppermute | solution.py:35
  31.4 1.6 %collective-permute-start.13 = (bf16[192,1024]{1,0:T(8,128)(2,1)S(1)}, bf16[192,1024]{1,0:T(8,128)(2,1)S(1)}, u32[]{:S(2)}, u32[]{:S(2)}) collective-permute-start(bf16[192,1024]{1,0:T(8,128)(2,1)S(1)} %collective-permute-done.11.refs_0_), channel_id=1, source_target_pairs={{0,2},{1,15},{2,4},{3,1},{4,6},{5,3},{6,8},{7,5},{8,10},{9,7},{10,... | collective-permute-start | bytes 1179656 | tf_op jit(solution)/shard_map/ppermute | solution.py:35
  33.1 2.3 %match.3 = (bf16[1536,1024]{1,0:T(8,128)(2,1)S(1)}, f32[8,1536]{1,0:T(8,128)S(1)}) custom-call(s32[8,1536]{1,0:T(8,128)S(1)} %get-tuple-element.14.low_ref, s32[1,1536]{1,0:T(1,128)S(1)} %fusion.high_ref, bf16[192,1024]{1,0:T(8,128)(2,1)S(1)} %normalize.1.refs_0_.refs_8_, bf16[192,1024]{1,0:T(8,128)(2,1)S(1)} %collective-permute-done.1.refs_1_, ...), custom_call_target="tpu_custom_call" | custom-call | flops 1811939328 | bytes 7575552 | tf_op jit(solution)/shard_map/match/pallas_call | solution.py:56
  35.4 1.5 %match.4.best_ref = f32[8,1536]{1,0:T(8,128)S(1)} custom-call(s32[8,1536]{1,0:T(8,128)S(1)} %get-tuple-element.14.low_ref, f32[8,1536]{1,0:T(8,128)S(1)} %get-tuple-element.11.best_ref, bf16[1536,1024]{1,0:T(8,128)(2,1)S(1)} %get-tuple-element.12.right_ref, bf16[192,1024]{1,0:T(8,128)(2,1)S(1)} %collective-permute-done.9.refs_0_, ...), custom_call_target="tpu_custom_call" | custom-call | flops 1207959552 | bytes 4079616 | tf_op jit(solution)/shard_map/match/pallas_call | solution.py:56
  36.9 1.5 %match.5.best_ref = f32[8,1536]{1,0:T(8,128)S(1)} custom-call(s32[8,1536]{1,0:T(8,128)S(1)} %get-tuple-element.14.low_ref, f32[8,1536]{1,0:T(8,128)S(1)} %match.4.best_ref, bf16[1536,1024]{1,0:T(8,128)(2,1)S(1)} %get-tuple-element.12.right_ref, bf16[192,1024]{1,0:T(8,128)(2,1)S(1)} %collective-permute-done.11.refs_0_, ...), custom_call_target="tpu_custom_call" | custom-call | flops 1207959552 | bytes 4079616 | tf_op jit(solution)/shard_map/match/pallas_call | solution.py:56
  38.3 1.5 %collective-permute-done.13.piece_ref = bf16[192,1024]{1,0:T(8,128)(2,1)S(1)} collective-permute-done((bf16[192,1024]{1,0:T(8,128)(2,1)S(1)}, bf16[192,1024]{1,0:T(8,128)(2,1)S(1)}, u32[]{:S(2)}, u32[]{:S(2)}) %collective-permute-start.13) | collective-permute-done | bytes 393248 | tf_op jit(solution)/shard_map/ppermute | solution.py:35
  40.5 1.7 %collective-permute-start.14 = (f32[1,768]{1,0:T(1,128)S(1)}, f32[1,768]{1,0:T(1,128)S(1)}, u32[]{:S(2)}, u32[]{:S(2)}) collective-permute-start(f32[1,768]{1,0:T(1,128)S(1)} %last.3), channel_id=1, source_target_pairs={{0,1},{1,0},{2,3},{3,2},{4,5},{5,4},{6,7},{7,6},{8,9},{9,8},{10,11... | collective-permute-start | bytes 9224 | tf_op jit(solution)/shard_map/ppermute | solution.py:35
  43.1 2.9 %collective-permute-start.15 = (f32[192]{0:T(256)S(1)}, f32[192]{0:T(256)S(1)}, u32[]{:S(2)}, u32[]{:S(2)}) collective-permute-start(f32[192]{0:T(256)S(1)} %bitcast.9), channel_id=1, source_target_pairs={{0,32},{1,33},{2,34},{3,35},{4,36},{5,37},{6,38},{7,39},{8,40},{9,... | collective-permute-start | bytes 2312 | tf_op jit(solution)/shard_map/ppermute | solution.py:35
  46.0 0.8 %collective-permute-start.16 = (f32[192]{0:T(256)S(1)}, f32[192]{0:T(256)S(1)}, u32[]{:S(2)}, u32[]{:S(2)}) collective-permute-start(f32[192]{0:T(256)S(1)} %bitcast.8), channel_id=1, source_target_pairs={{0,16},{1,49},{2,18},{3,51},{4,20},{5,53},{6,22},{7,55},{8,24},{9,... | collective-permute-start | bytes 2312 | tf_op jit(solution)/shard_map/ppermute | solution.py:35
  46.8 0.7 %collective-permute-start.17 = (f32[192]{0:T(256)S(1)}, f32[192]{0:T(256)S(1)}, u32[]{:S(2)}, u32[]{:S(2)}) collective-permute-start(f32[192]{0:T(256)S(1)} %bitcast.7), channel_id=1, source_target_pairs={{0,48},{1,17},{2,50},{3,19},{4,52},{5,21},{6,54},{7,23},{8,56},{9,... | collective-permute-start | bytes 2312 | tf_op jit(solution)/shard_map/ppermute | solution.py:35
  47.5 0.9 %collective-permute-done.16 = f32[192]{0:T(256)S(1)} collective-permute-done((f32[192]{0:T(256)S(1)}, f32[192]{0:T(256)S(1)}, u32[]{:S(2)}, u32[]{:S(2)}) %collective-permute-start.16) | collective-permute-done | bytes 800 | tf_op jit(solution)/shard_map/ppermute | solution.py:35
  48.5 2.0 %collective-permute-done.17 = f32[192]{0:T(256)S(1)} collective-permute-done((f32[192]{0:T(256)S(1)}, f32[192]{0:T(256)S(1)}, u32[]{:S(2)}, u32[]{:S(2)}) %collective-permute-start.17) | collective-permute-done | bytes 800 | tf_op jit(solution)/shard_map/ppermute | solution.py:35
  (31 shorter events, 3.8 us)
Async XLA Ops:
  0.0 1.0 %copy-start = (bf16[192,1024]{1,0:T(8,128)(2,1)S(1)}, bf16[192,1024]{1,0:T(8,128)(2,1)}, u32[]{:S(2)}) copy-start(bf16[192,1024]{1,0:T(8,128)(2,1)} %rows_ref.1) | copy-start | bytes 1179652
  1.2 7.9 %collective-permute-start = (bf16[192,1024]{1,0:T(8,128)(2,1)S(1)}, bf16[192,1024]{1,0:T(8,128)(2,1)S(1)}, u32[]{:S(2)}, u32[]{:S(2)}) collective-permute-start(bf16[192,1024]{1,0:T(8,128)(2,1)S(1)} %normalize.1.refs_0_.refs_8_), channel_id=1, source_target_pairs={{0,1},{1,0},{2,3},{3,2},{4,5},{5,4},{6,7},{7,6},{8,9},{9,8},{10,11... | collective-permute-start | bytes 1179656 | tf_op jit(solution)/shard_map/ppermute | solution.py:35
  4.5 8.7 %collective-permute-start.8 = (bf16[192,1024]{1,0:T(8,128)(2,1)S(1)}, bf16[192,1024]{1,0:T(8,128)(2,1)S(1)}, u32[]{:S(2)}, u32[]{:S(2)}) collective-permute-start(bf16[192,1024]{1,0:T(8,128)(2,1)S(1)} %normalize.1.refs_0_.refs_8_), channel_id=1, source_target_pairs={{0,2},{1,15},{2,4},{3,1},{4,6},{5,3},{6,8},{7,5},{8,10},{9,7},{10,... | collective-permute-start | bytes 1179656 | tf_op jit(solution)/shard_map/ppermute | solution.py:35
  9.0 7.5 %collective-permute-start.1 = (bf16[192,1024]{1,0:T(8,128)(2,1)S(1)}, bf16[192,1024]{1,0:T(8,128)(2,1)S(1)}, u32[]{:S(2)}, u32[]{:S(2)}) collective-permute-start(bf16[192,1024]{1,0:T(8,128)(2,1)S(1)} %normalize.1.refs_0_.refs_8_), channel_id=1, source_target_pairs={{0,16},{1,49},{2,18},{3,51},{4,20},{5,53},{6,22},{7,55},{8,24},{9,... | collective-permute-start | bytes 1179656 | tf_op jit(solution)/shard_map/ppermute | solution.py:35
  11.8 8.1 %collective-permute-start.5 = (bf16[192,1024]{1,0:T(8,128)(2,1)S(1)}, bf16[192,1024]{1,0:T(8,128)(2,1)S(1)}, u32[]{:S(2)}, u32[]{:S(2)}) collective-permute-start(bf16[192,1024]{1,0:T(8,128)(2,1)S(1)} %collective-permute-done.refs_4_), channel_id=1, source_target_pairs={{0,2},{1,15},{2,4},{3,1},{4,6},{5,3},{6,8},{7,5},{8,10},{9,7},{10,... | collective-permute-start | bytes 1179656 | tf_op jit(solution)/shard_map/ppermute | solution.py:35
  12.6 8.3 %collective-permute-start.2 = (bf16[192,1024]{1,0:T(8,128)(2,1)S(1)}, bf16[192,1024]{1,0:T(8,128)(2,1)S(1)}, u32[]{:S(2)}, u32[]{:S(2)}) collective-permute-start(bf16[192,1024]{1,0:T(8,128)(2,1)S(1)} %collective-permute-done.refs_4_), channel_id=1, source_target_pairs={{0,16},{1,49},{2,18},{3,51},{4,20},{5,53},{6,22},{7,55},{8,24},{9,... | collective-permute-start | bytes 1179656 | tf_op jit(solution)/shard_map/ppermute | solution.py:35
  13.2 9.8 %collective-permute-start.9 = (bf16[192,1024]{1,0:T(8,128)(2,1)S(1)}, bf16[192,1024]{1,0:T(8,128)(2,1)S(1)}, u32[]{:S(2)}, u32[]{:S(2)}) collective-permute-start(bf16[192,1024]{1,0:T(8,128)(2,1)S(1)} %collective-permute-done.8.refs_9_), channel_id=1, source_target_pairs={{0,2},{1,15},{2,4},{3,1},{4,6},{5,3},{6,8},{7,5},{8,10},{9,7},{10,... | collective-permute-start | bytes 1179656 | tf_op jit(solution)/shard_map/ppermute | solution.py:35
  16.6 8.4 %collective-permute-start.4 = (bf16[192,1024]{1,0:T(8,128)(2,1)S(1)}, bf16[192,1024]{1,0:T(8,128)(2,1)S(1)}, u32[]{:S(2)}, u32[]{:S(2)}) collective-permute-start(bf16[192,1024]{1,0:T(8,128)(2,1)S(1)} %collective-permute-done.1.refs_1_), channel_id=1, source_target_pairs={{0,16},{1,49},{2,18},{3,51},{4,20},{5,53},{6,22},{7,55},{8,24},{9,... | collective-permute-start | bytes 1179656 | tf_op jit(solution)/shard_map/ppermute | solution.py:35
  20.0 7.2 %collective-permute-start.10 = (bf16[192,1024]{1,0:T(8,128)(2,1)S(1)}, bf16[192,1024]{1,0:T(8,128)(2,1)S(1)}, u32[]{:S(2)}, u32[]{:S(2)}) collective-permute-start(bf16[192,1024]{1,0:T(8,128)(2,1)S(1)} %collective-permute-done.5.refs_10_), channel_id=1, source_target_pairs={{0,2},{1,15},{2,4},{3,1},{4,6},{5,3},{6,8},{7,5},{8,10},{9,7},{10,... | collective-permute-start | bytes 1179656 | tf_op jit(solution)/shard_map/ppermute | solution.py:35
  20.8 12.3 %collective-permute-start.6 = (bf16[192,1024]{1,0:T(8,128)(2,1)S(1)}, bf16[192,1024]{1,0:T(8,128)(2,1)S(1)}, u32[]{:S(2)}, u32[]{:S(2)}) collective-permute-start(bf16[192,1024]{1,0:T(8,128)(2,1)S(1)} %collective-permute-done.1.refs_1_), channel_id=1, source_target_pairs={{0,1},{1,0},{2,3},{3,2},{4,5},{5,4},{6,7},{7,6},{8,9},{9,8},{10,11... | collective-permute-start | bytes 1179656 | tf_op jit(solution)/shard_map/ppermute | solution.py:35
  20.9 12.2 %collective-permute-start.3 = (bf16[192,1024]{1,0:T(8,128)(2,1)S(1)}, bf16[192,1024]{1,0:T(8,128)(2,1)S(1)}, u32[]{:S(2)}, u32[]{:S(2)}) collective-permute-start(bf16[192,1024]{1,0:T(8,128)(2,1)S(1)} %collective-permute-done.2.refs_6_), channel_id=1, source_target_pairs={{0,1},{1,0},{2,3},{3,2},{4,5},{5,4},{6,7},{7,6},{8,9},{9,8},{10,11... | collective-permute-start | bytes 1179656 | tf_op jit(solution)/shard_map/ppermute | solution.py:35
  23.0 8.4 %collective-permute-start.11 = (bf16[192,1024]{1,0:T(8,128)(2,1)S(1)}, bf16[192,1024]{1,0:T(8,128)(2,1)S(1)}, u32[]{:S(2)}, u32[]{:S(2)}) collective-permute-start(bf16[192,1024]{1,0:T(8,128)(2,1)S(1)} %collective-permute-done.9.refs_0_), channel_id=1, source_target_pairs={{0,2},{1,15},{2,4},{3,1},{4,6},{5,3},{6,8},{7,5},{8,10},{9,7},{10,... | collective-permute-start | bytes 1179656 | tf_op jit(solution)/shard_map/ppermute | solution.py:35
  25.0 8.1 %collective-permute-start.7 = (bf16[192,1024]{1,0:T(8,128)(2,1)S(1)}, bf16[192,1024]{1,0:T(8,128)(2,1)S(1)}, u32[]{:S(2)}, u32[]{:S(2)}) collective-permute-start(bf16[192,1024]{1,0:T(8,128)(2,1)S(1)} %collective-permute-done.4.refs_3_), channel_id=1, source_target_pairs={{0,1},{1,0},{2,3},{3,2},{4,5},{5,4},{6,7},{7,6},{8,9},{9,8},{10,11... | collective-permute-start | bytes 1179656 | tf_op jit(solution)/shard_map/ppermute | solution.py:35
  27.2 9.7 %collective-permute-start.12 = (bf16[192,1024]{1,0:T(8,128)(2,1)S(1)}, bf16[192,1024]{1,0:T(8,128)(2,1)S(1)}, u32[]{:S(2)}, u32[]{:S(2)}) collective-permute-start(bf16[192,1024]{1,0:T(8,128)(2,1)S(1)} %collective-permute-done.10.refs_1_), channel_id=1, source_target_pairs={{0,2},{1,15},{2,4},{3,1},{4,6},{5,3},{6,8},{7,5},{8,10},{9,7},{10,... | collective-permute-start | bytes 1179656 | tf_op jit(solution)/shard_map/ppermute | solution.py:35
  31.4 8.4 %collective-permute-start.13 = (bf16[192,1024]{1,0:T(8,128)(2,1)S(1)}, bf16[192,1024]{1,0:T(8,128)(2,1)S(1)}, u32[]{:S(2)}, u32[]{:S(2)}) collective-permute-start(bf16[192,1024]{1,0:T(8,128)(2,1)S(1)} %collective-permute-done.11.refs_0_), channel_id=1, source_target_pairs={{0,2},{1,15},{2,4},{3,1},{4,6},{5,3},{6,8},{7,5},{8,10},{9,7},{10,... | collective-permute-start | bytes 1179656 | tf_op jit(solution)/shard_map/ppermute | solution.py:35
  40.5 2.5 %collective-permute-start.14 = (f32[1,768]{1,0:T(1,128)S(1)}, f32[1,768]{1,0:T(1,128)S(1)}, u32[]{:S(2)}, u32[]{:S(2)}) collective-permute-start(f32[1,768]{1,0:T(1,128)S(1)} %last.3), channel_id=1, source_target_pairs={{0,1},{1,0},{2,3},{3,2},{4,5},{5,4},{6,7},{7,6},{8,9},{9,8},{10,11... | collective-permute-start | bytes 9224 | tf_op jit(solution)/shard_map/ppermute | solution.py:35
  43.1 4.4 %collective-permute-start.15 = (f32[192]{0:T(256)S(1)}, f32[192]{0:T(256)S(1)}, u32[]{:S(2)}, u32[]{:S(2)}) collective-permute-start(f32[192]{0:T(256)S(1)} %bitcast.9), channel_id=1, source_target_pairs={{0,32},{1,33},{2,34},{3,35},{4,36},{5,37},{6,38},{7,39},{8,40},{9,... | collective-permute-start | bytes 2312 | tf_op jit(solution)/shard_map/ppermute | solution.py:35
  46.0 2.4 %collective-permute-start.16 = (f32[192]{0:T(256)S(1)}, f32[192]{0:T(256)S(1)}, u32[]{:S(2)}, u32[]{:S(2)}) collective-permute-start(f32[192]{0:T(256)S(1)} %bitcast.8), channel_id=1, source_target_pairs={{0,16},{1,49},{2,18},{3,51},{4,20},{5,53},{6,22},{7,55},{8,24},{9,... | collective-permute-start | bytes 2312 | tf_op jit(solution)/shard_map/ppermute | solution.py:35
  46.8 3.6 %collective-permute-start.17 = (f32[192]{0:T(256)S(1)}, f32[192]{0:T(256)S(1)}, u32[]{:S(2)}, u32[]{:S(2)}) collective-permute-start(f32[192]{0:T(256)S(1)} %bitcast.7), channel_id=1, source_target_pairs={{0,48},{1,17},{2,50},{3,19},{4,52},{5,21},{6,54},{7,23},{8,56},{9,... | collective-permute-start | bytes 2312 | tf_op jit(solution)/shard_map/ppermute | solution.py:35

commit v6 on v5

--- a/solution.py
+++ b/solution.py
@@ -187,7 +187,7 @@
     near_other = along_y(partner, 1)
     far = along_y(near, 1)
     mine = [unit, near, swap(near_other), far]
-    theirs = [partner, swap(after(near, other[1])), near_other, swap(far)]
+    theirs = [partner, swap(near), near_other, swap(far)]
 
     right, best = match(first_kernel, (0, 1, 2), [low, high, *mine, *theirs, unit, own[1], other[1]])
     best = match(match_kernel, (3, 4), [low, best, right, own[2], other[2]])

time: 51.1 us -> 51.1 us (level)
  no operation moved by 1% of the time
where the time goes in v6:
time: 51.1 us; the launch traced here: 51 us
  starting transfers between devices  30.6 us (60%)
  waiting for transfers between devices  11.1 us (22%)
  Pallas kernels  6.75 us (13%)
  local copies, waits for them, and re-layouts  1.07 us (2%)
  between operations  0.79 us (2%)
  other arithmetic  0.71 us (1%)
    ppermute x18, starting transfers between devices, permute(): return lax.ppermute(value, 'member', pairs)  30.6 us
    ppermute x18, waiting for transfers between devices, permute(): return lax.ppermute(value, 'member', pairs)  11.1 us
    pallas_call x6, Pallas kernels, local(): pl.pallas_call(kernel, out_shape=out_shape, in_specs=[VMEM] * len(operand...  6.75 us
  transfers between devices with their start and end apart: 18, of which 9 were waited for; matrix products, arithmetic and copies ran while one was open for 0% of the time, Pallas kernels for 12%

profile of v6, /device:TPU:1, one launch (start us, length us, event | category | flops | bytes accessed | tf_op | source)
XLA Modules:
  0.0 51.0 jit_solution(7560300268147926073)
XLA Ops:
  0.0 1.0 %copy-done = bf16[192,1024]{1,0:T(8,128)(2,1)S(1)} copy-done((bf16[192,1024]{1,0:T(8,128)(2,1)S(1)}, bf16[192,1024]{1,0:T(8,128)(2,1)}, u32[]{:S(2)}) %copy-start) | copy-done | bytes 393240
  1.2 3.3 %collective-permute-start = (bf16[192,1024]{1,0:T(8,128)(2,1)S(1)}, bf16[192,1024]{1,0:T(8,128)(2,1)S(1)}, u32[]{:S(2)}, u32[]{:S(2)}) collective-permute-start(bf16[192,1024]{1,0:T(8,128)(2,1)S(1)} %normalize.1.refs_0_.refs_8_), channel_id=1, source_target_pairs={{0,1},{1,0},{2,3},{3,2},{4,5},{5,4},{6,7},{7,6},{8,9},{9,8},{10,11... | collective-permute-start | bytes 1179656 | tf_op jit(solution)/shard_map/ppermute | solution.py:35
  4.5 3.8 %collective-permute-start.7 = (bf16[192,1024]{1,0:T(8,128)(2,1)S(1)}, bf16[192,1024]{1,0:T(8,128)(2,1)S(1)}, u32[]{:S(2)}, u32[]{:S(2)}) collective-permute-start(bf16[192,1024]{1,0:T(8,128)(2,1)S(1)} %normalize.1.refs_0_.refs_8_), channel_id=1, source_target_pairs={{0,2},{1,15},{2,4},{3,1},{4,6},{5,3},{6,8},{7,5},{8,10},{9,7},{10,... | collective-permute-start | bytes 1179656 | tf_op jit(solution)/shard_map/ppermute | solution.py:35
  9.0 2.8 %collective-permute-start.1 = (bf16[192,1024]{1,0:T(8,128)(2,1)S(1)}, bf16[192,1024]{1,0:T(8,128)(2,1)S(1)}, u32[]{:S(2)}, u32[]{:S(2)}) collective-permute-start(bf16[192,1024]{1,0:T(8,128)(2,1)S(1)} %normalize.1.refs_0_.refs_8_), channel_id=1, source_target_pairs={{0,16},{1,49},{2,18},{3,51},{4,20},{5,53},{6,22},{7,55},{8,24},{9,... | collective-permute-start | bytes 1179656 | tf_op jit(solution)/shard_map/ppermute | solution.py:35
  11.8 0.7 %collective-permute-start.8 = (bf16[192,1024]{1,0:T(8,128)(2,1)S(1)}, bf16[192,1024]{1,0:T(8,128)(2,1)S(1)}, u32[]{:S(2)}, u32[]{:S(2)}) collective-permute-start(bf16[192,1024]{1,0:T(8,128)(2,1)S(1)} %collective-permute-done.refs_4_), channel_id=1, source_target_pairs={{0,2},{1,15},{2,4},{3,1},{4,6},{5,3},{6,8},{7,5},{8,10},{9,7},{10,... | collective-permute-start | bytes 1179656 | tf_op jit(solution)/shard_map/ppermute | solution.py:35
  13.2 3.3 %collective-permute-start.9 = (bf16[192,1024]{1,0:T(8,128)(2,1)S(1)}, bf16[192,1024]{1,0:T(8,128)(2,1)S(1)}, u32[]{:S(2)}, u32[]{:S(2)}) collective-permute-start(bf16[192,1024]{1,0:T(8,128)(2,1)S(1)} %collective-permute-done.7.refs_9_), channel_id=1, source_target_pairs={{0,2},{1,15},{2,4},{3,1},{4,6},{5,3},{6,8},{7,5},{8,10},{9,7},{10,... | collective-permute-start | bytes 1179656 | tf_op jit(solution)/shard_map/ppermute | solution.py:35
  16.6 3.4 %collective-permute-start.4 = (bf16[192,1024]{1,0:T(8,128)(2,1)S(1)}, bf16[192,1024]{1,0:T(8,128)(2,1)S(1)}, u32[]{:S(2)}, u32[]{:S(2)}) collective-permute-start(bf16[192,1024]{1,0:T(8,128)(2,1)S(1)} %collective-permute-done.1.refs_1_), channel_id=1, source_target_pairs={{0,16},{1,49},{2,18},{3,51},{4,20},{5,53},{6,22},{7,55},{8,24},{9,... | collective-permute-start | bytes 1179656 | tf_op jit(solution)/shard_map/ppermute | solution.py:35
  20.0 0.7 %collective-permute-start.10 = (bf16[192,1024]{1,0:T(8,128)(2,1)S(1)}, bf16[192,1024]{1,0:T(8,128)(2,1)S(1)}, u32[]{:S(2)}, u32[]{:S(2)}) collective-permute-start(bf16[192,1024]{1,0:T(8,128)(2,1)S(1)} %collective-permute-done.8.refs_10_), channel_id=1, source_target_pairs={{0,2},{1,15},{2,4},{3,1},{4,6},{5,3},{6,8},{7,5},{8,10},{9,7},{10,... | collective-permute-start | bytes 1179656 | tf_op jit(solution)/shard_map/ppermute | solution.py:35
  21.4 1.6 %collective-permute-done.9.refs_0_ = bf16[192,1024]{1,0:T(8,128)(2,1)S(1)} collective-permute-done((bf16[192,1024]{1,0:T(8,128)(2,1)S(1)}, bf16[192,1024]{1,0:T(8,128)(2,1)S(1)}, u32[]{:S(2)}, u32[]{:S(2)}) %collective-permute-start.9) | collective-permute-done | bytes 393248 | tf_op jit(solution)/shard_map/ppermute | solution.py:35
  23.0 1.9 %collective-permute-start.11 = (bf16[192,1024]{1,0:T(8,128)(2,1)S(1)}, bf16[192,1024]{1,0:T(8,128)(2,1)S(1)}, u32[]{:S(2)}, u32[]{:S(2)}) collective-permute-start(bf16[192,1024]{1,0:T(8,128)(2,1)S(1)} %collective-permute-done.9.refs_0_), channel_id=1, source_target_pairs={{0,2},{1,15},{2,4},{3,1},{4,6},{5,3},{6,8},{7,5},{8,10},{9,7},{10,... | collective-permute-start | bytes 1179656 | tf_op jit(solution)/shard_map/ppermute | solution.py:35
  25.0 2.2 %collective-permute-done.10.refs_1_ = bf16[192,1024]{1,0:T(8,128)(2,1)S(1)} collective-permute-done((bf16[192,1024]{1,0:T(8,128)(2,1)S(1)}, bf16[192,1024]{1,0:T(8,128)(2,1)S(1)}, u32[]{:S(2)}, u32[]{:S(2)}) %collective-permute-start.10) | collective-permute-done | bytes 393248 | tf_op jit(solution)/shard_map/ppermute | solution.py:35
  27.2 1.6 %collective-permute-start.12 = (bf16[192,1024]{1,0:T(8,128)(2,1)S(1)}, bf16[192,1024]{1,0:T(8,128)(2,1)S(1)}, u32[]{:S(2)}, u32[]{:S(2)}) collective-permute-start(bf16[192,1024]{1,0:T(8,128)(2,1)S(1)} %collective-permute-done.10.refs_1_), channel_id=1, source_target_pairs={{0,2},{1,15},{2,4},{3,1},{4,6},{5,3},{6,8},{7,5},{8,10},{9,7},{10,... | collective-permute-start | bytes 1179656 | tf_op jit(solution)/shard_map/ppermute | solution.py:35
  28.9 2.6 %collective-permute-done.11.refs_0_ = bf16[192,1024]{1,0:T(8,128)(2,1)S(1)} collective-permute-done((bf16[192,1024]{1,0:T(8,128)(2,1)S(1)}, bf16[192,1024]{1,0:T(8,128)(2,1)S(1)}, u32[]{:S(2)}, u32[]{:S(2)}) %collective-permute-start.11) | collective-permute-done | bytes 393248 | tf_op jit(solution)/shard_map/ppermute | solution.py:35
  31.4 1.6 %collective-permute-start.13 = (bf16[192,1024]{1,0:T(8,128)(2,1)S(1)}, bf16[192,1024]{1,0:T(8,128)(2,1)S(1)}, u32[]{:S(2)}, u32[]{:S(2)}) collective-permute-start(bf16[192,1024]{1,0:T(8,128)(2,1)S(1)} %collective-permute-done.11.refs_0_), channel_id=1, source_target_pairs={{0,2},{1,15},{2,4},{3,1},{4,6},{5,3},{6,8},{7,5},{8,10},{9,7},{10,... | collective-permute-start | bytes 1179656 | tf_op jit(solution)/shard_map/ppermute | solution.py:35
  33.1 2.3 %match.3 = (bf16[1536,1024]{1,0:T(8,128)(2,1)S(1)}, f32[8,1536]{1,0:T(8,128)S(1)}) custom-call(s32[8,1536]{1,0:T(8,128)S(1)} %get-tuple-element.12.low_ref, s32[1,1536]{1,0:T(1,128)S(1)} %fusion.high_ref, bf16[192,1024]{1,0:T(8,128)(2,1)S(1)} %normalize.1.refs_0_.refs_8_, bf16[192,1024]{1,0:T(8,128)(2,1)S(1)} %collective-permute-done.1.refs_1_, ...), custom_call_target="tpu_custom_call" | custom-call | flops 1811939328 | bytes 7575552 | tf_op jit(solution)/shard_map/match/pallas_call | solution.py:56
  35.4 1.5 %match.4.best_ref = f32[8,1536]{1,0:T(8,128)S(1)} custom-call(s32[8,1536]{1,0:T(8,128)S(1)} %get-tuple-element.12.low_ref, f32[8,1536]{1,0:T(8,128)S(1)} %get-tuple-element.9.best_ref, bf16[1536,1024]{1,0:T(8,128)(2,1)S(1)} %get-tuple-element.10.right_ref, bf16[192,1024]{1,0:T(8,128)(2,1)S(1)} %collective-permute-done.9.refs_0_, ...), custom_call_target="tpu_custom_call" | custom-call | flops 1207959552 | bytes 4079616 | tf_op jit(solution)/shard_map/match/pallas_call | solution.py:56
  36.9 1.5 %match.5.best_ref = f32[8,1536]{1,0:T(8,128)S(1)} custom-call(s32[8,1536]{1,0:T(8,128)S(1)} %get-tuple-element.12.low_ref, f32[8,1536]{1,0:T(8,128)S(1)} %match.4.best_ref, bf16[1536,1024]{1,0:T(8,128)(2,1)S(1)} %get-tuple-element.10.right_ref, bf16[192,1024]{1,0:T(8,128)(2,1)S(1)} %collective-permute-done.11.refs_0_, ...), custom_call_target="tpu_custom_call" | custom-call | flops 1207959552 | bytes 4079616 | tf_op jit(solution)/shard_map/match/pallas_call | solution.py:56
  38.3 1.5 %collective-permute-done.13.piece_ref = bf16[192,1024]{1,0:T(8,128)(2,1)S(1)} collective-permute-done((bf16[192,1024]{1,0:T(8,128)(2,1)S(1)}, bf16[192,1024]{1,0:T(8,128)(2,1)S(1)}, u32[]{:S(2)}, u32[]{:S(2)}) %collective-permute-start.13) | collective-permute-done | bytes 393248 | tf_op jit(solution)/shard_map/ppermute | solution.py:35
  40.5 1.7 %collective-permute-start.14 = (f32[1,768]{1,0:T(1,128)S(1)}, f32[1,768]{1,0:T(1,128)S(1)}, u32[]{:S(2)}, u32[]{:S(2)}) collective-permute-start(f32[1,768]{1,0:T(1,128)S(1)} %last.3), channel_id=1, source_target_pairs={{0,1},{1,0},{2,3},{3,2},{4,5},{5,4},{6,7},{7,6},{8,9},{9,8},{10,11... | collective-permute-start | bytes 9224 | tf_op jit(solution)/shard_map/ppermute | solution.py:35
  43.1 2.9 %collective-permute-start.15 = (f32[192]{0:T(256)S(1)}, f32[192]{0:T(256)S(1)}, u32[]{:S(2)}, u32[]{:S(2)}) collective-permute-start(f32[192]{0:T(256)S(1)} %bitcast.9), channel_id=1, source_target_pairs={{0,32},{1,33},{2,34},{3,35},{4,36},{5,37},{6,38},{7,39},{8,40},{9,... | collective-permute-start | bytes 2312 | tf_op jit(solution)/shard_map/ppermute | solution.py:35
  46.0 0.8 %collective-permute-start.16 = (f32[192]{0:T(256)S(1)}, f32[192]{0:T(256)S(1)}, u32[]{:S(2)}, u32[]{:S(2)}) collective-permute-start(f32[192]{0:T(256)S(1)} %bitcast.8), channel_id=1, source_target_pairs={{0,16},{1,49},{2,18},{3,51},{4,20},{5,53},{6,22},{7,55},{8,24},{9,... | collective-permute-start | bytes 2312 | tf_op jit(solution)/shard_map/ppermute | solution.py:35
  46.8 0.7 %collective-permute-start.17 = (f32[192]{0:T(256)S(1)}, f32[192]{0:T(256)S(1)}, u32[]{:S(2)}, u32[]{:S(2)}) collective-permute-start(f32[192]{0:T(256)S(1)} %bitcast.7), channel_id=1, source_target_pairs={{0,48},{1,17},{2,50},{3,19},{4,52},{5,21},{6,54},{7,23},{8,56},{9,... | collective-permute-start | bytes 2312 | tf_op jit(solution)/shard_map/ppermute | solution.py:35
  47.5 0.9 %collective-permute-done.16 = f32[192]{0:T(256)S(1)} collective-permute-done((f32[192]{0:T(256)S(1)}, f32[192]{0:T(256)S(1)}, u32[]{:S(2)}, u32[]{:S(2)}) %collective-permute-start.16) | collective-permute-done | bytes 800 | tf_op jit(solution)/shard_map/ppermute | solution.py:35
  48.5 2.0 %collective-permute-done.17 = f32[192]{0:T(256)S(1)} collective-permute-done((f32[192]{0:T(256)S(1)}, f32[192]{0:T(256)S(1)}, u32[]{:S(2)}, u32[]{:S(2)}) %collective-permute-start.17) | collective-permute-done | bytes 800 | tf_op jit(solution)/shard_map/ppermute | solution.py:35
  (31 shorter events, 3.8 us)
Async XLA Ops:
  0.0 1.0 %copy-start = (bf16[192,1024]{1,0:T(8,128)(2,1)S(1)}, bf16[192,1024]{1,0:T(8,128)(2,1)}, u32[]{:S(2)}) copy-start(bf16[192,1024]{1,0:T(8,128)(2,1)} %rows_ref.1) | copy-start | bytes 1179652
  1.2 7.9 %collective-permute-start = (bf16[192,1024]{1,0:T(8,128)(2,1)S(1)}, bf16[192,1024]{1,0:T(8,128)(2,1)S(1)}, u32[]{:S(2)}, u32[]{:S(2)}) collective-permute-start(bf16[192,1024]{1,0:T(8,128)(2,1)S(1)} %normalize.1.refs_0_.refs_8_), channel_id=1, source_target_pairs={{0,1},{1,0},{2,3},{3,2},{4,5},{5,4},{6,7},{7,6},{8,9},{9,8},{10,11... | collective-permute-start | bytes 1179656 | tf_op jit(solution)/shard_map/ppermute | solution.py:35
  4.5 8.7 %collective-permute-start.7 = (bf16[192,1024]{1,0:T(8,128)(2,1)S(1)}, bf16[192,1024]{1,0:T(8,128)(2,1)S(1)}, u32[]{:S(2)}, u32[]{:S(2)}) collective-permute-start(bf16[192,1024]{1,0:T(8,128)(2,1)S(1)} %normalize.1.refs_0_.refs_8_), channel_id=1, source_target_pairs={{0,2},{1,15},{2,4},{3,1},{4,6},{5,3},{6,8},{7,5},{8,10},{9,7},{10,... | collective-permute-start | bytes 1179656 | tf_op jit(solution)/shard_map/ppermute | solution.py:35
  9.0 7.5 %collective-permute-start.1 = (bf16[192,1024]{1,0:T(8,128)(2,1)S(1)}, bf16[192,1024]{1,0:T(8,128)(2,1)S(1)}, u32[]{:S(2)}, u32[]{:S(2)}) collective-permute-start(bf16[192,1024]{1,0:T(8,128)(2,1)S(1)} %normalize.1.refs_0_.refs_8_), channel_id=1, source_target_pairs={{0,16},{1,49},{2,18},{3,51},{4,20},{5,53},{6,22},{7,55},{8,24},{9,... | collective-permute-start | bytes 1179656 | tf_op jit(solution)/shard_map/ppermute | solution.py:35
  11.8 8.1 %collective-permute-start.8 = (bf16[192,1024]{1,0:T(8,128)(2,1)S(1)}, bf16[192,1024]{1,0:T(8,128)(2,1)S(1)}, u32[]{:S(2)}, u32[]{:S(2)}) collective-permute-start(bf16[192,1024]{1,0:T(8,128)(2,1)S(1)} %collective-permute-done.refs_4_), channel_id=1, source_target_pairs={{0,2},{1,15},{2,4},{3,1},{4,6},{5,3},{6,8},{7,5},{8,10},{9,7},{10,... | collective-permute-start | bytes 1179656 | tf_op jit(solution)/shard_map/ppermute | solution.py:35
  12.6 8.3 %collective-permute-start.2 = (bf16[192,1024]{1,0:T(8,128)(2,1)S(1)}, bf16[192,1024]{1,0:T(8,128)(2,1)S(1)}, u32[]{:S(2)}, u32[]{:S(2)}) collective-permute-start(bf16[192,1024]{1,0:T(8,128)(2,1)S(1)} %collective-permute-done.refs_4_), channel_id=1, source_target_pairs={{0,16},{1,49},{2,18},{3,51},{4,20},{5,53},{6,22},{7,55},{8,24},{9,... | collective-permute-start | bytes 1179656 | tf_op jit(solution)/shard_map/ppermute | solution.py:35
  13.2 9.8 %collective-permute-start.9 = (bf16[192,1024]{1,0:T(8,128)(2,1)S(1)}, bf16[192,1024]{1,0:T(8,128)(2,1)S(1)}, u32[]{:S(2)}, u32[]{:S(2)}) collective-permute-start(bf16[192,1024]{1,0:T(8,128)(2,1)S(1)} %collective-permute-done.7.refs_9_), channel_id=1, source_target_pairs={{0,2},{1,15},{2,4},{3,1},{4,6},{5,3},{6,8},{7,5},{8,10},{9,7},{10,... | collective-permute-start | bytes 1179656 | tf_op jit(solution)/shard_map/ppermute | solution.py:35
  16.6 8.4 %collective-permute-start.4 = (bf16[192,1024]{1,0:T(8,128)(2,1)S(1)}, bf16[192,1024]{1,0:T(8,128)(2,1)S(1)}, u32[]{:S(2)}, u32[]{:S(2)}) collective-permute-start(bf16[192,1024]{1,0:T(8,128)(2,1)S(1)} %collective-permute-done.1.refs_1_), channel_id=1, source_target_pairs={{0,16},{1,49},{2,18},{3,51},{4,20},{5,53},{6,22},{7,55},{8,24},{9,... | collective-permute-start | bytes 1179656 | tf_op jit(solution)/shard_map/ppermute | solution.py:35
  20.0 7.2 %collective-permute-start.10 = (bf16[192,1024]{1,0:T(8,128)(2,1)S(1)}, bf16[192,1024]{1,0:T(8,128)(2,1)S(1)}, u32[]{:S(2)}, u32[]{:S(2)}) collective-permute-start(bf16[192,1024]{1,0:T(8,128)(2,1)S(1)} %collective-permute-done.8.refs_10_), channel_id=1, source_target_pairs={{0,2},{1,15},{2,4},{3,1},{4,6},{5,3},{6,8},{7,5},{8,10},{9,7},{10,... | collective-permute-start | bytes 1179656 | tf_op jit(solution)/shard_map/ppermute | solution.py:35
  20.8 12.3 %collective-permute-start.5 = (bf16[192,1024]{1,0:T(8,128)(2,1)S(1)}, bf16[192,1024]{1,0:T(8,128)(2,1)S(1)}, u32[]{:S(2)}, u32[]{:S(2)}) collective-permute-start(bf16[192,1024]{1,0:T(8,128)(2,1)S(1)} %collective-permute-done.1.refs_1_), channel_id=1, source_target_pairs={{0,1},{1,0},{2,3},{3,2},{4,5},{5,4},{6,7},{7,6},{8,9},{9,8},{10,11... | collective-permute-start | bytes 1179656 | tf_op jit(solution)/shard_map/ppermute | solution.py:35
  20.9 12.2 %collective-permute-start.3 = (bf16[192,1024]{1,0:T(8,128)(2,1)S(1)}, bf16[192,1024]{1,0:T(8,128)(2,1)S(1)}, u32[]{:S(2)}, u32[]{:S(2)}) collective-permute-start(bf16[192,1024]{1,0:T(8,128)(2,1)S(1)} %collective-permute-done.2.refs_6_), channel_id=1, source_target_pairs={{0,1},{1,0},{2,3},{3,2},{4,5},{5,4},{6,7},{7,6},{8,9},{9,8},{10,11... | collective-permute-start | bytes 1179656 | tf_op jit(solution)/shard_map/ppermute | solution.py:35
  23.0 8.4 %collective-permute-start.11 = (bf16[192,1024]{1,0:T(8,128)(2,1)S(1)}, bf16[192,1024]{1,0:T(8,128)(2,1)S(1)}, u32[]{:S(2)}, u32[]{:S(2)}) collective-permute-start(bf16[192,1024]{1,0:T(8,128)(2,1)S(1)} %collective-permute-done.9.refs_0_), channel_id=1, source_target_pairs={{0,2},{1,15},{2,4},{3,1},{4,6},{5,3},{6,8},{7,5},{8,10},{9,7},{10,... | collective-permute-start | bytes 1179656 | tf_op jit(solution)/shard_map/ppermute | solution.py:35
  25.0 8.1 %collective-permute-start.6 = (bf16[192,1024]{1,0:T(8,128)(2,1)S(1)}, bf16[192,1024]{1,0:T(8,128)(2,1)S(1)}, u32[]{:S(2)}, u32[]{:S(2)}) collective-permute-start(bf16[192,1024]{1,0:T(8,128)(2,1)S(1)} %collective-permute-done.4.refs_3_), channel_id=1, source_target_pairs={{0,1},{1,0},{2,3},{3,2},{4,5},{5,4},{6,7},{7,6},{8,9},{9,8},{10,11... | collective-permute-start | bytes 1179656 | tf_op jit(solution)/shard_map/ppermute | solution.py:35
  27.2 9.7 %collective-permute-start.12 = (bf16[192,1024]{1,0:T(8,128)(2,1)S(1)}, bf16[192,1024]{1,0:T(8,128)(2,1)S(1)}, u32[]{:S(2)}, u32[]{:S(2)}) collective-permute-start(bf16[192,1024]{1,0:T(8,128)(2,1)S(1)} %collective-permute-done.10.refs_1_), channel_id=1, source_target_pairs={{0,2},{1,15},{2,4},{3,1},{4,6},{5,3},{6,8},{7,5},{8,10},{9,7},{10,... | collective-permute-start | bytes 1179656 | tf_op jit(solution)/shard_map/ppermute | solution.py:35
  31.4 8.4 %collective-permute-start.13 = (bf16[192,1024]{1,0:T(8,128)(2,1)S(1)}, bf16[192,1024]{1,0:T(8,128)(2,1)S(1)}, u32[]{:S(2)}, u32[]{:S(2)}) collective-permute-start(bf16[192,1024]{1,0:T(8,128)(2,1)S(1)} %collective-permute-done.11.refs_0_), channel_id=1, source_target_pairs={{0,2},{1,15},{2,4},{3,1},{4,6},{5,3},{6,8},{7,5},{8,10},{9,7},{10,... | collective-permute-start | bytes 1179656 | tf_op jit(solution)/shard_map/ppermute | solution.py:35
  40.5 2.5 %collective-permute-start.14 = (f32[1,768]{1,0:T(1,128)S(1)}, f32[1,768]{1,0:T(1,128)S(1)}, u32[]{:S(2)}, u32[]{:S(2)}) collective-permute-start(f32[1,768]{1,0:T(1,128)S(1)} %last.3), channel_id=1, source_target_pairs={{0,1},{1,0},{2,3},{3,2},{4,5},{5,4},{6,7},{7,6},{8,9},{9,8},{10,11... | collective-permute-start | bytes 9224 | tf_op jit(solution)/shard_map/ppermute | solution.py:35
  43.1 4.4 %collective-permute-start.15 = (f32[192]{0:T(256)S(1)}, f32[192]{0:T(256)S(1)}, u32[]{:S(2)}, u32[]{:S(2)}) collective-permute-start(f32[192]{0:T(256)S(1)} %bitcast.9), channel_id=1, source_target_pairs={{0,32},{1,33},{2,34},{3,35},{4,36},{5,37},{6,38},{7,39},{8,40},{9,... | collective-permute-start | bytes 2312 | tf_op jit(solution)/shard_map/ppermute | solution.py:35
  46.0 2.4 %collective-permute-start.16 = (f32[192]{0:T(256)S(1)}, f32[192]{0:T(256)S(1)}, u32[]{:S(2)}, u32[]{:S(2)}) collective-permute-start(f32[192]{0:T(256)S(1)} %bitcast.8), channel_id=1, source_target_pairs={{0,16},{1,49},{2,18},{3,51},{4,20},{5,53},{6,22},{7,55},{8,24},{9,... | collective-permute-start | bytes 2312 | tf_op jit(solution)/shard_map/ppermute | solution.py:35
  46.8 3.6 %collective-permute-start.17 = (f32[192]{0:T(256)S(1)}, f32[192]{0:T(256)S(1)}, u32[]{:S(2)}, u32[]{:S(2)}) collective-permute-start(f32[192]{0:T(256)S(1)} %bitcast.7), channel_id=1, source_target_pairs={{0,48},{1,17},{2,50},{3,19},{4,52},{5,21},{6,54},{7,23},{8,56},{9,... | collective-permute-start | bytes 2312 | tf_op jit(solution)/shard_map/ppermute | solution.py:35

commit v7 on v5

--- a/solution.py
+++ b/solution.py
@@ -183,7 +183,7 @@
         other.append(along_z(other[k]))
     own.append(along_z(own[3]))
 
-    near = along_y(after(unit, partner), 1)
+    near = along_y(unit, 1)
     near_other = along_y(partner, 1)
     far = along_y(near, 1)
     mine = [unit, near, swap(near_other), far]

time: 51.1 us -> 52.7 us (1.031)
  starting transfers between devices: 30.6 us -> 34.7 us
  waiting for transfers between devices: 11.1 us -> 8.56 us
    ppermute x18, starting transfers between devices: 30.6 us -> 34.7 us  [permute(): return lax.ppermute(value, 'member', pairs)]
    ppermute x18, waiting for transfers between devices: 11.1 us -> 8.56 us  [permute(): return lax.ppermute(value, 'member', pairs)]
  transfers between devices with their start and end apart: 18 -> 18, of which waited for: 9 -> 7; matrix products, arithmetic and copies ran while one was open for 0% -> 0% of each run, Pallas kernels for 12% -> 11%
where the time goes in v7:
time: 52.7 us; the launch traced here: 52.6 us
  starting transfers between devices  34.7 us (66%)
  waiting for transfers between devices  8.56 us (16%)
  Pallas kernels  6.76 us (13%)
  local copies, waits for them, and re-layouts  1.07 us (2%)
  between operations  0.79 us (1%)
  other arithmetic  0.71 us (1%)
    ppermute x18, starting transfers between devices, permute(): return lax.ppermute(value, 'member', pairs)  34.7 us
    ppermute x18, waiting for transfers between devices, permute(): return lax.ppermute(value, 'member', pairs)  8.56 us
    pallas_call x6, Pallas kernels, local(): pl.pallas_call(kernel, out_shape=out_shape, in_specs=[VMEM] * len(operand...  6.76 us
  transfers between devices with their start and end apart: 18, of which 7 were waited for; matrix products, arithmetic and copies ran while one was open for 0% of the time, Pallas kernels for 11%

profile of v7, /device:TPU:1, one launch (start us, length us, event | category | flops | bytes accessed | tf_op | source)
XLA Modules:
  0.0 52.6 jit_solution(2151957525790732239)
XLA Ops:
  0.0 1.0 %copy-done = bf16[192,1024]{1,0:T(8,128)(2,1)S(1)} copy-done((bf16[192,1024]{1,0:T(8,128)(2,1)S(1)}, bf16[192,1024]{1,0:T(8,128)(2,1)}, u32[]{:S(2)}) %copy-start) | copy-done | bytes 393240
  1.2 3.3 %collective-permute-start.1 = (bf16[192,1024]{1,0:T(8,128)(2,1)S(1)}, bf16[192,1024]{1,0:T(8,128)(2,1)S(1)}, u32[]{:S(2)}, u32[]{:S(2)}) collective-permute-start(bf16[192,1024]{1,0:T(8,128)(2,1)S(1)} %normalize.1.refs_0_.refs_8_), channel_id=1, source_target_pairs={{0,1},{1,0},{2,3},{3,2},{4,5},{5,4},{6,7},{7,6},{8,9},{9,8},{10,11... | collective-permute-start | bytes 1179656 | tf_op jit(solution)/shard_map/ppermute | solution.py:35
  4.5 1.0 %collective-permute-start = (bf16[192,1024]{1,0:T(8,128)(2,1)S(1)}, bf16[192,1024]{1,0:T(8,128)(2,1)S(1)}, u32[]{:S(2)}, u32[]{:S(2)}) collective-permute-start(bf16[192,1024]{1,0:T(8,128)(2,1)S(1)} %normalize.1.refs_0_.refs_8_), channel_id=1, source_target_pairs={{0,16},{1,49},{2,18},{3,51},{4,20},{5,53},{6,22},{7,55},{8,24},{9,... | collective-permute-start | bytes 1179656 | tf_op jit(solution)/shard_map/ppermute | solution.py:35
  5.5 5.6 %collective-permute-start.8 = (bf16[192,1024]{1,0:T(8,128)(2,1)S(1)}, bf16[192,1024]{1,0:T(8,128)(2,1)S(1)}, u32[]{:S(2)}, u32[]{:S(2)}) collective-permute-start(bf16[192,1024]{1,0:T(8,128)(2,1)S(1)} %normalize.1.refs_0_.refs_8_), channel_id=1, source_target_pairs={{0,2},{1,15},{2,4},{3,1},{4,6},{5,3},{6,8},{7,5},{8,10},{9,7},{10,... | collective-permute-start | bytes 1179656 | tf_op jit(solution)/shard_map/ppermute | solution.py:35
  11.8 0.8 %collective-permute-start.5 = (bf16[192,1024]{1,0:T(8,128)(2,1)S(1)}, bf16[192,1024]{1,0:T(8,128)(2,1)S(1)}, u32[]{:S(2)}, u32[]{:S(2)}) collective-permute-start(bf16[192,1024]{1,0:T(8,128)(2,1)S(1)} %collective-permute-done.1.refs_4_), channel_id=1, source_target_pairs={{0,2},{1,15},{2,4},{3,1},{4,6},{5,3},{6,8},{7,5},{8,10},{9,7},{10,... | collective-permute-start | bytes 1179656 | tf_op jit(solution)/shard_map/ppermute | solution.py:35
  13.6 2.2 %collective-permute-done.8.refs_9_ = bf16[192,1024]{1,0:T(8,128)(2,1)S(1)} collective-permute-done((bf16[192,1024]{1,0:T(8,128)(2,1)S(1)}, bf16[192,1024]{1,0:T(8,128)(2,1)S(1)}, u32[]{:S(2)}, u32[]{:S(2)}) %collective-permute-start.8) | collective-permute-done | bytes 393248 | tf_op jit(solution)/shard_map/ppermute | solution.py:35
  15.8 3.4 %collective-permute-start.9 = (bf16[192,1024]{1,0:T(8,128)(2,1)S(1)}, bf16[192,1024]{1,0:T(8,128)(2,1)S(1)}, u32[]{:S(2)}, u32[]{:S(2)}) collective-permute-start(bf16[192,1024]{1,0:T(8,128)(2,1)S(1)} %collective-permute-done.8.refs_9_), channel_id=1, source_target_pairs={{0,2},{1,15},{2,4},{3,1},{4,6},{5,3},{6,8},{7,5},{8,10},{9,7},{10,... | collective-permute-start | bytes 1179656 | tf_op jit(solution)/shard_map/ppermute | solution.py:35
  19.2 0.8 %collective-permute-done.5.refs_10_ = bf16[192,1024]{1,0:T(8,128)(2,1)S(1)} collective-permute-done((bf16[192,1024]{1,0:T(8,128)(2,1)S(1)}, bf16[192,1024]{1,0:T(8,128)(2,1)S(1)}, u32[]{:S(2)}, u32[]{:S(2)}) %collective-permute-start.5) | collective-permute-done | bytes 393248 | tf_op jit(solution)/shard_map/ppermute | solution.py:35
  20.0 3.4 %collective-permute-start.10 = (bf16[192,1024]{1,0:T(8,128)(2,1)S(1)}, bf16[192,1024]{1,0:T(8,128)(2,1)S(1)}, u32[]{:S(2)}, u32[]{:S(2)}) collective-permute-start(bf16[192,1024]{1,0:T(8,128)(2,1)S(1)} %collective-permute-done.5.refs_10_), channel_id=1, source_target_pairs={{0,2},{1,15},{2,4},{3,1},{4,6},{5,3},{6,8},{7,5},{8,10},{9,7},{10,... | collective-permute-start | bytes 1179656 | tf_op jit(solution)/shard_map/ppermute | solution.py:35
  24.2 3.1 %collective-permute-start.11 = (bf16[192,1024]{1,0:T(8,128)(2,1)S(1)}, bf16[192,1024]{1,0:T(8,128)(2,1)S(1)}, u32[]{:S(2)}, u32[]{:S(2)}) collective-permute-start(bf16[192,1024]{1,0:T(8,128)(2,1)S(1)} %collective-permute-done.9.refs_0_), channel_id=1, source_target_pairs={{0,2},{1,15},{2,4},{3,1},{4,6},{5,3},{6,8},{7,5},{8,10},{9,7},{10,... | collective-permute-start | bytes 1179656 | tf_op jit(solution)/shard_map/ppermute | solution.py:35
  27.3 1.1 %collective-permute-done.10.refs_1_ = bf16[192,1024]{1,0:T(8,128)(2,1)S(1)} collective-permute-done((bf16[192,1024]{1,0:T(8,128)(2,1)S(1)}, bf16[192,1024]{1,0:T(8,128)(2,1)S(1)}, u32[]{:S(2)}, u32[]{:S(2)}) %collective-permute-start.10) | collective-permute-done | bytes 393248 | tf_op jit(solution)/shard_map/ppermute | solution.py:35
  28.4 3.1 %collective-permute-start.12 = (bf16[192,1024]{1,0:T(8,128)(2,1)S(1)}, bf16[192,1024]{1,0:T(8,128)(2,1)S(1)}, u32[]{:S(2)}, u32[]{:S(2)}) collective-permute-start(bf16[192,1024]{1,0:T(8,128)(2,1)S(1)} %collective-permute-done.10.refs_1_), channel_id=1, source_target_pairs={{0,2},{1,15},{2,4},{3,1},{4,6},{5,3},{6,8},{7,5},{8,10},{9,7},{10,... | collective-permute-start | bytes 1179656 | tf_op jit(solution)/shard_map/ppermute | solution.py:35
  31.6 1.1 %collective-permute-done.11.refs_0_ = bf16[192,1024]{1,0:T(8,128)(2,1)S(1)} collective-permute-done((bf16[192,1024]{1,0:T(8,128)(2,1)S(1)}, bf16[192,1024]{1,0:T(8,128)(2,1)S(1)}, u32[]{:S(2)}, u32[]{:S(2)}) %collective-permute-start.11) | collective-permute-done | bytes 393248 | tf_op jit(solution)/shard_map/ppermute | solution.py:35
  32.6 3.1 %collective-permute-start.13 = (bf16[192,1024]{1,0:T(8,128)(2,1)S(1)}, bf16[192,1024]{1,0:T(8,128)(2,1)S(1)}, u32[]{:S(2)}, u32[]{:S(2)}) collective-permute-start(bf16[192,1024]{1,0:T(8,128)(2,1)S(1)} %collective-permute-done.11.refs_0_), channel_id=1, source_target_pairs={{0,2},{1,15},{2,4},{3,1},{4,6},{5,3},{6,8},{7,5},{8,10},{9,7},{10,... | collective-permute-start | bytes 1179656 | tf_op jit(solution)/shard_map/ppermute | solution.py:35
  35.8 2.3 %match.3 = (bf16[1536,1024]{1,0:T(8,128)(2,1)S(1)}, f32[8,1536]{1,0:T(8,128)S(1)}) custom-call(s32[8,1536]{1,0:T(8,128)S(1)} %get-tuple-element.12.low_ref, s32[1,1536]{1,0:T(1,128)S(1)} %fusion.high_ref, bf16[192,1024]{1,0:T(8,128)(2,1)S(1)} %normalize.1.refs_0_.refs_8_, bf16[192,1024]{1,0:T(8,128)(2,1)S(1)} %collective-permute-done.refs_1_, ...), custom_call_target="tpu_custom_call" | custom-call | flops 1811939328 | bytes 7575552 | tf_op jit(solution)/shard_map/match/pallas_call | solution.py:56
  38.1 1.5 %match.4.best_ref = f32[8,1536]{1,0:T(8,128)S(1)} custom-call(s32[8,1536]{1,0:T(8,128)S(1)} %get-tuple-element.12.low_ref, f32[8,1536]{1,0:T(8,128)S(1)} %get-tuple-element.9.best_ref, bf16[1536,1024]{1,0:T(8,128)(2,1)S(1)} %get-tuple-element.10.right_ref, bf16[192,1024]{1,0:T(8,128)(2,1)S(1)} %collective-permute-done.9.refs_0_, ...), custom_call_target="tpu_custom_call" | custom-call | flops 1207959552 | bytes 4079616 | tf_op jit(solution)/shard_map/match/pallas_call | solution.py:56
  39.6 1.5 %match.5.best_ref = f32[8,1536]{1,0:T(8,128)S(1)} custom-call(s32[8,1536]{1,0:T(8,128)S(1)} %get-tuple-element.12.low_ref, f32[8,1536]{1,0:T(8,128)S(1)} %match.4.best_ref, bf16[1536,1024]{1,0:T(8,128)(2,1)S(1)} %get-tuple-element.10.right_ref, bf16[192,1024]{1,0:T(8,128)(2,1)S(1)} %collective-permute-done.11.refs_0_, ...), custom_call_target="tpu_custom_call" | custom-call | flops 1207959552 | bytes 4079616 | tf_op jit(solution)/shard_map/match/pallas_call | solution.py:56
  41.1 0.7 %last.3 = f32[1,768]{1,0:T(1,128)S(1)} custom-call(s32[8,1536]{1,0:T(8,128)S(1)} %get-tuple-element.12.low_ref, f32[8,1536]{1,0:T(8,128)S(1)} %match.5.best_ref, bf16[1536,1024]{1,0:T(8,128)(2,1)S(1)} %get-tuple-element.10.right_ref, bf16[192,1024]{1,0:T(8,128)(2,1)S(1)} %collective-permute-done.13.piece_ref), custom_call_target="tpu_custom_call" | custom-call | flops 301989888 | bytes 3640320 | tf_op jit(solution)/shard_map/last/pallas_call | solution.py:56
  41.8 2.0 %collective-permute-start.14 = (f32[1,768]{1,0:T(1,128)S(1)}, f32[1,768]{1,0:T(1,128)S(1)}, u32[]{:S(2)}, u32[]{:S(2)}) collective-permute-start(f32[1,768]{1,0:T(1,128)S(1)} %last.3), channel_id=1, source_target_pairs={{0,1},{1,0},{2,3},{3,2},{4,5},{5,4},{6,7},{7,6},{8,9},{9,8},{10,11... | collective-permute-start | bytes 9224 | tf_op jit(solution)/shard_map/ppermute | solution.py:35
  43.8 0.7 %last.2 = f32[1,768]{1,0:T(1,128)S(1)} custom-call(s32[8,1536]{1,0:T(8,128)S(1)} %get-tuple-element.12.low_ref, f32[8,1536]{1,0:T(8,128)S(1)} %match.5.best_ref, bf16[1536,1024]{1,0:T(8,128)(2,1)S(1)} %get-tuple-element.10.right_ref, bf16[192,1024]{1,0:T(8,128)(2,1)S(1)} %collective-permute-done.13.piece_ref), custom_call_target="tpu_custom_call" | custom-call | flops 301989888 | bytes 3640320 | tf_op jit(solution)/shard_map/last/pallas_call | solution.py:56
  44.7 2.6 %collective-permute-start.15 = (f32[192]{0:T(256)S(1)}, f32[192]{0:T(256)S(1)}, u32[]{:S(2)}, u32[]{:S(2)}) collective-permute-start(f32[192]{0:T(256)S(1)} %bitcast.9), channel_id=1, source_target_pairs={{0,32},{1,33},{2,34},{3,35},{4,36},{5,37},{6,38},{7,39},{8,40},{9,... | collective-permute-start | bytes 2312 | tf_op jit(solution)/shard_map/ppermute | solution.py:35
  47.3 1.1 %collective-permute-start.16 = (f32[192]{0:T(256)S(1)}, f32[192]{0:T(256)S(1)}, u32[]{:S(2)}, u32[]{:S(2)}) collective-permute-start(f32[192]{0:T(256)S(1)} %bitcast.8), channel_id=1, source_target_pairs={{0,16},{1,49},{2,18},{3,51},{4,20},{5,53},{6,22},{7,55},{8,24},{9,... | collective-permute-start | bytes 2312 | tf_op jit(solution)/shard_map/ppermute | solution.py:35
  48.8 0.9 %collective-permute-done.16 = f32[192]{0:T(256)S(1)} collective-permute-done((f32[192]{0:T(256)S(1)}, f32[192]{0:T(256)S(1)}, u32[]{:S(2)}, u32[]{:S(2)}) %collective-permute-start.16) | collective-permute-done | bytes 800 | tf_op jit(solution)/shard_map/ppermute | solution.py:35
  49.7 2.3 %collective-permute-done.17 = f32[192]{0:T(256)S(1)} collective-permute-done((f32[192]{0:T(256)S(1)}, f32[192]{0:T(256)S(1)}, u32[]{:S(2)}, u32[]{:S(2)}) %collective-permute-start.17) | collective-permute-done | bytes 800 | tf_op jit(solution)/shard_map/ppermute | solution.py:35
  (31 shorter events, 3.2 us)
Async XLA Ops:
  0.0 1.0 %copy-start = (bf16[192,1024]{1,0:T(8,128)(2,1)S(1)}, bf16[192,1024]{1,0:T(8,128)(2,1)}, u32[]{:S(2)}) copy-start(bf16[192,1024]{1,0:T(8,128)(2,1)} %rows_ref.1) | copy-start | bytes 1179652
  1.2 10.6 %collective-permute-start.1 = (bf16[192,1024]{1,0:T(8,128)(2,1)S(1)}, bf16[192,1024]{1,0:T(8,128)(2,1)S(1)}, u32[]{:S(2)}, u32[]{:S(2)}) collective-permute-start(bf16[192,1024]{1,0:T(8,128)(2,1)S(1)} %normalize.1.refs_0_.refs_8_), channel_id=1, source_target_pairs={{0,1},{1,0},{2,3},{3,2},{4,5},{5,4},{6,7},{7,6},{8,9},{9,8},{10,11... | collective-permute-start | bytes 1179656 | tf_op jit(solution)/shard_map/ppermute | solution.py:35
  4.5 8.7 %collective-permute-start = (bf16[192,1024]{1,0:T(8,128)(2,1)S(1)}, bf16[192,1024]{1,0:T(8,128)(2,1)S(1)}, u32[]{:S(2)}, u32[]{:S(2)}) collective-permute-start(bf16[192,1024]{1,0:T(8,128)(2,1)S(1)} %normalize.1.refs_0_.refs_8_), channel_id=1, source_target_pairs={{0,16},{1,49},{2,18},{3,51},{4,20},{5,53},{6,22},{7,55},{8,24},{9,... | collective-permute-start | bytes 1179656 | tf_op jit(solution)/shard_map/ppermute | solution.py:35
  5.5 10.3 %collective-permute-start.8 = (bf16[192,1024]{1,0:T(8,128)(2,1)S(1)}, bf16[192,1024]{1,0:T(8,128)(2,1)S(1)}, u32[]{:S(2)}, u32[]{:S(2)}) collective-permute-start(bf16[192,1024]{1,0:T(8,128)(2,1)S(1)} %normalize.1.refs_0_.refs_8_), channel_id=1, source_target_pairs={{0,2},{1,15},{2,4},{3,1},{4,6},{5,3},{6,8},{7,5},{8,10},{9,7},{10,... | collective-permute-start | bytes 1179656 | tf_op jit(solution)/shard_map/ppermute | solution.py:35
  11.8 8.2 %collective-permute-start.5 = (bf16[192,1024]{1,0:T(8,128)(2,1)S(1)}, bf16[192,1024]{1,0:T(8,128)(2,1)S(1)}, u32[]{:S(2)}, u32[]{:S(2)}) collective-permute-start(bf16[192,1024]{1,0:T(8,128)(2,1)S(1)} %collective-permute-done.1.refs_4_), channel_id=1, source_target_pairs={{0,2},{1,15},{2,4},{3,1},{4,6},{5,3},{6,8},{7,5},{8,10},{9,7},{10,... | collective-permute-start | bytes 1179656 | tf_op jit(solution)/shard_map/ppermute | solution.py:35
  12.6 11.0 %collective-permute-start.2 = (bf16[192,1024]{1,0:T(8,128)(2,1)S(1)}, bf16[192,1024]{1,0:T(8,128)(2,1)S(1)}, u32[]{:S(2)}, u32[]{:S(2)}) collective-permute-start(bf16[192,1024]{1,0:T(8,128)(2,1)S(1)} %collective-permute-done.1.refs_4_), channel_id=1, source_target_pairs={{0,16},{1,49},{2,18},{3,51},{4,20},{5,53},{6,22},{7,55},{8,24},{9,... | collective-permute-start | bytes 1179656 | tf_op jit(solution)/shard_map/ppermute | solution.py:35
  13.2 10.9 %collective-permute-start.4 = (bf16[192,1024]{1,0:T(8,128)(2,1)S(1)}, bf16[192,1024]{1,0:T(8,128)(2,1)S(1)}, u32[]{:S(2)}, u32[]{:S(2)}) collective-permute-start(bf16[192,1024]{1,0:T(8,128)(2,1)S(1)} %collective-permute-done.refs_1_), channel_id=1, source_target_pairs={{0,16},{1,49},{2,18},{3,51},{4,20},{5,53},{6,22},{7,55},{8,24},{9,... | collective-permute-start | bytes 1179656 | tf_op jit(solution)/shard_map/ppermute | solution.py:35
  15.8 8.4 %collective-permute-start.9 = (bf16[192,1024]{1,0:T(8,128)(2,1)S(1)}, bf16[192,1024]{1,0:T(8,128)(2,1)S(1)}, u32[]{:S(2)}, u32[]{:S(2)}) collective-permute-start(bf16[192,1024]{1,0:T(8,128)(2,1)S(1)} %collective-permute-done.8.refs_9_), channel_id=1, source_target_pairs={{0,2},{1,15},{2,4},{3,1},{4,6},{5,3},{6,8},{7,5},{8,10},{9,7},{10,... | collective-permute-start | bytes 1179656 | tf_op jit(solution)/shard_map/ppermute | solution.py:35
  20.0 8.4 %collective-permute-start.10 = (bf16[192,1024]{1,0:T(8,128)(2,1)S(1)}, bf16[192,1024]{1,0:T(8,128)(2,1)S(1)}, u32[]{:S(2)}, u32[]{:S(2)}) collective-permute-start(bf16[192,1024]{1,0:T(8,128)(2,1)S(1)} %collective-permute-done.5.refs_10_), channel_id=1, source_target_pairs={{0,2},{1,15},{2,4},{3,1},{4,6},{5,3},{6,8},{7,5},{8,10},{9,7},{10,... | collective-permute-start | bytes 1179656 | tf_op jit(solution)/shard_map/ppermute | solution.py:35
  23.5 12.3 %collective-permute-start.6 = (bf16[192,1024]{1,0:T(8,128)(2,1)S(1)}, bf16[192,1024]{1,0:T(8,128)(2,1)S(1)}, u32[]{:S(2)}, u32[]{:S(2)}) collective-permute-start(bf16[192,1024]{1,0:T(8,128)(2,1)S(1)} %collective-permute-done.refs_1_), channel_id=1, source_target_pairs={{0,1},{1,0},{2,3},{3,2},{4,5},{5,4},{6,7},{7,6},{8,9},{9,8},{10,11... | collective-permute-start | bytes 1179656 | tf_op jit(solution)/shard_map/ppermute | solution.py:35
  23.6 12.2 %collective-permute-start.3 = (bf16[192,1024]{1,0:T(8,128)(2,1)S(1)}, bf16[192,1024]{1,0:T(8,128)(2,1)S(1)}, u32[]{:S(2)}, u32[]{:S(2)}) collective-permute-start(bf16[192,1024]{1,0:T(8,128)(2,1)S(1)} %collective-permute-done.2.refs_6_), channel_id=1, source_target_pairs={{0,1},{1,0},{2,3},{3,2},{4,5},{5,4},{6,7},{7,6},{8,9},{9,8},{10,11... | collective-permute-start | bytes 1179656 | tf_op jit(solution)/shard_map/ppermute | solution.py:35
  24.1 11.7 %collective-permute-start.7 = (bf16[192,1024]{1,0:T(8,128)(2,1)S(1)}, bf16[192,1024]{1,0:T(8,128)(2,1)S(1)}, u32[]{:S(2)}, u32[]{:S(2)}) collective-permute-start(bf16[192,1024]{1,0:T(8,128)(2,1)S(1)} %collective-permute-done.4.refs_3_), channel_id=1, source_target_pairs={{0,1},{1,0},{2,3},{3,2},{4,5},{5,4},{6,7},{7,6},{8,9},{9,8},{10,11... | collective-permute-start | bytes 1179656 | tf_op jit(solution)/shard_map/ppermute | solution.py:35
  24.2 8.4 %collective-permute-start.11 = (bf16[192,1024]{1,0:T(8,128)(2,1)S(1)}, bf16[192,1024]{1,0:T(8,128)(2,1)S(1)}, u32[]{:S(2)}, u32[]{:S(2)}) collective-permute-start(bf16[192,1024]{1,0:T(8,128)(2,1)S(1)} %collective-permute-done.9.refs_0_), channel_id=1, source_target_pairs={{0,2},{1,15},{2,4},{3,1},{4,6},{5,3},{6,8},{7,5},{8,10},{9,7},{10,... | collective-permute-start | bytes 1179656 | tf_op jit(solution)/shard_map/ppermute | solution.py:35
  28.4 11.1 %collective-permute-start.12 = (bf16[192,1024]{1,0:T(8,128)(2,1)S(1)}, bf16[192,1024]{1,0:T(8,128)(2,1)S(1)}, u32[]{:S(2)}, u32[]{:S(2)}) collective-permute-start(bf16[192,1024]{1,0:T(8,128)(2,1)S(1)} %collective-permute-done.10.refs_1_), channel_id=1, source_target_pairs={{0,2},{1,15},{2,4},{3,1},{4,6},{5,3},{6,8},{7,5},{8,10},{9,7},{10,... | collective-permute-start | bytes 1179656 | tf_op jit(solution)/shard_map/ppermute | solution.py:35
  32.6 8.4 %collective-permute-start.13 = (bf16[192,1024]{1,0:T(8,128)(2,1)S(1)}, bf16[192,1024]{1,0:T(8,128)(2,1)S(1)}, u32[]{:S(2)}, u32[]{:S(2)}) collective-permute-start(bf16[192,1024]{1,0:T(8,128)(2,1)S(1)} %collective-permute-done.11.refs_0_), channel_id=1, source_target_pairs={{0,2},{1,15},{2,4},{3,1},{4,6},{5,3},{6,8},{7,5},{8,10},{9,7},{10,... | collective-permute-start | bytes 1179656 | tf_op jit(solution)/shard_map/ppermute | solution.py:35
  41.8 2.8 %collective-permute-start.14 = (f32[1,768]{1,0:T(1,128)S(1)}, f32[1,768]{1,0:T(1,128)S(1)}, u32[]{:S(2)}, u32[]{:S(2)}) collective-permute-start(f32[1,768]{1,0:T(1,128)S(1)} %last.3), channel_id=1, source_target_pairs={{0,1},{1,0},{2,3},{3,2},{4,5},{5,4},{6,7},{7,6},{8,9},{9,8},{10,11... | collective-permute-start | bytes 9224 | tf_op jit(solution)/shard_map/ppermute | solution.py:35
  44.7 4.1 %collective-permute-start.15 = (f32[192]{0:T(256)S(1)}, f32[192]{0:T(256)S(1)}, u32[]{:S(2)}, u32[]{:S(2)}) collective-permute-start(f32[192]{0:T(256)S(1)} %bitcast.9), channel_id=1, source_target_pairs={{0,32},{1,33},{2,34},{3,35},{4,36},{5,37},{6,38},{7,39},{8,40},{9,... | collective-permute-start | bytes 2312 | tf_op jit(solution)/shard_map/ppermute | solution.py:35
  47.3 2.4 %collective-permute-start.16 = (f32[192]{0:T(256)S(1)}, f32[192]{0:T(256)S(1)}, u32[]{:S(2)}, u32[]{:S(2)}) collective-permute-start(f32[192]{0:T(256)S(1)} %bitcast.8), channel_id=1, source_target_pairs={{0,16},{1,49},{2,18},{3,51},{4,20},{5,53},{6,22},{7,55},{8,24},{9,... | collective-permute-start | bytes 2312 | tf_op jit(solution)/shard_map/ppermute | solution.py:35
  48.4 3.6 %collective-permute-start.17 = (f32[192]{0:T(256)S(1)}, f32[192]{0:T(256)S(1)}, u32[]{:S(2)}, u32[]{:S(2)}) collective-permute-start(f32[192]{0:T(256)S(1)} %bitcast.7), channel_id=1, source_target_pairs={{0,48},{1,17},{2,50},{3,19},{4,52},{5,21},{6,54},{7,23},{8,56},{9,... | collective-permute-start | bytes 2312 | tf_op jit(solution)/shard_map/ppermute | solution.py:35
